TPU v7x, 128 devices: a whole 4x4x4 slice. The times are simulated.
128 devices in a mesh: scan: 32 (over y_hi, z, x), mode: 4 (over y_lo, core).
Axes of the slice: x: 4, y: 4 (y_hi: 2, y_lo: 2; y = y_hi * 2 + y_lo), z: 4, core: 2. Of those that a mesh axis runs over, the one named last changes fastest.
Arguments:
- object_field: float32 [2, 8192, 8192], P(None, 'scan', 'mode'), may hold values from -6 to 6
- probe_modes: float32 [2, 2, 256, 256], replicated, may hold values from -3 to 3
- measured: float32 [2048, 256, 256], P(('scan', 'mode')), may hold values from 0.3 to 4
- offsets: int32 [2048, 2], P(('scan', 'mode')), may hold values from 0 to 8191, as said below
- live_count: int32 [128], P(('scan', 'mode')), may hold values from 1 to 16, as said below
Outputs:
- object_step: float32 [2, 8192, 8192], P(None, 'scan', 'mode')
- probe_step: float32 [2, 2, 256, 256], replicated
Inputs may be any that keep to these rules, and one draw needn't show every extreme that they name: `offsets`: slot q of device d = q div 16, with s = d div (4) and m = d mod (4), has its row in [s * 256, (s + 1) * 256) and its column in [m * 2048, (m + 1) * 2048); on every device one slot starts at the last row and last column of that range, and another at its first row and first column. `live_count`: the live slots of a device are its first ones; some device has all 16 slots live.
All inputs are finite; a program needn't handle non-finite values.
Results may differ from a plain program's by a relative error of at most 0.003.
The roundings to bfloat16 on the way count: a program that leaves them out, or rounds other values in their place, can miss the bound.
Values sent between devices are 32-bit elements; how exact they have to be, the bound alone decides.
No kernel may reach another device: no remote copies, remote signals or barrier semaphores. Data moves between devices by JAX's collectives and lax.ppermute only.
A program may use at most 128 MiB of HBM per device.

v0:
```python
import math

import jax
import jax.numpy as jnp
from jax import lax
from jax.sharding import PartitionSpec as P

P_DEV = 16


floor_level = 0.5


def shifted(array, axis, by):
    count = lax.axis_size(axis)
    pairs = [(i, i + by) for i in range(count) if 0 <= i + by < count]
    return lax.ppermute(array, axis, pairs)


def dft_tables(length, direction):
    positions = jnp.arange(length, dtype=jnp.int32)
    phase_int = positions[:, None] * positions[None, :] % length
    angles = phase_int.astype(jnp.float32) * (2.0 * math.pi / length)
    scaling = 1.0 / math.sqrt(length)
    cosine = jnp.cos(angles) * scaling
    sine_part = jnp.sin(angles) * scaling * direction
    left_table = jnp.stack(
        [jnp.stack([cosine, sine_part]), jnp.stack([-sine_part, cosine])]
    ).astype(jnp.bfloat16)
    right_table = jnp.stack(
        [jnp.stack([cosine, -sine_part]), jnp.stack([sine_part, cosine])]
    ).astype(jnp.bfloat16)
    return (left_table, right_table)


def transform(stacked, tables):
    left_table, right_table = tables
    half_done = jnp.einsum(
        "ijab,kjbc->kiac", left_table, stacked, preferred_element_type=jnp.float32
    )
    half_done = half_done.astype(jnp.bfloat16)
    return jnp.einsum("kjac,jicd->kiad", half_done, right_table, preferred_element_type=jnp.float32)


def pattern_terms(window, probe_modes, amplitude, forward, backward):
    exit_re = probe_modes[:, 0] * window[0] - probe_modes[:, 1] * window[1]
    exit_im = probe_modes[:, 0] * window[1] + probe_modes[:, 1] * window[0]
    exit_wave = jnp.stack([exit_re, exit_im], axis=1).astype(jnp.bfloat16)
    far_field = transform(exit_wave, forward)
    intensity = jnp.sum(far_field * far_field, axis=(0, 1))
    factor = amplitude * lax.rsqrt(jnp.maximum(intensity, floor_level)) - 1.0
    change = (far_field * factor).astype(jnp.bfloat16)
    delta_wave = transform(change, backward)
    object_re = jnp.sum(
        probe_modes[:, 0] * delta_wave[:, 0] + probe_modes[:, 1] * delta_wave[:, 1], axis=0
    )
    object_im = jnp.sum(
        probe_modes[:, 0] * delta_wave[:, 1] - probe_modes[:, 1] * delta_wave[:, 0], axis=0
    )
    probe_re = window[0] * delta_wave[:, 0] + window[1] * delta_wave[:, 1]
    probe_im = window[0] * delta_wave[:, 1] - window[1] * delta_wave[:, 0]
    return (jnp.stack([object_re, object_im]), jnp.stack([probe_re, probe_im], axis=1))


def shards(object_field, probe_modes, measured, offsets, live_count):
    block_rows = object_field.shape[1]
    block_cols = object_field.shape[2]
    frame_size = probe_modes.shape[2]
    row_base = lax.axis_index("scan") * block_rows
    col_base = lax.axis_index("mode") * block_cols
    from_below = shifted(object_field, "scan", -1)
    from_right = shifted(object_field[:, :, :frame_size], "mode", -1)
    corner = shifted(from_right, "scan", -1)
    upper_part = jnp.concatenate([object_field, from_right], axis=2)
    bottom_part = jnp.concatenate([from_below, corner], axis=2)
    extended = jnp.concatenate([upper_part, bottom_part], axis=1)
    forward = dft_tables(frame_size, 1.0)
    backward = dft_tables(frame_size, -1.0)

    def visit(slot_index, carried):
        gradient, probe_acc = carried
        anchor = (
            jnp.int32(0),
            offsets[slot_index, 0] - row_base,
            offsets[slot_index, 1] - col_base,
        )
        window = lax.dynamic_slice(extended, anchor, (2, frame_size, frame_size))
        object_term, probe_term = pattern_terms(
            window, probe_modes, measured[slot_index], forward, backward
        )
        current = lax.dynamic_slice(gradient, anchor, (2, frame_size, frame_size))
        gradient = lax.dynamic_update_slice(gradient, current + object_term, anchor)
        return (gradient, probe_acc + probe_term)

    zero_grad = jnp.zeros(extended.shape, jnp.float32)
    zero_probe = jnp.zeros(probe_modes.shape, jnp.float32)
    gradient, probe_acc = lax.fori_loop(jnp.int32(0), live_count[0], visit, (zero_grad, zero_probe))
    beside = shifted(gradient[:, :, block_cols:], "mode", 1)
    gradient = gradient.at[:, :, :frame_size].add(beside)
    bottom_part = shifted(gradient[:, block_rows:, :block_cols], "scan", 1)
    interior = gradient[:, :block_rows, :block_cols].at[:, :frame_size, :].add(bottom_part)
    summed = lax.psum(probe_acc, ("scan", "mode"))
    patterns_all = lax.axis_size("scan") * lax.axis_size("mode") * P_DEV
    return (interior, summed / math.sqrt(patterns_all))


def solution(mesh):
    in_specs = (
        P(None, "scan", "mode"),
        P(),
        P(("scan", "mode"), None, None),
        P(("scan", "mode"), None),
        P(("scan", "mode")),
    )
    out_specs = (P(None, "scan", "mode"), P())
    return jax.shard_map(shards, mesh=mesh, in_specs=in_specs, out_specs=out_specs, check_vma=False)
```

profile of v0, /device:TPU:1, one launch (start us, length us, event | category | flops | bytes accessed | tf_op | source)
XLA Modules:
  0.0 662.0 jit_solution(15039947617020034320)
XLA Ops:
  9.6 3.3 collective-permute-start
  17.9 3.5 collective-permute-done
  25.5 86.9 %collective-permute-done.2 = f32[2,256,256]{2,1,0:T(8,128)S(1)} collective-permute-done((f32[2,256,256]{2,1,0:T(8,128)S(1)}, f32[2,256,256]{2,1,0:T(8,128)S(1)}, u32[]{:S(2)}, u32[]{:S(2)}) %collective-permute-start.2) | collective-permute-done | bytes 524320 | tf_op jit(solution)/shard_map/ppermute | solution.py:17
  112.4 6.2 maximum_maximum_fusion
  119.7 4.3 broadcast_in_dim.4
  123.9 121.9 %while.17 = (s32[]{:T(128)}, f32[2,512,2304]{2,1,0:T(8,128)}, f32[2,2,256,256]{3,2,1,0:T(8,128)}, s32[]{:T(128)}, s32[16,2]{0,1:T(2,128)S(1)}, /*index=5*/s32[]{...) while((s32[]{:T(128)}, f32[2,512,2304]{2,1,0:T(8,128)}, ...), condition=%wide.region_4.5_spmd, body=%wide.region_0.4_spmd.sunk | while | flops 1080033280 | bytes 20185464 | solution.py:97
  126.4 1.3 dynamic-slice_bitcast_fusion.3
  127.9 2.9 multiply_reduce_fusion.2
  131.9 2.1 convolution_bitcast_fusion.5
  134.2 1.4 maximum_add_fusion.4
  135.6 2.3 maximum_add_fusion.5
  138.0 5.9 dynamic_update_slice.7
  146.3 1.3 dynamic-slice_bitcast_fusion.3
  147.8 2.9 multiply_reduce_fusion.2
  151.8 2.1 convolution_bitcast_fusion.5
  154.1 1.4 maximum_add_fusion.4
  155.5 2.3 maximum_add_fusion.5
  157.9 5.9 dynamic_update_slice.7
  166.2 1.3 dynamic-slice_bitcast_fusion.3
  167.7 3.0 multiply_reduce_fusion.2
  171.7 2.1 convolution_bitcast_fusion.5
  174.1 1.4 maximum_add_fusion.4
  175.4 2.3 maximum_add_fusion.5
  177.8 6.1 dynamic_update_slice.7
  186.4 1.3 dynamic-slice_bitcast_fusion.3
  187.8 2.9 multiply_reduce_fusion.2
  191.8 2.1 convolution_bitcast_fusion.5
  194.2 1.4 maximum_add_fusion.4
  195.5 2.3 maximum_add_fusion.5
  197.9 6.8 %dynamic_update_slice.7 = f32[2,512,2304]{2,1,0:T(8,128)} dynamic-update-slice(f32[2,512,2304]{2,1,0:T(8,128)} %get-tuple-element.416, f32[2,256,256]{2,1,0:T(8,128)S(1)} %maximum_add_fusion.4, s32[]{:T(128)} %constant.133.clone.1..sunk, s32[]{:T(128)S(6)} %select_n.108, s32[]{:T(128)S(6)} %select_n.109) | dynamic-update-slice | bytes 1048580 | tf_op jit(solution)/shard_map/while/body/dynamic_update_slice | solution.py:92
  208.6 2.9 multiply_reduce_fusion.2
  212.6 2.1 convolution_bitcast_fusion.5
  214.9 1.4 maximum_add_fusion.4
  216.3 2.3 maximum_add_fusion.5
  218.7 5.8 dynamic_update_slice.7
  228.4 2.9 multiply_reduce_fusion.2
  232.3 2.1 convolution_bitcast_fusion.5
  234.7 1.4 maximum_add_fusion.4
  236.1 2.3 maximum_add_fusion.5
  238.4 6.8 %dynamic_update_slice.7 = f32[2,512,2304]{2,1,0:T(8,128)} dynamic-update-slice(f32[2,512,2304]{2,1,0:T(8,128)} %get-tuple-element.416, f32[2,256,256]{2,1,0:T(8,128)S(1)} %maximum_add_fusion.4, s32[]{:T(128)} %constant.133.clone.1..sunk, s32[]{:T(128)S(6)} %select_n.108, s32[]{:T(128)S(6)} %select_n.109) | dynamic-update-slice | bytes 1048580 | tf_op jit(solution)/shard_map/while/body/dynamic_update_slice | solution.py:92
  247.1 1.9 collective-permute-start.3
  249.1 11.7 %collective-permute-done.3 = f32[2,512,256]{2,1,0:T(8,128)S(1)} collective-permute-done((f32[2,512,256]{2,1,0:T(8,128)S(1)}, f32[2,512,256]{2,1,0:T(8,128)S(1)}, u32[]{:S(2)}, u32[]{:S(2)}) %collective-permute-start.3) | collective-permute-done | bytes 1048608 | tf_op jit(solution)/shard_map/ppermute | solution.py:17
  260.8 2.4 add_dynamic-update-slice_fusion
  263.2 4.7 slice.117
  267.9 29.9 %collective-permute-start.4 = (f32[2,256,2048]{2,1,0:T(8,128)}, f32[2,256,2048]{2,1,0:T(8,128)}, u32[]{:S(2)}, u32[]{:S(2)}) collective-permute-start(f32[2,256,2048]{2,1,0:T(8,128)} %slice.117), channel_id=1, source_target_pairs={{0,4},{4,8},{8,12},{12,16},{16,20},{20,24},{24,28},{28,32},{32,36}... | collective-permute-start | bytes 12582920 | tf_op jit(solution)/shard_map/ppermute | solution.py:17
  297.9 348.4 %all-reduce.2.cloned.1.call-done = f32[2,2,256,256]{3,2,1,0:T(8,128)} async-done(((f32[2,2,256,256]{3,2,1,0:T(8,128)}), f32[2,2,256,256]{3,2,1,0:T(8,128)}) %all-reduce.2.cloned.1.call-update) | async-done | bytes 1048592 | tf_op jit(solution)/shard_map/psum | solution.py:102
  646.2 2.3 broadcast_multiply_fusion
  648.6 6.6 slice_add_fusion
  (49 shorter events, 28.5 us)
Async XLA Ops:
  7.2 639.1 %all-reduce.2.cloned.1.call-start = ((), (), s32[]{:S(2)}) async-start(), calls=%async_computation | async-start | bytes 2097152 | tf_op jit(solution)/shard_map/psum | solution.py:102
  7.2 105.2 %collective-permute-start.1 = (f32[2,256,2048]{2,1,0:T(8,128)}, f32[2,256,2048]{2,1,0:T(8,128)}, u32[]{:S(2)}, u32[]{:S(2)}) collective-permute-start(f32[2,256,2048]{2,1,0:T(8,128)} %param.13), channel_id=1, source_target_pairs={{4,0},{8,4},{12,8},{16,12},{20,16},{24,20},{28,24},{32,28},{36,32}... | collective-permute-start | bytes 12582920 | tf_op jit(solution)/shard_map/ppermute | solution.py:17
  9.6 11.9 %collective-permute-start = (f32[2,256,256]{2,1,0:T(8,128)S(1)}, f32[2,256,256]{2,1,0:T(8,128)S(1)}, u32[]{:S(2)}, u32[]{:S(2)}) collective-permute-start(f32[2,256,256]{2,1,0:T(8,128)S(1)} %slice.109), channel_id=1, source_target_pairs={{1,0},{2,1},{3,2},{5,4},{6,5},{7,6},{9,8},{10,9},{11,10},{13,12},{... | collective-permute-start | bytes 1572872 | tf_op jit(solution)/shard_map/ppermute | solution.py:17
  21.4 90.9 %collective-permute-start.2 = (f32[2,256,256]{2,1,0:T(8,128)S(1)}, f32[2,256,256]{2,1,0:T(8,128)S(1)}, u32[]{:S(2)}, u32[]{:S(2)}) collective-permute-start(f32[2,256,256]{2,1,0:T(8,128)S(1)} %collective-permute-done), channel_id=1, source_target_pairs={{4,0},{8,4},{12,8},{16,12},{20,16},{24,20},{28,24},{32,28},{36,32}... | collective-permute-start | bytes 1572872 | tf_op jit(solution)/shard_map/ppermute | solution.py:17
  118.6 5.3 copy-start
  118.6 5.3 copy-start.1
  247.1 13.7 %collective-permute-start.3 = (f32[2,512,256]{2,1,0:T(8,128)S(1)}, f32[2,512,256]{2,1,0:T(8,128)S(1)}, u32[]{:S(2)}, u32[]{:S(2)}) collective-permute-start(f32[2,512,256]{2,1,0:T(8,128)S(1)} %slice.111), channel_id=1, source_target_pairs={{0,1},{1,2},{2,3},{4,5},{5,6},{6,7},{8,9},{9,10},{10,11},{12,13},{... | collective-permute-start | bytes 3145736 | tf_op jit(solution)/shard_map/ppermute | solution.py:17
  267.9 380.7 %collective-permute-start.4 = (f32[2,256,2048]{2,1,0:T(8,128)}, f32[2,256,2048]{2,1,0:T(8,128)}, u32[]{:S(2)}, u32[]{:S(2)}) collective-permute-start(f32[2,256,2048]{2,1,0:T(8,128)} %slice.117), channel_id=1, source_target_pairs={{0,4},{4,8},{8,12},{12,16},{16,20},{20,24},{24,28},{28,32},{32,36}... | collective-permute-start | bytes 12582920 | tf_op jit(solution)/shard_map/ppermute | solution.py:17
Sparse Core Ops, SparseCore 0:
  298.0 348.2 all-reduce.1
where the time goes:
time: 669 us; the launch traced here: 662 us
  waiting for transfers between devices  451 us (67%)
  local copies, waits for them, and re-layouts  62 us (9%)
  other arithmetic  55 us (8%)
  starting transfers between devices  37.8 us (6%)
  matrix products  30.3 us (5%)
  between operations  14.1 us (2%)
  loops' own time  12.2 us (2%)
    psum x1, waiting for transfers between devices, shards(): summed = lax.psum(probe_acc, ('scan', 'mode'))  348 us
    ppermute x5, waiting for transfers between devices, shifted(): return lax.ppermute(array, axis, pairs)  102 us
    ppermute x5, starting transfers between devices, shifted(): return lax.ppermute(array, axis, pairs)  37.8 us
    dynamic_update_slice x6, local copies, waits for them, and re-layouts, visit(): gradient = lax.dynamic_update_slice(gradient, current + object_term, anchor)  37.1 us
    dot_general x12, matrix products, transform(): jnp.einsum('kjac,jicd->kiad', half_done, right_table, preferred_element_t...  30.3 us
    add x6, other arithmetic, visit(): return (gradient, probe_acc + probe_term)  14 us
  transfers between devices with their start and end apart: 6, of which 4 were waited for; matrix products, arithmetic and copies ran while one was open for 2% of the time, Pallas kernels for 0%

commit v1 on v0

v1 whole, which is shorter than its diff:
```python
import functools
import math

import jax
import jax.numpy as jnp
import ml_dtypes
import numpy as np
from jax import lax
from jax.experimental import pallas as pl
from jax.experimental.pallas import tpu as pltpu
from jax.sharding import PartitionSpec as P

SLOTS = 16
SIZE = 256
LANE = 128
CHUNK = 256
FLOOR = 0.5
AXES = ("scan", "mode")
f32 = jnp.float32
bf16 = jnp.bfloat16


def tables():
    place = np.arange(SIZE)
    angles = (place[:, None] * place[None, :] % SIZE) * (2.0 * math.pi / SIZE)
    c = np.cos(angles) / math.sqrt(SIZE)
    s = np.sin(angles) / math.sqrt(SIZE)
    order = np.concatenate([place[0::2], place[1::2]])

    def block(c, s):
        return np.block([[c, s], [-s, c]]).astype(ml_dtypes.bfloat16)

    return (
        block(c[:, order], s[:, order]),
        block(c, -s),
        block(c[order], -s[order]),
        block(c, s),
    )


def turned(h):
    n = SIZE
    return jnp.concatenate(
        [
            jnp.concatenate([h[:n, :n], h[n:, :n]], 1),
            jnp.concatenate([h[:n, n:], h[n:, n:]], 1),
        ],
        0,
    )


def pattern(ext, grad, acc, probe, amplitude, tabs, r, c):
    left_fwd, right_fwd, left_bwd, right_bwd = tabs
    n = SIZE
    half = n // 2
    block = c // LANE
    shift = c % LANE
    dot = functools.partial(jnp.dot, preferred_element_type=f32)

    def window(part):
        cols = []
        for j in range(3):
            view = ext.at[part, block + j]
            cols.append(
                jnp.concatenate(
                    [view[pl.ds(r + p, half, stride=2), :] for p in (0, 1)], 0
                )
            )
        wide = jnp.concatenate(cols, 1)
        return pltpu.roll(wide, 3 * LANE - shift, 1)[:, :n]

    wr = window(0)
    wi = window(1)
    x_re = [probe[k, 0] * wr - probe[k, 1] * wi for k in (0, 1)]
    x_im = [probe[k, 0] * wi + probe[k, 1] * wr for k in (0, 1)]
    x = jnp.concatenate([jnp.concatenate(x_re, 1), jnp.concatenate(x_im, 1)], 0).astype(bf16)
    h = turned(dot(left_fwd[...], x).astype(bf16))
    far = dot(h, right_fwd[...])
    sq = far * far
    intensity = (sq[:n, :n] + sq[:n, n:]) + (sq[n:, :n] + sq[n:, n:])
    factor = amplitude * lax.rsqrt(jnp.maximum(intensity, FLOOR)) - 1.0
    factor = jnp.concatenate([jnp.concatenate([factor, factor], 1)] * 2, 0)
    change = turned((far * factor).astype(bf16))
    h = turned(dot(left_bwd[...], change).astype(bf16))
    delta = dot(h, right_bwd[...])
    terms = [None, None]
    for k in (0, 1):
        d_re = delta[n * k : n * k + n, :n]
        d_im = delta[n * k : n * k + n, n:]
        new = (
            probe[k, 0] * d_re + probe[k, 1] * d_im,
            probe[k, 0] * d_im - probe[k, 1] * d_re,
        )
        terms = [b if a is None else a + b for a, b in zip(terms, new)]
        acc[k, 0] += wr * d_re + wi * d_im
        acc[k, 1] += wr * d_im - wi * d_re
    blank = jnp.zeros((n, LANE), f32)
    for part, term in enumerate(terms):
        moved = pltpu.roll(jnp.concatenate([term, blank], 1), shift, 1)
        for j in range(3):
            view = grad.at[part, block + j]
            for p in (0, 1):
                rows = pl.ds(r + p, half, stride=2)
                view[rows, :] = view[rows, :] + moved[half * p : half * (p + 1), LANE * j : LANE * (j + 1)]


def group_kernel(first, count, own_blocks, live, off, *refs):
    wide = count + 2
    n_halo = wide // 2
    has_right = first + wide > own_blocks
    refs = list(refs)
    field = refs.pop(0)
    right = refs.pop(0) if has_right else None
    halos = [refs.pop(0) for _ in range(n_halo)]
    measured, probe, t0, t1, t2, t3, carry, acc_in = refs[:8]
    done, carry_out, acc = refs[8:11]
    ext, grad, frame, picked, load_sem, frame_sem = refs[11:]

    def pick(q, n):
        b = off[q, 1] // LANE - first
        picked[n] = q
        return n + jnp.where((b >= 0) & (b < count), 1, 0)

    n = lax.fori_loop(0, live[0], pick, jnp.int32(0))

    def loads():
        out = []
        for b in range(wide):
            at = (first + b) * LANE
            if first + b < own_blocks:
                src = field.at[:, :, at : at + LANE]
            else:
                at -= own_blocks * LANE
                src = right.at[:, :, at : at + LANE]
            out.append(pltpu.make_async_copy(src, ext.at[:, b, 0:SIZE, :], load_sem.at[2 * b]))
            low = (b % 2) * LANE
            src = halos[b // 2].at[:, :, low : low + LANE]
            out.append(
                pltpu.make_async_copy(src, ext.at[:, b, SIZE : 2 * SIZE, :], load_sem.at[2 * b + 1])
            )
        return out

    def frame_copy(i):
        slot = i % 2
        return pltpu.make_async_copy(measured.at[picked[i]], frame.at[slot], frame_sem.at[slot])

    @pl.when(n > 0)
    def _():
        for copy in loads():
            copy.start()
        frame_copy(0).start()

    grad[:, 0:2] = carry[...]
    grad[:, 2:] = jnp.zeros((2, count, 2 * SIZE, LANE), f32)
    acc[...] = acc_in[...]

    @pl.when(n > 0)
    def _():
        for copy in loads():
            copy.wait()

    def step(i, _):
        @pl.when(i + 1 < n)
        def _():
            frame_copy(i + 1).start()

        frame_copy(i).wait()
        q = picked[i]
        pattern(
            ext, grad, acc, probe, frame[i % 2], (t0, t1, t2, t3), off[q, 0], off[q, 1] - first * LANE
        )
        return 0

    lax.fori_loop(0, n, step, 0)
    done[...] = grad[:, 0:count]
    carry_out[...] = grad[:, count:]


def run_group(first, count, own_blocks, live, off, field, right, halos, measured, probe, tabs, carry, acc):
    wide = count + 2
    anywhere = pl.BlockSpec(memory_space=pl.ANY)
    smem = pl.BlockSpec(memory_space=pltpu.SMEM)
    vmem = pl.BlockSpec(memory_space=pltpu.VMEM)
    rights = [right] if first + wide > own_blocks else []
    args = [live, off, field, *rights, *halos, measured, probe, *tabs, carry, acc]
    specs = [smem, smem] + [anywhere] * (2 + len(rights) + len(halos)) + [vmem] * 7
    out_shape = (
        jax.ShapeDtypeStruct((2, count, 2 * SIZE, LANE), f32),
        jax.ShapeDtypeStruct((2, 2, 2 * SIZE, LANE), f32),
        jax.ShapeDtypeStruct((2, 2, SIZE, SIZE), f32),
    )
    return pl.pallas_call(
        functools.partial(group_kernel, first, count, own_blocks),
        out_shape=out_shape,
        in_specs=specs,
        out_specs=(vmem,) * 3,
        scratch_shapes=[
            pltpu.VMEM((2, wide, 2 * SIZE, LANE), f32),
            pltpu.VMEM((2, wide, 2 * SIZE, LANE), f32),
            pltpu.VMEM((2, SIZE, SIZE), f32),
            pltpu.SMEM((SLOTS + 1,), jnp.int32),
            pltpu.SemaphoreType.DMA((2 * wide,)),
            pltpu.SemaphoreType.DMA((2,)),
        ],
        compiler_params=pltpu.CompilerParams(vmem_limit_bytes=32 * 2**20),
        cost_estimate=pl.CostEstimate(
            flops=2 * 1024**3, bytes_accessed=8 * 2**20, transcendentals=0
        ),
        name=f"group_{first}",
    )(*args)


def shifted(array, axis, by):
    count = lax.axis_size(axis)
    pairs = [(i, i + by) for i in range(count) if 0 <= i + by < count]
    return lax.ppermute(array, axis, pairs)


def shifted_both(array):
    rows, cols = (lax.axis_size(a) for a in AXES)
    pairs = [
        (i * cols + j, (i + 1) * cols + j + 1) for i in range(rows - 1) for j in range(cols - 1)
    ]
    return lax.ppermute(array, AXES, pairs)


def place_of(index):
    s, m = divmod(index, 4)
    return [m % 2, (s // 16) * 2 + m // 2, (s // 4) % 4, s % 4]


def index_of(place):
    core, y, z, x = place
    return ((y // 2) * 16 + z * 4 + x) * 4 + (y % 2) * 2 + core


def swapped(array, axis, bits):
    pairs = []
    for i in range(128):
        place = place_of(i)
        place[axis] ^= bits
        pairs.append((i, index_of(place)))
    return lax.ppermute(array, AXES, pairs)


def sum_everywhere(total):
    s = lax.axis_index("scan")
    m = lax.axis_index("mode")
    core, y = m % 2, (s // 16) * 2 + m // 2
    pick = functools.partial(lax.dynamic_index_in_dim, axis=0, keepdims=False)
    v = total.reshape(2, 512, 256)
    v = pick(v, core) + swapped(pick(v, 1 - core), 0, 1)
    v = v.reshape(4, 128, 256)
    a, b, c = [swapped(pick(v, y ^ k), 1, k) for k in (1, 2, 3)]
    v = (pick(v, y) + a) + (b + c)
    for axis in (2, 3):
        a, b, c = [swapped(v, axis, k) for k in (1, 2, 3)]
        v = (v + a) + (b + c)
    parts = jnp.stack([v] + [swapped(v, 1, k) for k in (1, 2, 3)])
    v = jnp.concatenate([pick(parts, y ^ i) for i in range(4)], 0)
    w = swapped(v, 0, 1)
    low = jnp.where(core == 0, v, w)
    high = jnp.where(core == 0, w, v)
    return jnp.stack([low, high]).reshape(total.shape)


def unblocked(part):
    return jnp.transpose(part, (0, 2, 1, 3)).reshape(2, SIZE, -1)


def shards(field, probe, measured, offsets, live):
    rows, cols = field.shape[1:]
    base = jnp.stack([lax.axis_index("scan") * rows, lax.axis_index("mode") * cols])
    off = offsets - base[None, :]
    tabs = [jnp.asarray(t) for t in tables()]
    probe_rows = probe.reshape(2, 2, 128, 2, 256).transpose(0, 1, 3, 2, 4).reshape(probe.shape)
    chunks = cols // CHUNK
    blocks = cols // LANE
    halos = [shifted(field[:, :, CHUNK * i : CHUNK * (i + 1)], "scan", -1) for i in range(chunks)]
    right = shifted(field[:, :, :CHUNK], "mode", -1)
    halos.append(shifted(halos[0], "mode", -1))
    carry = jnp.zeros((2, 2, 2 * SIZE, LANE), f32)
    acc = jnp.zeros(probe.shape, f32)
    uppers, lowers = [], []
    plan = [(2 * i, 2) for i in range(chunks - 2)] + [(blocks - 4, 4)]
    for first, count in plan:
        near = halos[first // 2 : first // 2 + count // 2 + 1]
        done, carry, acc = run_group(
            first, count, blocks, live, off, field, right, near, measured, probe_rows, tabs, carry, acc
        )
        uppers.append(unblocked(done[:, :, :SIZE]))
        lowers.append(unblocked(shifted(done[:, :, SIZE:], "scan", 1)))
    beside = unblocked(shifted(carry[:, :, :SIZE], "mode", 1)) + unblocked(shifted_both(carry[:, :, SIZE:]))
    uppers[0] = uppers[0] + beside
    step = jnp.concatenate([a + b for a, b in zip(uppers, lowers)], 2)
    acc = sum_everywhere(acc)
    acc = acc.reshape(2, 2, 2, 128, 256).transpose(0, 1, 3, 2, 4).reshape(probe.shape)
    slots_all = lax.axis_size("scan") * lax.axis_size("mode") * SLOTS
    return (step, acc * (1.0 / math.sqrt(slots_all)))


def solution(mesh):
    in_specs = (
        P(None, "scan", "mode"),
        P(),
        P(AXES, None, None),
        P(AXES, None),
        P(AXES),
    )
    out_specs = (P(None, "scan", "mode"), P())
    return jax.shard_map(shards, mesh=mesh, in_specs=in_specs, out_specs=out_specs, check_vma=False)
```

time: 669 us -> 252 us (0.38)
  waiting for transfers between devices: 451 us -> 80.1 us
  starting transfers between devices: 37.8 us -> 107 us
  other arithmetic: 55 us -> 7.09 us
  matrix products: 30.3 us -> 0 us
  local copies, waits for them, and re-layouts: 62 us -> 35.8 us
  Pallas kernels: 0 us -> 16 us
  loops' own time: 12.2 us -> 0 us
  between operations: 14.1 us -> 2.03 us
    psum x1 -> x0, waiting for transfers between devices: 348 us -> none  [shards(): summed = lax.psum(probe_acc, ('scan', 'mode'))]
    ppermute x5 -> x18, waiting for transfers between devices: 102 us -> 47 us  [shifted(): return lax.ppermute(array, axis, pairs)]
    ppermute x0 -> x15, starting transfers between devices: none -> 54.2 us  [the longest x14 49.2 us: swapped(): return lax.ppermute(array, AXES, pairs)]
    dynamic_update_slice x6 -> x0, local copies, waits for them, and re-layouts: 37.1 us -> none  [visit(): gradient = lax.dynamic_update_slice(gradient, current + object_term, anchor)]
    ppermute x0 -> x15, waiting for transfers between devices: none -> 33.1 us  [the longest x14 33.1 us: swapped(): return lax.ppermute(array, AXES, pairs)]
    dot_general x12 -> x0, matrix products: 30.3 us -> none  [transform(): jnp.einsum('kjac,jicd->kiad', half_done, right_table, preferred_element_t...]
    add x19 -> x11, other arithmetic: 30.4 us -> 5.98 us  [the longest x7 3.87 us: shards(): step = jnp.concatenate([a + b for a, b in zip(uppers, lowers)], 2)]
    unnamed x4 -> x43, local copies, waits for them, and re-layouts: 0.01 us -> 18.2 us
  transfers between devices with their start and end apart: 6 -> 33, of which waited for: 4 -> 13; matrix products, arithmetic and copies ran while one was open for 2% -> 13% of each run, Pallas kernels for 0% -> 6%
where the time goes in v1:
time: 252 us; the launch traced here: 248 us
  starting transfers between devices  107 us (42%)
  waiting for transfers between devices  80.1 us (32%)
  local copies, waits for them, and re-layouts  35.8 us (14%)
  Pallas kernels  16 us (6%)
  other arithmetic  7.09 us (3%)
    ppermute x18, starting transfers between devices, shifted(): return lax.ppermute(array, axis, pairs)  53.1 us
    ppermute x14, starting transfers between devices, swapped(): return lax.ppermute(array, AXES, pairs)  49.2 us
    ppermute x18, waiting for transfers between devices, shifted(): return lax.ppermute(array, axis, pairs)  47 us
    ppermute x14, waiting for transfers between devices, swapped(): return lax.ppermute(array, AXES, pairs)  33.1 us
    unnamed x43, local copies, waits for them, and re-layouts  18.2 us
    pallas_call x7, Pallas kernels, run_group(): pl.pallas_call(functools.partial(group_kernel, first, count, own_blocks),...  16 us
    ppermute x1, starting transfers between devices, shifted_both(): return lax.ppermute(array, AXES, pairs)  5.05 us
  transfers between devices with their start and end apart: 33, of which 13 were waited for; matrix products, arithmetic and copies ran while one was open for 13% of the time, Pallas kernels for 6%

profile of v1, /device:TPU:1, one launch (start us, length us, event | category | flops | bytes accessed | tf_op | source)
XLA Modules:
  0.0 248.4 jit_solution(16265436088050461414)
XLA Ops:
  0.6 4.3 %fusion.2 = (f32[2,256,256]{2,1,0:T(8,128)}, f32[2,256,256]{2,1,0:T(8,128)}, f32[2,256,256]{2,1,0:T(8,128)}, f32[2,256,256]{2,1,0:T(8,128)}, f32[2,256,256]{2,1,...) fusion(f32[2,256,2048]{2,1,0:T(8,128)} %refs_0_.13), kind=kLoop, calls=%fused_computation.35 | loop fusion | bytes 8388608 | tf_op jit(solution)/shard_map/slice | solution.py:279
  5.0 1.4 collective-permute-start
  7.7 3.3 %collective-permute-start.2 = (f32[2,256,256]{2,1,0:T(8,128)}, f32[2,256,256]{2,1,0:T(8,128)}, u32[]{:S(2)}, u32[]{:S(2)}) collective-permute-start(f32[2,256,256]{2,1,0:T(8,128)} %get-tuple-element.55), channel_id=1, source_target_pairs={{1,0},{2,1},{3,2},{5,4},{6,5},{7,6},{9,8},{10,9},{11,10},{13,12},{... | collective-permute-start | bytes 1572872 | tf_op jit(solution)/shard_map/ppermute | solution.py:216
  11.1 1.3 collective-permute-start.9
  12.4 1.3 collective-permute-start.8
  13.8 1.6 reshape.49
  15.4 1.3 copy.24
  17.5 3.0 %collective-permute-done.refs_1_ = f32[2,256,256]{2,1,0:T(8,128)} collective-permute-done((f32[2,256,256]{2,1,0:T(8,128)}, f32[2,256,256]{2,1,0:T(8,128)}, u32[]{:S(2)}, u32[]{:S(2)}) %collective-permute-start) | collective-permute-done | bytes 524320 | tf_op jit(solution)/shard_map/ppermute | solution.py:216
  21.8 9.9 %collective-permute-done.1.refs_2_.refs_1_ = f32[2,256,256]{2,1,0:T(8,128)} collective-permute-done((f32[2,256,256]{2,1,0:T(8,128)}, f32[2,256,256]{2,1,0:T(8,128)}, u32[]{:S(2)}, u32[]{:S(2)}) %collective-permute-start.1) | collective-permute-done | bytes 524320 | tf_op jit(solution)/shard_map/ppermute | solution.py:216
  33.2 2.2 copy-done
  35.4 2.2 copy-done.1
  39.6 3.3 %collective-permute-done.9.refs_2_.refs_1_ = f32[2,256,256]{2,1,0:T(8,128)} collective-permute-done((f32[2,256,256]{2,1,0:T(8,128)}, f32[2,256,256]{2,1,0:T(8,128)}, u32[]{:S(2)}, u32[]{:S(2)}) %collective-permute-start.9) | collective-permute-done | bytes 524320 | tf_op jit(solution)/shard_map/ppermute | solution.py:216
  45.5 8.7 %collective-permute-done.8.refs_2_.refs_1_ = f32[2,256,256]{2,1,0:T(8,128)} collective-permute-done((f32[2,256,256]{2,1,0:T(8,128)}, f32[2,256,256]{2,1,0:T(8,128)}, u32[]{:S(2)}, u32[]{:S(2)}) %collective-permute-start.8) | collective-permute-done | bytes 524320 | tf_op jit(solution)/shard_map/ppermute | solution.py:216
  56.7 8.6 %collective-permute-done.7.refs_2_.refs_1_ = f32[2,256,256]{2,1,0:T(8,128)S(1)} collective-permute-done((f32[2,256,256]{2,1,0:T(8,128)}, f32[2,256,256]{2,1,0:T(8,128)S(1)}, u32[]{:S(2)}, u32[]{:S(2)}) %collective-permute-start.7) | collective-permute-done | bytes 524320 | tf_op jit(solution)/shard_map/ppermute | solution.py:216
  65.3 5.0 %collective-permute-start.5 = (f32[2,256,256]{2,1,0:T(8,128)}, f32[2,256,256]{2,1,0:T(8,128)S(1)}, u32[]{:S(2)}, u32[]{:S(2)}) collective-permute-start(f32[2,256,256]{2,1,0:T(8,128)} %collective-permute-done.refs_1_), channel_id=1, source_target_pairs={{1,0},{2,1},{3,2},{5,4},{6,5},{7,6},{9,8},{10,9},{11,10},{13,12},{... | collective-permute-start | bytes 1572872 | tf_op jit(solution)/shard_map/ppermute | solution.py:216
  71.6 5.0 %collective-permute-done.6.refs_2_.refs_1_ = f32[2,256,256]{2,1,0:T(8,128)S(1)} collective-permute-done((f32[2,256,256]{2,1,0:T(8,128)}, f32[2,256,256]{2,1,0:T(8,128)S(1)}, u32[]{:S(2)}, u32[]{:S(2)}) %collective-permute-start.6) | collective-permute-done | bytes 524320 | tf_op jit(solution)/shard_map/ppermute | solution.py:216
  76.6 6.0 %collective-permute-start.12 = (f32[2,2,256,128]{3,2,1,0:T(8,128)}, f32[2,2,256,128]{3,2,1,0:T(8,128)}, u32[]{:S(2)}, u32[]{:S(2)}) collective-permute-start(f32[2,2,256,128]{3,2,1,0:T(8,128)} %slice.84), channel_id=1, source_target_pairs={{0,4},{4,8},{8,12},{12,16},{16,20},{20,24},{24,28},{28,32},{32,36}... | collective-permute-start | bytes 1572872 | tf_op jit(solution)/shard_map/ppermute | solution.py:216
  82.6 1.3 group_8.1
  83.9 3.9 %collective-permute-done.3.refs_2_ = f32[2,256,256]{2,1,0:T(8,128)S(1)} collective-permute-done((f32[2,256,256]{2,1,0:T(8,128)S(1)}, f32[2,256,256]{2,1,0:T(8,128)S(1)}, u32[]{:S(2)}, u32[]{:S(2)}) %collective-permute-start.3) | collective-permute-done | bytes 524320 | tf_op jit(solution)/shard_map/ppermute | solution.py:216
  87.8 4.5 %collective-permute-start.13 = (f32[2,2,256,128]{3,2,1,0:T(8,128)S(1)}, f32[2,2,256,128]{3,2,1,0:T(8,128)S(1)}, u32[]{:S(2)}, u32[]{:S(2)}) collective-permute-start(f32[2,2,256,128]{3,2,1,0:T(8,128)S(1)} %slice.86), channel_id=1, source_target_pairs={{0,4},{4,8},{8,12},{12,16},{16,20},{20,24},{24,28},{28,32},{32,36}... | collective-permute-start | bytes 1572872 | tf_op jit(solution)/shard_map/ppermute | solution.py:216
  92.3 3.5 %group_10.1 = (f32[2,2,512,128]{3,2,1,0:T(8,128)S(1)}, f32[2,2,512,128]{3,2,1,0:T(8,128)S(1)}, f32[2,2,256,256]{3,2,1,0:T(8,128)S(1)}) custom-call(s32[1]{0:T(128)S(6)} %copy.41.live, s32[16,2]{1,0:T(8,128)S(1)} %broadcast_subtract_fusion.off, f32[2,256,2048]{2,1,0:T(8,128)S(1)} %copy-done, f32[2,256,256]{2,1,0:T(8,128)S(1)} %collective-permute-done.6.refs_2_.refs_1_, ...), custom_call_target="tpu_custom_call" | custom-call | flops 2147483648 | bytes 8388608 | tf_op jit(solution)/shard_map/group_10/pallas_call | solution.py:192
  95.9 4.2 %collective-permute-start.14 = (f32[2,2,256,128]{3,2,1,0:T(8,128)S(1)}, f32[2,2,256,128]{3,2,1,0:T(8,128)S(1)}, u32[]{:S(2)}, u32[]{:S(2)}) collective-permute-start(f32[2,2,256,128]{3,2,1,0:T(8,128)S(1)} %slice.88), channel_id=1, source_target_pairs={{0,4},{4,8},{8,12},{12,16},{16,20},{20,24},{24,28},{28,32},{32,36}... | collective-permute-start | bytes 1572872 | tf_op jit(solution)/shard_map/ppermute | solution.py:216
  100.1 7.4 %collective-permute-start.15 = (f32[2,2,256,128]{3,2,1,0:T(8,128)S(1)}, f32[2,2,256,128]{3,2,1,0:T(8,128)S(1)}, u32[]{:S(2)}, u32[]{:S(2)}) collective-permute-start(f32[2,2,256,128]{3,2,1,0:T(8,128)S(1)} %slice.90), channel_id=1, source_target_pairs={{0,4},{4,8},{8,12},{12,16},{16,20},{20,24},{24,28},{28,32},{32,36}... | collective-permute-start | bytes 1572872 | tf_op jit(solution)/shard_map/ppermute | solution.py:216
  107.5 1.9 collective-permute-start.16
  109.4 6.5 %group_12.1 = (f32[2,4,512,128]{3,2,1,0:T(8,128)S(1)}, f32[2,2,512,128]{3,2,1,0:T(8,128)S(1)}, f32[2,2,256,256]{3,2,1,0:T(8,128)S(1)}) custom-call(s32[1]{0:T(128)S(6)} %copy.41.live, s32[16,2]{1,0:T(8,128)S(1)} %broadcast_subtract_fusion.off, f32[2,256,2048]{2,1,0:T(8,128)S(1)} %copy-done, f32[2,256,256]{2,1,0:T(8,128)} %collective-permute-done.2.refs_1_, ...), custom_call_target="tpu_custom_call" | custom-call | flops 2147483648 | bytes 8388608 | tf_op jit(solution)/shard_map/group_12/pallas_call | solution.py:192
  117.2 1.3 collective-permute-start.17
  118.6 6.8 %collective-permute-start.19 = (f32[512,256]{1,0:T(8,128)S(1)}, f32[512,256]{1,0:T(8,128)S(1)}, u32[]{:S(2)}, u32[]{:S(2)}) collective-permute-start(f32[512,256]{1,0:T(8,128)S(1)} %dynamic-slice_bitcast_fusion), channel_id=1, source_target_pairs={{0,1},{1,0},{2,3},{3,2},{4,5},{5,4},{6,7},{7,6},{8,9},{9,8},{10,11... | collective-permute-start | bytes 1572872 | tf_op jit(solution)/shard_map/ppermute | solution.py:243
  125.5 6.8 %collective-permute-start.10 = (f32[2,2,256,128]{3,2,1,0:T(8,128)}, f32[2,2,256,128]{3,2,1,0:T(8,128)}, u32[]{:S(2)}, u32[]{:S(2)}) collective-permute-start(f32[2,2,256,128]{3,2,1,0:T(8,128)} %get-tuple-element.59), channel_id=1, source_target_pairs={{0,1},{1,2},{2,3},{4,5},{5,6},{6,7},{8,9},{9,10},{10,11},{12,13},{... | collective-permute-start | bytes 1572872 | tf_op jit(solution)/shard_map/ppermute | solution.py:216
  132.3 5.0 %collective-permute-start.11 = (f32[2,2,256,128]{3,2,1,0:T(8,128)}, f32[2,2,256,128]{3,2,1,0:T(8,128)}, u32[]{:S(2)}, u32[]{:S(2)}) collective-permute-start(f32[2,2,256,128]{3,2,1,0:T(8,128)} %get-tuple-element.58), channel_id=1, source_target_pairs={{0,5},{1,6},{2,7},{4,9},{5,10},{6,11},{8,13},{9,14},{10,15},{12,17... | collective-permute-start | bytes 1572872 | tf_op jit(solution)/shard_map/ppermute | solution.py:224
  137.5 4.1 %collective-permute-start.20 = (f32[128,256]{1,0:T(8,128)S(1)}, f32[128,256]{1,0:T(8,128)S(1)}, u32[]{:S(2)}, u32[]{:S(2)}) collective-permute-start(f32[128,256]{1,0:T(8,128)S(1)} %get-tuple-element.66), channel_id=1, source_target_pairs={{0,2},{1,3},{2,0},{3,1},{4,6},{5,7},{6,4},{7,5},{8,10},{9,11},{10,... | collective-permute-start | bytes 393224 | tf_op jit(solution)/shard_map/ppermute | solution.py:243
  141.7 4.5 %collective-permute-done.17 = f32[2,2,256,128]{3,2,1,0:T(8,128)S(1)} collective-permute-done((f32[2,2,256,128]{3,2,1,0:T(8,128)S(1)}, f32[2,2,256,128]{3,2,1,0:T(8,128)S(1)}, u32[]{:S(2)}, u32[]{:S(2)}) %collective-permute-start.17) | collective-permute-done | bytes 524320 | tf_op jit(solution)/shard_map/ppermute | solution.py:216
  146.2 13.2 %collective-permute-start.21 = (f32[128,256]{1,0:T(8,128)S(1)}, f32[128,256]{1,0:T(8,128)}, u32[]{:S(2)}, u32[]{:S(2)}) collective-permute-start(f32[128,256]{1,0:T(8,128)S(1)} %get-tuple-element.65), channel_id=1, source_target_pairs={{0,64},{1,65},{2,66},{3,67},{4,68},{5,69},{6,70},{7,71},{8,72},{9,... | collective-permute-start | bytes 393224 | tf_op jit(solution)/shard_map/ppermute | solution.py:243
  159.5 5.4 %collective-permute-start.22 = (f32[128,256]{1,0:T(8,128)S(1)}, f32[128,256]{1,0:T(8,128)}, u32[]{:S(2)}, u32[]{:S(2)}) collective-permute-start(f32[128,256]{1,0:T(8,128)S(1)} %get-tuple-element.64), channel_id=1, source_target_pairs={{0,66},{1,67},{2,64},{3,65},{4,70},{5,71},{6,68},{7,69},{8,74},{9,... | collective-permute-start | bytes 393224 | tf_op jit(solution)/shard_map/ppermute | solution.py:243
  171.3 2.3 collective-permute-start.18
  174.8 10.1 %collective-permute-start.24 = (f32[128,256]{1,0:T(8,128)S(1)}, f32[128,256]{1,0:T(8,128)S(1)}, u32[]{:S(2)}, u32[]{:S(2)}) collective-permute-start(f32[128,256]{1,0:T(8,128)S(1)} %fusion.1), channel_id=1, source_target_pairs={{0,32},{1,33},{2,34},{3,35},{4,36},{5,37},{6,38},{7,39},{8,40},{9,... | collective-permute-start | bytes 393224 | tf_op jit(solution)/shard_map/ppermute | solution.py:243
  185.0 1.5 add_bitcast_fusion.6
  187.5 9.3 %collective-permute-done.23 = f32[128,256]{1,0:T(8,128)S(1)} collective-permute-done((f32[128,256]{1,0:T(8,128)S(1)}, f32[128,256]{1,0:T(8,128)S(1)}, u32[]{:S(2)}, u32[]{:S(2)}) %collective-permute-start.23) | collective-permute-done | bytes 131104 | tf_op jit(solution)/shard_map/ppermute | solution.py:243
  196.8 16.5 %collective-permute-done.24 = f32[128,256]{1,0:T(8,128)S(1)} collective-permute-done((f32[128,256]{1,0:T(8,128)S(1)}, f32[128,256]{1,0:T(8,128)S(1)}, u32[]{:S(2)}, u32[]{:S(2)}) %collective-permute-start.24) | collective-permute-done | bytes 131104 | tf_op jit(solution)/shard_map/ppermute | solution.py:243
  214.6 3.5 %collective-permute-start.28 = (f32[128,256]{1,0:T(8,128)S(1)}, f32[128,256]{1,0:T(8,128)S(1)}, u32[]{:S(2)}, u32[]{:S(2)}) collective-permute-start(f32[128,256]{1,0:T(8,128)S(1)} %add_add_fusion.1), channel_id=1, source_target_pairs={{0,12},{1,13},{2,14},{3,15},{4,8},{5,9},{6,10},{7,11},{8,4},{9,5},... | collective-permute-start | bytes 393224 | tf_op jit(solution)/shard_map/ppermute | solution.py:243
  218.1 1.9 constant_dynamic-update-slice_fusion.5
  220.0 2.0 constant_dynamic-update-slice_fusion.4
  222.1 1.8 collective-permute-done.28
  224.0 3.4 %collective-permute-start.30 = (f32[128,256]{1,0:T(8,128)S(1)}, f32[128,256]{1,0:T(8,128)S(1)}, u32[]{:S(2)}, u32[]{:S(2)}) collective-permute-start(f32[128,256]{1,0:T(8,128)S(1)} %add_add_fusion), channel_id=1, source_target_pairs={{0,64},{1,65},{2,66},{3,67},{4,68},{5,69},{6,70},{7,71},{8,72},{9,... | collective-permute-start | bytes 393224 | tf_op jit(solution)/shard_map/ppermute | solution.py:243
  229.5 2.7 %collective-permute-done.30 = f32[128,256]{1,0:T(8,128)S(1)} collective-permute-done((f32[128,256]{1,0:T(8,128)S(1)}, f32[128,256]{1,0:T(8,128)S(1)}, u32[]{:S(2)}, u32[]{:S(2)}) %collective-permute-start.30) | collective-permute-done | bytes 131104 | tf_op jit(solution)/shard_map/ppermute | solution.py:243
  232.2 2.8 %collective-permute-done.31 = f32[128,256]{1,0:T(8,128)S(1)} collective-permute-done((f32[128,256]{1,0:T(8,128)S(1)}, f32[128,256]{1,0:T(8,128)S(1)}, u32[]{:S(2)}, u32[]{:S(2)}) %collective-permute-start.31) | collective-permute-done | bytes 131104 | tf_op jit(solution)/shard_map/ppermute | solution.py:243
  235.9 1.5 collective-permute-start.32
  238.2 1.3 add_bitcast_fusion
  241.0 5.3 %copy.33 = f32[2,256,2048]{2,1,0:T(8,128)} copy(f32[2,256,2048]{1,2,0:T(8,128)} %constant_dynamic-update-slice_fusion) | data formatting | bytes 8388608
  (110 shorter events, 31.5 us)
Async XLA Ops:
  0.6 13.1 %copy-start.16 = (s32[16,2]{0,1:T(2,128)S(1)}, s32[16,2]{0,1:T(2,128)}, u32[]{:S(2)}) copy-start(s32[16,2]{0,1:T(2,128)} %param.12) | copy-start | bytes 388
  0.6 13.2 %copy-start.13 = (f32[2,2,256,256]{3,2,1,0:T(8,128)S(1)}, f32[2,2,256,256]{3,2,1,0:T(8,128)}, u32[]{:S(2)}) copy-start(f32[2,2,256,256]{3,2,1,0:T(8,128)} %param.10) | copy-start | bytes 3145732
  5.0 28.2 %copy-start.3 = (bf16[512,512]{1,0:T(8,128)(2,1)S(1)}, bf16[512,512]{1,0:T(8,128)(2,1)}, u32[]{:S(2)}) copy-start(bf16[512,512]{1,0:T(8,128)(2,1)} %constant.90.clone.refs_5_.refs_7_) | copy-start | bytes 1572868
  5.0 28.2 %copy-start.4 = (bf16[512,512]{1,0:T(8,128)(2,1)S(1)}, bf16[512,512]{1,0:T(8,128)(2,1)}, u32[]{:S(2)}) copy-start(bf16[512,512]{1,0:T(8,128)(2,1)} %constant.91.clone.refs_6_.refs_8_) | copy-start | bytes 1572868
  5.0 28.2 %copy-start.5 = (bf16[512,512]{1,0:T(8,128)(2,1)S(1)}, bf16[512,512]{1,0:T(8,128)(2,1)}, u32[]{:S(2)}) copy-start(bf16[512,512]{1,0:T(8,128)(2,1)} %constant.92.clone.refs_7_.refs_9_) | copy-start | bytes 1572868
  5.0 28.2 %copy-start.6 = (bf16[512,512]{1,0:T(8,128)(2,1)S(1)}, bf16[512,512]{1,0:T(8,128)(2,1)}, u32[]{:S(2)}) copy-start(bf16[512,512]{1,0:T(8,128)(2,1)} %constant.93.clone.refs_8_.refs_10_) | copy-start | bytes 1572868
  5.0 15.5 %collective-permute-start = (f32[2,256,256]{2,1,0:T(8,128)}, f32[2,256,256]{2,1,0:T(8,128)}, u32[]{:S(2)}, u32[]{:S(2)}) collective-permute-start(f32[2,256,256]{2,1,0:T(8,128)} %get-tuple-element.55), channel_id=1, source_target_pairs={{4,0},{8,4},{12,8},{16,12},{20,16},{24,20},{28,24},{32,28},{36,32}... | collective-permute-start | bytes 1572872 | tf_op jit(solution)/shard_map/ppermute | solution.py:216
  6.4 25.3 %collective-permute-start.1 = (f32[2,256,256]{2,1,0:T(8,128)}, f32[2,256,256]{2,1,0:T(8,128)}, u32[]{:S(2)}, u32[]{:S(2)}) collective-permute-start(f32[2,256,256]{2,1,0:T(8,128)} %get-tuple-element.54), channel_id=1, source_target_pairs={{4,0},{8,4},{12,8},{16,12},{20,16},{24,20},{28,24},{32,28},{36,32}... | collective-permute-start | bytes 1572872 | tf_op jit(solution)/shard_map/ppermute | solution.py:216
  7.7 88.1 %collective-permute-start.2 = (f32[2,256,256]{2,1,0:T(8,128)}, f32[2,256,256]{2,1,0:T(8,128)}, u32[]{:S(2)}, u32[]{:S(2)}) collective-permute-start(f32[2,256,256]{2,1,0:T(8,128)} %get-tuple-element.55), channel_id=1, source_target_pairs={{1,0},{2,1},{3,2},{5,4},{6,5},{7,6},{9,8},{10,9},{11,10},{13,12},{... | collective-permute-start | bytes 1572872 | tf_op jit(solution)/shard_map/ppermute | solution.py:216
  11.1 31.9 %collective-permute-start.9 = (f32[2,256,256]{2,1,0:T(8,128)}, f32[2,256,256]{2,1,0:T(8,128)}, u32[]{:S(2)}, u32[]{:S(2)}) collective-permute-start(f32[2,256,256]{2,1,0:T(8,128)} %get-tuple-element.48), channel_id=1, source_target_pairs={{4,0},{8,4},{12,8},{16,12},{20,16},{24,20},{28,24},{32,28},{36,32}... | collective-permute-start | bytes 1572872 | tf_op jit(solution)/shard_map/ppermute | solution.py:216
  12.4 41.8 %collective-permute-start.8 = (f32[2,256,256]{2,1,0:T(8,128)}, f32[2,256,256]{2,1,0:T(8,128)}, u32[]{:S(2)}, u32[]{:S(2)}) collective-permute-start(f32[2,256,256]{2,1,0:T(8,128)} %get-tuple-element.49), channel_id=1, source_target_pairs={{4,0},{8,4},{12,8},{16,12},{20,16},{24,20},{28,24},{32,28},{36,32}... | collective-permute-start | bytes 1572872 | tf_op jit(solution)/shard_map/ppermute | solution.py:216
  20.5 44.8 %collective-permute-start.7 = (f32[2,256,256]{2,1,0:T(8,128)}, f32[2,256,256]{2,1,0:T(8,128)S(1)}, u32[]{:S(2)}, u32[]{:S(2)}) collective-permute-start(f32[2,256,256]{2,1,0:T(8,128)} %get-tuple-element.50), channel_id=1, source_target_pairs={{4,0},{8,4},{12,8},{16,12},{20,16},{24,20},{28,24},{32,28},{36,32}... | collective-permute-start | bytes 1572872 | tf_op jit(solution)/shard_map/ppermute | solution.py:216
  31.7 44.8 %collective-permute-start.6 = (f32[2,256,256]{2,1,0:T(8,128)}, f32[2,256,256]{2,1,0:T(8,128)S(1)}, u32[]{:S(2)}, u32[]{:S(2)}) collective-permute-start(f32[2,256,256]{2,1,0:T(8,128)} %get-tuple-element.51), channel_id=1, source_target_pairs={{4,0},{8,4},{12,8},{16,12},{20,16},{24,20},{28,24},{32,28},{36,32}... | collective-permute-start | bytes 1572872 | tf_op jit(solution)/shard_map/ppermute | solution.py:216
  37.6 5.4 %copy-start.15 = (f32[2,256,256]{2,1,0:T(8,128)S(1)}, f32[2,256,256]{2,1,0:T(8,128)}, u32[]{:S(2)}) copy-start(f32[2,256,256]{2,1,0:T(8,128)} %get-tuple-element.53) | copy-start | bytes 1572868
  37.6 6.7 %copy-start.2 = (f32[16,256,256]{2,1,0:T(8,128)S(1)}, f32[16,256,256]{2,1,0:T(8,128)}, u32[]{:S(2)}) copy-start(f32[16,256,256]{2,1,0:T(8,128)} %refs_5_.7) | copy-start | bytes 12582916
  38.8 6.7 %copy-start.9 = (f32[2,2,512,128]{3,2,1,0:T(8,128)}, f32[2,2,512,128]{3,2,1,0:T(8,128)S(1)}, u32[]{:S(2)}) copy-start(f32[2,2,512,128]{3,2,1,0:T(8,128)S(1)} %get-tuple-element.23) | copy-start | bytes 3145732
  43.0 44.8 %collective-permute-start.3 = (f32[2,256,256]{2,1,0:T(8,128)S(1)}, f32[2,256,256]{2,1,0:T(8,128)S(1)}, u32[]{:S(2)}, u32[]{:S(2)}) collective-permute-start(f32[2,256,256]{2,1,0:T(8,128)S(1)} %copy-done.15), channel_id=1, source_target_pairs={{4,0},{8,4},{12,8},{16,12},{20,16},{24,20},{28,24},{32,28},{36,32}... | collective-permute-start | bytes 1572872 | tf_op jit(solution)/shard_map/ppermute | solution.py:216
  44.3 9.9 %copy-start.14 = (f32[2,256,256]{2,1,0:T(8,128)S(1)}, f32[2,256,256]{2,1,0:T(8,128)}, u32[]{:S(2)}) copy-start(f32[2,256,256]{2,1,0:T(8,128)} %get-tuple-element.52) | copy-start | bytes 1572868
  54.2 45.9 %collective-permute-start.4 = (f32[2,256,256]{2,1,0:T(8,128)S(1)}, f32[2,256,256]{2,1,0:T(8,128)S(1)}, u32[]{:S(2)}, u32[]{:S(2)}) collective-permute-start(f32[2,256,256]{2,1,0:T(8,128)S(1)} %copy-done.14), channel_id=1, source_target_pairs={{4,0},{8,4},{12,8},{16,12},{20,16},{24,20},{28,24},{32,28},{36,32}... | collective-permute-start | bytes 1572872 | tf_op jit(solution)/shard_map/ppermute | solution.py:216
  65.3 42.2 %collective-permute-start.5 = (f32[2,256,256]{2,1,0:T(8,128)}, f32[2,256,256]{2,1,0:T(8,128)S(1)}, u32[]{:S(2)}, u32[]{:S(2)}) collective-permute-start(f32[2,256,256]{2,1,0:T(8,128)} %collective-permute-done.refs_1_), channel_id=1, source_target_pairs={{1,0},{2,1},{3,2},{5,4},{6,5},{7,6},{9,8},{10,9},{11,10},{13,12},{... | collective-permute-start | bytes 1572872 | tf_op jit(solution)/shard_map/ppermute | solution.py:216
  76.6 98.2 %collective-permute-start.12 = (f32[2,2,256,128]{3,2,1,0:T(8,128)}, f32[2,2,256,128]{3,2,1,0:T(8,128)}, u32[]{:S(2)}, u32[]{:S(2)}) collective-permute-start(f32[2,2,256,128]{3,2,1,0:T(8,128)} %slice.84), channel_id=1, source_target_pairs={{0,4},{4,8},{8,12},{12,16},{16,20},{20,24},{24,28},{28,32},{32,36}... | collective-permute-start | bytes 1572872 | tf_op jit(solution)/shard_map/ppermute | solution.py:216
  87.8 29.4 %collective-permute-start.13 = (f32[2,2,256,128]{3,2,1,0:T(8,128)S(1)}, f32[2,2,256,128]{3,2,1,0:T(8,128)S(1)}, u32[]{:S(2)}, u32[]{:S(2)}) collective-permute-start(f32[2,2,256,128]{3,2,1,0:T(8,128)S(1)} %slice.86), channel_id=1, source_target_pairs={{0,4},{4,8},{8,12},{12,16},{16,20},{20,24},{24,28},{28,32},{32,36}... | collective-permute-start | bytes 1572872 | tf_op jit(solution)/shard_map/ppermute | solution.py:216
  95.9 22.7 %collective-permute-start.14 = (f32[2,2,256,128]{3,2,1,0:T(8,128)S(1)}, f32[2,2,256,128]{3,2,1,0:T(8,128)S(1)}, u32[]{:S(2)}, u32[]{:S(2)}) collective-permute-start(f32[2,2,256,128]{3,2,1,0:T(8,128)S(1)} %slice.88), channel_id=1, source_target_pairs={{0,4},{4,8},{8,12},{12,16},{16,20},{20,24},{24,28},{28,32},{32,36}... | collective-permute-start | bytes 1572872 | tf_op jit(solution)/shard_map/ppermute | solution.py:216
  100.1 25.4 %collective-permute-start.15 = (f32[2,2,256,128]{3,2,1,0:T(8,128)S(1)}, f32[2,2,256,128]{3,2,1,0:T(8,128)S(1)}, u32[]{:S(2)}, u32[]{:S(2)}) collective-permute-start(f32[2,2,256,128]{3,2,1,0:T(8,128)S(1)} %slice.90), channel_id=1, source_target_pairs={{0,4},{4,8},{8,12},{12,16},{16,20},{20,24},{24,28},{28,32},{32,36}... | collective-permute-start | bytes 1572872 | tf_op jit(solution)/shard_map/ppermute | solution.py:216
  107.5 30.0 %collective-permute-start.16 = (f32[2,2,256,128]{3,2,1,0:T(8,128)S(1)}, f32[2,2,256,128]{3,2,1,0:T(8,128)S(1)}, u32[]{:S(2)}, u32[]{:S(2)}) collective-permute-start(f32[2,2,256,128]{3,2,1,0:T(8,128)S(1)} %slice.92), channel_id=1, source_target_pairs={{0,4},{4,8},{8,12},{12,16},{16,20},{20,24},{24,28},{28,32},{32,36}... | collective-permute-start | bytes 1572872 | tf_op jit(solution)/shard_map/ppermute | solution.py:216
  116.0 49.8 %copy-start.7 = (f32[2,4,512,128]{3,2,1,0:T(8,128)}, f32[2,4,512,128]{3,2,1,0:T(8,128)S(1)}, u32[]{:S(2)}) copy-start(f32[2,4,512,128]{3,2,1,0:T(8,128)S(1)} %get-tuple-element.42) | copy-start | bytes 6291460
  117.2 29.0 %collective-permute-start.17 = (f32[2,2,256,128]{3,2,1,0:T(8,128)S(1)}, f32[2,2,256,128]{3,2,1,0:T(8,128)S(1)}, u32[]{:S(2)}, u32[]{:S(2)}) collective-permute-start(f32[2,2,256,128]{3,2,1,0:T(8,128)S(1)} %slice.94), channel_id=1, source_target_pairs={{0,4},{4,8},{8,12},{12,16},{16,20},{20,24},{24,28},{28,32},{32,36}... | collective-permute-start | bytes 1572872 | tf_op jit(solution)/shard_map/ppermute | solution.py:216
  118.6 13.7 %collective-permute-start.19 = (f32[512,256]{1,0:T(8,128)S(1)}, f32[512,256]{1,0:T(8,128)S(1)}, u32[]{:S(2)}, u32[]{:S(2)}) collective-permute-start(f32[512,256]{1,0:T(8,128)S(1)} %dynamic-slice_bitcast_fusion), channel_id=1, source_target_pairs={{0,1},{1,0},{2,3},{3,2},{4,5},{5,4},{6,7},{7,6},{8,9},{9,8},{10,11... | collective-permute-start | bytes 1572872 | tf_op jit(solution)/shard_map/ppermute | solution.py:243
  125.5 59.5 %collective-permute-start.10 = (f32[2,2,256,128]{3,2,1,0:T(8,128)}, f32[2,2,256,128]{3,2,1,0:T(8,128)}, u32[]{:S(2)}, u32[]{:S(2)}) collective-permute-start(f32[2,2,256,128]{3,2,1,0:T(8,128)} %get-tuple-element.59), channel_id=1, source_target_pairs={{0,1},{1,2},{2,3},{4,5},{5,6},{6,7},{8,9},{9,10},{10,11},{12,13},{... | collective-permute-start | bytes 1572872 | tf_op jit(solution)/shard_map/ppermute | solution.py:216
  132.3 52.6 %collective-permute-start.11 = (f32[2,2,256,128]{3,2,1,0:T(8,128)}, f32[2,2,256,128]{3,2,1,0:T(8,128)}, u32[]{:S(2)}, u32[]{:S(2)}) collective-permute-start(f32[2,2,256,128]{3,2,1,0:T(8,128)} %get-tuple-element.58), channel_id=1, source_target_pairs={{0,5},{1,6},{2,7},{4,9},{5,10},{6,11},{8,13},{9,14},{10,15},{12,17... | collective-permute-start | bytes 1572872 | tf_op jit(solution)/shard_map/ppermute | solution.py:224
  137.5 28.3 %copy-start.12 = (f32[512,256]{1,0:T(8,128)}, f32[512,256]{1,0:T(8,128)S(1)}, u32[]{:S(2)}) copy-start(f32[512,256]{1,0:T(8,128)S(1)} %bitcast_add_fusion) | copy-start | bytes 1572868
  137.5 21.9 %collective-permute-start.20 = (f32[128,256]{1,0:T(8,128)S(1)}, f32[128,256]{1,0:T(8,128)S(1)}, u32[]{:S(2)}, u32[]{:S(2)}) collective-permute-start(f32[128,256]{1,0:T(8,128)S(1)} %get-tuple-element.66), channel_id=1, source_target_pairs={{0,2},{1,3},{2,0},{3,1},{4,6},{5,7},{6,4},{7,5},{8,10},{9,11},{10,... | collective-permute-start | bytes 393224 | tf_op jit(solution)/shard_map/ppermute | solution.py:243
  146.2 25.1 %collective-permute-start.21 = (f32[128,256]{1,0:T(8,128)S(1)}, f32[128,256]{1,0:T(8,128)}, u32[]{:S(2)}, u32[]{:S(2)}) collective-permute-start(f32[128,256]{1,0:T(8,128)S(1)} %get-tuple-element.65), channel_id=1, source_target_pairs={{0,64},{1,65},{2,66},{3,67},{4,68},{5,69},{6,70},{7,71},{8,72},{9,... | collective-permute-start | bytes 393224 | tf_op jit(solution)/shard_map/ppermute | solution.py:243
  159.5 14.2 %collective-permute-start.22 = (f32[128,256]{1,0:T(8,128)S(1)}, f32[128,256]{1,0:T(8,128)}, u32[]{:S(2)}, u32[]{:S(2)}) collective-permute-start(f32[128,256]{1,0:T(8,128)S(1)} %get-tuple-element.64), channel_id=1, source_target_pairs={{0,66},{1,67},{2,64},{3,65},{4,70},{5,71},{6,68},{7,69},{8,74},{9,... | collective-permute-start | bytes 393224 | tf_op jit(solution)/shard_map/ppermute | solution.py:243
  165.7 19.2 %copy-start.10 = (f32[2,2,512,128]{3,2,1,0:T(8,128)S(1)}, f32[2,2,512,128]{3,2,1,0:T(8,128)}, u32[]{:S(2)}) copy-start(f32[2,2,512,128]{3,2,1,0:T(8,128)} %copy-done.9) | copy-start | bytes 3145732
  171.3 66.9 %collective-permute-start.18 = (f32[2,4,256,128]{3,2,1,0:T(8,128)}, f32[2,4,256,128]{3,2,1,0:T(8,128)}, u32[]{:S(2)}, u32[]{:S(2)}) collective-permute-start(f32[2,4,256,128]{3,2,1,0:T(8,128)} %slice.96), channel_id=1, source_target_pairs={{0,4},{4,8},{8,12},{12,16},{16,20},{20,24},{24,28},{28,32},{32,36}... | collective-permute-start | bytes 3145736 | tf_op jit(solution)/shard_map/ppermute | solution.py:216
  174.7 53.1 %copy-start.11 = (f32[2,256,2,128]{1,3,2,0:T(8,128)S(1)}, f32[2,256,2,128]{1,3,2,0:T(8,128)}, u32[]{:S(2)}) copy-start(f32[2,256,2,128]{1,3,2,0:T(8,128)} %copy.28) | copy-start | bytes 1572868
  174.7 22.1 %collective-permute-start.23 = (f32[128,256]{1,0:T(8,128)S(1)}, f32[128,256]{1,0:T(8,128)S(1)}, u32[]{:S(2)}, u32[]{:S(2)}) collective-permute-start(f32[128,256]{1,0:T(8,128)S(1)} %fusion.1), channel_id=1, source_target_pairs={{0,16},{1,17},{2,18},{3,19},{4,20},{5,21},{6,22},{7,23},{8,24},{9,... | collective-permute-start | bytes 393224 | tf_op jit(solution)/shard_map/ppermute | solution.py:243
  174.8 38.5 %collective-permute-start.24 = (f32[128,256]{1,0:T(8,128)S(1)}, f32[128,256]{1,0:T(8,128)S(1)}, u32[]{:S(2)}, u32[]{:S(2)}) collective-permute-start(f32[128,256]{1,0:T(8,128)S(1)} %fusion.1), channel_id=1, source_target_pairs={{0,32},{1,33},{2,34},{3,35},{4,36},{5,37},{6,38},{7,39},{8,40},{9,... | collective-permute-start | bytes 393224 | tf_op jit(solution)/shard_map/ppermute | solution.py:243
  184.9 28.3 %collective-permute-start.25 = (f32[128,256]{1,0:T(8,128)S(1)}, f32[128,256]{1,0:T(8,128)}, u32[]{:S(2)}, u32[]{:S(2)}) collective-permute-start(f32[128,256]{1,0:T(8,128)S(1)} %fusion.1), channel_id=1, source_target_pairs={{0,48},{1,49},{2,50},{3,51},{4,52},{5,53},{6,54},{7,55},{8,56},{9,... | collective-permute-start | bytes 393224 | tf_op jit(solution)/shard_map/ppermute | solution.py:243
  214.2 7.9 %collective-permute-start.26 = (f32[128,256]{1,0:T(8,128)S(1)}, f32[128,256]{1,0:T(8,128)S(1)}, u32[]{:S(2)}, u32[]{:S(2)}) collective-permute-start(f32[128,256]{1,0:T(8,128)S(1)} %add_add_fusion.1), channel_id=1, source_target_pairs={{0,4},{1,5},{2,6},{3,7},{4,0},{5,1},{6,2},{7,3},{8,12},{9,13},{10,... | collective-permute-start | bytes 393224 | tf_op jit(solution)/shard_map/ppermute | solution.py:243
  214.3 7.8 %collective-permute-start.27 = (f32[128,256]{1,0:T(8,128)S(1)}, f32[128,256]{1,0:T(8,128)S(1)}, u32[]{:S(2)}, u32[]{:S(2)}) collective-permute-start(f32[128,256]{1,0:T(8,128)S(1)} %add_add_fusion.1), channel_id=1, source_target_pairs={{0,8},{1,9},{2,10},{3,11},{4,12},{5,13},{6,14},{7,15},{8,0},{9,1},... | collective-permute-start | bytes 393224 | tf_op jit(solution)/shard_map/ppermute | solution.py:243
  214.6 9.2 %collective-permute-start.28 = (f32[128,256]{1,0:T(8,128)S(1)}, f32[128,256]{1,0:T(8,128)S(1)}, u32[]{:S(2)}, u32[]{:S(2)}) collective-permute-start(f32[128,256]{1,0:T(8,128)S(1)} %add_add_fusion.1), channel_id=1, source_target_pairs={{0,12},{1,13},{2,14},{3,15},{4,8},{5,9},{6,10},{7,11},{8,4},{9,5},... | collective-permute-start | bytes 393224 | tf_op jit(solution)/shard_map/ppermute | solution.py:243
  220.0 18.2 %copy-start.8 = (f32[2,4,512,128]{3,2,1,0:T(8,128)S(1)}, f32[2,4,512,128]{3,2,1,0:T(8,128)}, u32[]{:S(2)}) copy-start(f32[2,4,512,128]{3,2,1,0:T(8,128)} %copy-done.7) | copy-start | bytes 6291460
  223.9 5.6 %collective-permute-start.29 = (f32[128,256]{1,0:T(8,128)S(1)}, f32[128,256]{1,0:T(8,128)S(1)}, u32[]{:S(2)}, u32[]{:S(2)}) collective-permute-start(f32[128,256]{1,0:T(8,128)S(1)} %add_add_fusion), channel_id=1, source_target_pairs={{0,2},{1,3},{2,0},{3,1},{4,6},{5,7},{6,4},{7,5},{8,10},{9,11},{10,... | collective-permute-start | bytes 393224 | tf_op jit(solution)/shard_map/ppermute | solution.py:243
  224.0 8.2 %collective-permute-start.30 = (f32[128,256]{1,0:T(8,128)S(1)}, f32[128,256]{1,0:T(8,128)S(1)}, u32[]{:S(2)}, u32[]{:S(2)}) collective-permute-start(f32[128,256]{1,0:T(8,128)S(1)} %add_add_fusion), channel_id=1, source_target_pairs={{0,64},{1,65},{2,66},{3,67},{4,68},{5,69},{6,70},{7,71},{8,72},{9,... | collective-permute-start | bytes 393224 | tf_op jit(solution)/shard_map/ppermute | solution.py:243
  227.3 7.6 %collective-permute-start.31 = (f32[128,256]{1,0:T(8,128)S(1)}, f32[128,256]{1,0:T(8,128)S(1)}, u32[]{:S(2)}, u32[]{:S(2)}) collective-permute-start(f32[128,256]{1,0:T(8,128)S(1)} %add_add_fusion), channel_id=1, source_target_pairs={{0,66},{1,67},{2,64},{3,65},{4,70},{5,71},{6,68},{7,69},{8,74},{9,... | collective-permute-start | bytes 393224 | tf_op jit(solution)/shard_map/ppermute | solution.py:243
  235.9 10.4 %collective-permute-start.32 = (f32[512,256]{1,0:T(8,128)}, f32[512,256]{1,0:T(8,128)S(1)}, u32[]{:S(2)}, u32[]{:S(2)}) collective-permute-start(f32[512,256]{1,0:T(8,128)} %pad_maximum_fusion.1), channel_id=1, source_target_pairs={{0,1},{1,0},{2,3},{3,2},{4,5},{5,4},{6,7},{7,6},{8,9},{9,8},{10,11... | collective-permute-start | bytes 1572872 | tf_op jit(solution)/shard_map/ppermute | solution.py:243
  (2 other events, 4.4 us)

commit v2 on v1

--- a/solution.py
+++ b/solution.py
@@ -104,17 +104,14 @@
                 view[rows, :] = view[rows, :] + moved[half * p : half * (p + 1), LANE * j : LANE * (j + 1)]
 
 
-def group_kernel(first, count, own_blocks, live, off, *refs):
+def group_kernel(first, count, homes, n_after, last, live, off, *refs):
     wide = count + 2
-    n_halo = wide // 2
-    has_right = first + wide > own_blocks
     refs = list(refs)
-    field = refs.pop(0)
-    right = refs.pop(0) if has_right else None
-    halos = [refs.pop(0) for _ in range(n_halo)]
+    sources = refs[: len(homes[2])]
+    refs = refs[len(homes[2]) + n_after :]
     measured, probe, t0, t1, t2, t3, carry, acc_in = refs[:8]
-    done, carry_out, acc = refs[8:11]
-    ext, grad, frame, picked, load_sem, frame_sem = refs[11:]
+    upper, lower, carry_out, acc = refs[8:12]
+    ext, grad, frame, picked, load_sem, frame_sem = refs[12:]
 
     def pick(q, n):
         b = off[q, 1] // LANE - first
@@ -125,19 +122,12 @@
 
     def loads():
         out = []
-        for b in range(wide):
-            at = (first + b) * LANE
-            if first + b < own_blocks:
-                src = field.at[:, :, at : at + LANE]
-            else:
-                at -= own_blocks * LANE
-                src = right.at[:, :, at : at + LANE]
-            out.append(pltpu.make_async_copy(src, ext.at[:, b, 0:SIZE, :], load_sem.at[2 * b]))
-            low = (b % 2) * LANE
-            src = halos[b // 2].at[:, :, low : low + LANE]
-            out.append(
-                pltpu.make_async_copy(src, ext.at[:, b, SIZE : 2 * SIZE, :], load_sem.at[2 * b + 1])
-            )
+        for half in (0, 1):
+            for b in range(wide):
+                which, row, at = homes[half][b]
+                src = sources[which].at[:, row : row + SIZE, at : at + LANE]
+                dst = ext.at[:, b, SIZE * half : SIZE * (half + 1), :]
+                out.append(pltpu.make_async_copy(src, dst, load_sem.at[2 * b + half]))
         return out
 
     def frame_copy(i):
@@ -172,28 +162,63 @@
         return 0
 
     lax.fori_loop(0, n, step, 0)
-    done[...] = grad[:, 0:count]
+    upper[...] = grad[:, 0:count, :SIZE]
+    lower[...] = grad[:, 0:count, SIZE:]
     carry_out[...] = grad[:, count:]
-
-
-def run_group(first, count, own_blocks, live, off, field, right, halos, measured, probe, tabs, carry, acc):
+    if last:
+        for k in (0, 1):
+            for part in (0, 1):
+                for b in (0, 1):
+                    view = ext.at[part, 2 * k + b]
+                    at = slice(LANE * b, LANE * (b + 1))
+                    for p in (0, 1):
+                        rows = pl.ds(p, SIZE // 2, stride=2)
+                        view[rows, :] = acc[k, part, LANE * p : LANE * (p + 1), at]
+                    acc[k, part, :, at] = view[0:SIZE, :]
+
+
+ANYWHERE = pl.BlockSpec(memory_space=pl.ANY)
+IN_SMEM = pl.BlockSpec(memory_space=pltpu.SMEM)
+IN_VMEM = pl.BlockSpec(memory_space=pltpu.VMEM)
+
+
+def run_group(first, count, bounds, live, off, field, halos, corner, measured, probe, tabs, carry, acc, after):
     wide = count + 2
-    anywhere = pl.BlockSpec(memory_space=pl.ANY)
-    smem = pl.BlockSpec(memory_space=pltpu.SMEM)
-    vmem = pl.BlockSpec(memory_space=pltpu.VMEM)
-    rights = [right] if first + wide > own_blocks else []
-    args = [live, off, field, *rights, *halos, measured, probe, *tabs, carry, acc]
-    specs = [smem, smem] + [anywhere] * (2 + len(rights) + len(halos)) + [vmem] * 7
+    arrays, homes = [], [[], []]
+
+    def index_in(array):
+        for i, other in enumerate(arrays):
+            if other is array:
+                return i
+        arrays.append(array)
+        return len(arrays) - 1
+
+    for b in range(first, first + wide):
+        if b < bounds[-1]:
+            chunk = next(i for i, end in enumerate(bounds) if b < end)
+            begin = bounds[chunk - 1] if chunk else 0
+            homes[0].append((index_in(field), 0, b * LANE))
+            homes[1].append((index_in(halos[chunk]), 0, (b - begin) * LANE))
+        else:
+            at = (b - bounds[-1]) * LANE
+            homes[0].append((index_in(corner), 0, at))
+            homes[1].append((index_in(corner), SIZE, at))
+    homes.append(arrays)
+    args = [live, off, *arrays, *after, measured, probe, *tabs, carry, acc]
+    specs = [IN_SMEM] * 2 + [ANYWHERE] * (1 + len(arrays) + len(after)) + [IN_VMEM] * 7
+    part = jax.ShapeDtypeStruct((2, count, SIZE, LANE), f32)
     out_shape = (
-        jax.ShapeDtypeStruct((2, count, 2 * SIZE, LANE), f32),
+        part,
+        part,
         jax.ShapeDtypeStruct((2, 2, 2 * SIZE, LANE), f32),
         jax.ShapeDtypeStruct((2, 2, SIZE, SIZE), f32),
     )
     return pl.pallas_call(
-        functools.partial(group_kernel, first, count, own_blocks),
+        functools.partial(group_kernel, first, count, (homes[0], homes[1], [None] * len(arrays)),
+            len(after), first + count == bounds[-1]),
         out_shape=out_shape,
         in_specs=specs,
-        out_specs=(vmem,) * 3,
+        out_specs=(IN_VMEM,) * 4,
         scratch_shapes=[
             pltpu.VMEM((2, wide, 2 * SIZE, LANE), f32),
             pltpu.VMEM((2, wide, 2 * SIZE, LANE), f32),
@@ -202,18 +227,70 @@
             pltpu.SemaphoreType.DMA((2 * wide,)),
             pltpu.SemaphoreType.DMA((2,)),
         ],
-        compiler_params=pltpu.CompilerParams(vmem_limit_bytes=32 * 2**20),
-        cost_estimate=pl.CostEstimate(
-            flops=2 * 1024**3, bytes_accessed=8 * 2**20, transcendentals=0
-        ),
+        compiler_params=pltpu.CompilerParams(vmem_limit_bytes=30 * 2**20),
+        cost_estimate=pl.CostEstimate(flops=2**34, bytes_accessed=2**12, transcendentals=0),
         name=f"group_{first}",
     )(*args)
 
 
-def shifted(array, axis, by):
+def finish_kernel(parts, extra, *refs):
+    refs = list(refs)
+    uppers = [refs.pop(0) for _ in parts]
+    comings = [refs.pop(0) for _ in parts]
+    extras = [refs.pop(0) for _ in range(extra)]
+    refs = refs[-3:]
+    out, buf, sem = refs
+    copies = []
+    low = parts[0][0]
+    for (first, count), upper, coming in zip(parts, uppers, comings):
+        for b in range(count):
+            value = upper[:, b] + coming[:, b]
+            if first + b < 2:
+                for more in extras:
+                    value = value + more[:, b]
+            at = (first + b - low) * LANE
+            buf[:, :, at : at + LANE] = value
+        begin, end = (first - low) * LANE, (first - low + count) * LANE
+        copy = pltpu.make_async_copy(
+            buf.at[:, :, begin:end],
+            out.at[:, :, first * LANE : (first + count) * LANE],
+            sem.at[len(copies)],
+        )
+        copy.start()
+        copies.append(copy)
+    for copy in copies:
+        copy.wait()
+
+
+def finish(parts, uppers, comings, extras, shape, onto):
+    total = sum(count for _, count in parts)
+    args = [*uppers, *comings, *extras]
+    specs = [IN_VMEM] * len(args)
+    aliases = {}
+    if onto is not None:
+        aliases = {len(args): 0}
+        args.append(onto)
+        specs.append(ANYWHERE)
+    return pl.pallas_call(
+        functools.partial(finish_kernel, parts, len(extras)),
+        out_shape=jax.ShapeDtypeStruct(shape, f32),
+        in_specs=specs,
+        out_specs=ANYWHERE,
+        scratch_shapes=[
+            pltpu.VMEM((2, SIZE, total * LANE), f32),
+            pltpu.SemaphoreType.DMA((len(parts),)),
+        ],
+        input_output_aliases=aliases,
+        compiler_params=pltpu.CompilerParams(vmem_limit_bytes=24 * 2**20),
+        name=f"finish_{parts[0][0]}",
+    )(*args)
+
+
+def shifted(array, axis, by, name):
     count = lax.axis_size(axis)
     pairs = [(i, i + by) for i in range(count) if 0 <= i + by < count]
-    return lax.ppermute(array, axis, pairs)
+    with jax.named_scope(name):
+        return lax.ppermute(array, axis, pairs)
 
 
 def shifted_both(array):
@@ -221,7 +298,8 @@
     pairs = [
         (i * cols + j, (i + 1) * cols + j + 1) for i in range(rows - 1) for j in range(cols - 1)
     ]
-    return lax.ppermute(array, AXES, pairs)
+    with jax.named_scope("slant"):
+        return lax.ppermute(array, AXES, pairs)
 
 
 def place_of(index):
@@ -240,10 +318,11 @@
         place = place_of(i)
         place[axis] ^= bits
         pairs.append((i, index_of(place)))
-    return lax.ppermute(array, AXES, pairs)
-
-
-def sum_everywhere(total):
+    with jax.named_scope("swap_" + "cyzx"[axis] + str(bits)):
+        return lax.ppermute(array, AXES, pairs)
+
+
+def sum_everywhere(total, scale, before_x, after_x):
     s = lax.axis_index("scan")
     m = lax.axis_index("mode")
     core, y = m % 2, (s // 16) * 2 + m // 2
@@ -253,19 +332,22 @@
     v = v.reshape(4, 128, 256)
     a, b, c = [swapped(pick(v, y ^ k), 1, k) for k in (1, 2, 3)]
     v = (pick(v, y) + a) + (b + c)
-    for axis in (2, 3):
-        a, b, c = [swapped(v, axis, k) for k in (1, 2, 3)]
-        v = (v + a) + (b + c)
+    v, before_x = lax.optimization_barrier((v, before_x))
+    v = v + swapped(v, 3, 1)
+    v = v + swapped(v, 3, 2)
+    v, after_x = lax.optimization_barrier((v, after_x))
+    v = v + swapped(v, 2, 1)
+    v = v + swapped(v, 2, 2)
+    v = v * scale
     parts = jnp.stack([v] + [swapped(v, 1, k) for k in (1, 2, 3)])
     v = jnp.concatenate([pick(parts, y ^ i) for i in range(4)], 0)
     w = swapped(v, 0, 1)
     low = jnp.where(core == 0, v, w)
     high = jnp.where(core == 0, w, v)
-    return jnp.stack([low, high]).reshape(total.shape)
-
-
-def unblocked(part):
-    return jnp.transpose(part, (0, 2, 1, 3)).reshape(2, SIZE, -1)
+    return jnp.stack([low, high]).reshape(total.shape), before_x, after_x
+
+
+BOUNDS = (6, 9, 12, 15, 16)
 
 
 def shards(field, probe, measured, offsets, live):
@@ -274,29 +356,36 @@
     off = offsets - base[None, :]
     tabs = [jnp.asarray(t) for t in tables()]
     probe_rows = probe.reshape(2, 2, 128, 2, 256).transpose(0, 1, 3, 2, 4).reshape(probe.shape)
-    chunks = cols // CHUNK
-    blocks = cols // LANE
-    halos = [shifted(field[:, :, CHUNK * i : CHUNK * (i + 1)], "scan", -1) for i in range(chunks)]
-    right = shifted(field[:, :, :CHUNK], "mode", -1)
-    halos.append(shifted(halos[0], "mode", -1))
+    head, field_rest = lax.optimization_barrier((field[:, :, : LANE * BOUNDS[0]], field))
+    halos = [shifted(head, "scan", -1, "halo_0")]
+    halos += [
+        shifted(field_rest[:, :, LANE * a : LANE * b], "scan", -1, f"halo_{i + 1}")
+        for i, (a, b) in enumerate(zip(BOUNDS[:-1], BOUNDS[1:]))
+    ]
+    beside = jnp.concatenate([field[:, :, :SIZE], halos[0][:, :, :SIZE]], 1)
+    corner = shifted(beside, "mode", -1, "corner")
     carry = jnp.zeros((2, 2, 2 * SIZE, LANE), f32)
     acc = jnp.zeros(probe.shape, f32)
-    uppers, lowers = [], []
-    plan = [(2 * i, 2) for i in range(chunks - 2)] + [(blocks - 4, 4)]
-    for first, count in plan:
-        near = halos[first // 2 : first // 2 + count // 2 + 1]
-        done, carry, acc = run_group(
-            first, count, blocks, live, off, field, right, near, measured, probe_rows, tabs, carry, acc
+    ends = [b - 2 for b in BOUNDS[:-1]] + [BOUNDS[-1]]
+    plan = [(a, b - a) for a, b in zip([0] + ends[:-1], ends)]
+    uppers, comings = [], []
+    for i, (first, count) in enumerate(plan):
+        after = [comings[i - 2]] if i >= 2 else []
+        upper, lower, carry, acc = run_group(
+            first, count, BOUNDS, live, off, field, halos, corner, measured, probe_rows, tabs, carry, acc, after
         )
-        uppers.append(unblocked(done[:, :, :SIZE]))
-        lowers.append(unblocked(shifted(done[:, :, SIZE:], "scan", 1)))
-    beside = unblocked(shifted(carry[:, :, :SIZE], "mode", 1)) + unblocked(shifted_both(carry[:, :, SIZE:]))
-    uppers[0] = uppers[0] + beside
-    step = jnp.concatenate([a + b for a, b in zip(uppers, lowers)], 2)
-    acc = sum_everywhere(acc)
-    acc = acc.reshape(2, 2, 2, 128, 256).transpose(0, 1, 3, 2, 4).reshape(probe.shape)
+        uppers.append(upper)
+        if i + 1 < len(plan):
+            comings.append(shifted(lower, "scan", 1, f"grad_{i}"))
     slots_all = lax.axis_size("scan") * lax.axis_size("mode") * SLOTS
-    return (step, acc * (1.0 / math.sqrt(slots_all)))
+    slant = shifted_both(carry[:, :, SIZE:])
+    acc, (comings[-1], slant), (last, over) = sum_everywhere(
+        acc, 1.0 / math.sqrt(slots_all), (comings[-1], slant), (lower, carry[:, :, :SIZE])
+    )
+    extras = [slant, shifted(over, "mode", 1, "over")]
+    step = finish(plan[:-1], uppers[:-1], comings, extras, field.shape, None)
+    step = finish(plan[-1:], uppers[-1:], [shifted(last, "scan", 1, "grad_last")], [], field.shape, step)
+    return (step, acc)
 
 
 def solution(mesh):

time: 252 us -> 257 us (1.020)
  the two profiles are of different devices: /device:TPU:1 before, /device:TPU:104 now
where the time goes in v2:
time: 257 us; the launch traced here: 258 us
  waiting for transfers between devices  138 us (54%)
  starting transfers between devices  60.8 us (24%)
  local copies, waits for them, and re-layouts  34.6 us (13%)
  Pallas kernels  17.6 us (7%)
  other arithmetic  5.58 us (2%)
    ppermute x12, waiting for transfers between devices, shifted(): return lax.ppermute(array, axis, pairs)  84.5 us
    ppermute x12, waiting for transfers between devices, swapped(): return lax.ppermute(array, AXES, pairs)  53.3 us
    ppermute x12, starting transfers between devices, shifted(): return lax.ppermute(array, axis, pairs)  47.6 us
    unnamed x79, local copies, waits for them, and re-layouts  20.9 us
    pallas_call x5, Pallas kernels, run_group(): pl.pallas_call(functools.partial(group_kernel, first, count, (homes[0], h...  12.1 us
    ppermute x12, starting transfers between devices, swapped(): return lax.ppermute(array, AXES, pairs)  11.1 us
    pallas_call x2, Pallas kernels, finish(): pl.pallas_call(functools.partial(finish_kernel, parts, len(extras)), out_...  5.43 us
  transfers between devices with their start and end apart: 25, of which 12 were waited for; matrix products, arithmetic and copies ran while one was open for 5% of the time, Pallas kernels for 6%

profile of v2, /device:TPU:104, one launch (start us, length us, event | category | flops | bytes accessed | tf_op | source)
XLA Modules:
  0.0 258.2 jit_solution(16191980661279593179)
XLA Ops:
  0.7 2.8 %slice.27 = f32[2,256,768]{2,1,0:T(8,128)} slice(f32[2,256,2048]{2,1,0:T(8,128)} %refs_0_.9), slice={[0:2], [0:256], [0:768]} | slice | bytes 3145728 | tf_op jit(solution)/shard_map/slice | solution.py:359
  3.5 4.5 %collective-permute-start.2 = (f32[2,256,768]{2,1,0:T(8,128)}, f32[2,256,768]{2,1,0:T(8,128)S(1)}, u32[]{:S(2)}, u32[]{:S(2)}) collective-permute-start(f32[2,256,768]{2,1,0:T(8,128)} %slice.27), channel_id=1, source_target_pairs={{4,0},{8,4},{12,8},{16,12},{20,16},{24,20},{28,24},{32,28},{36,32}... | collective-permute-start | bytes 4718600 | tf_op jit(solution)/shard_map/halo_0/ppermute | solution.py:293
  8.0 3.1 %fusion.1 = (f32[2,256,384]{2,1,0:T(8,128)}, f32[2,256,384]{2,1,0:T(8,128)}, f32[2,256,384]{2,1,0:T(8,128)}) fusion(f32[2,256,2048]{2,1,0:T(8,128)} %refs_0_.9), kind=kLoop, calls=%fused_computation.20 | loop fusion | bytes 4718592 | tf_op jit(solution)/shard_map/slice | solution.py:362
  11.0 2.7 %collective-permute-start.4 = (f32[2,256,384]{2,1,0:T(8,128)}, f32[2,256,384]{2,1,0:T(8,128)}, u32[]{:S(2)}, u32[]{:S(2)}) collective-permute-start(f32[2,256,384]{2,1,0:T(8,128)} %get-tuple-element.59), channel_id=1, source_target_pairs={{4,0},{8,4},{12,8},{16,12},{20,16},{24,20},{28,24},{32,28},{36,32}... | collective-permute-start | bytes 2359304 | tf_op jit(solution)/shard_map/halo_1/ppermute | solution.py:293
  13.8 2.4 collective-permute-start.5
  16.2 2.4 collective-permute-start
  19.4 4.2 %collective-permute-start.1 = (f32[2,256,128]{2,1,0:T(8,128)}, f32[2,256,128]{2,1,0:T(8,128)S(1)}, u32[]{:S(2)}, u32[]{:S(2)}) collective-permute-start(f32[2,256,128]{2,1,0:T(8,128)} %slice.29), channel_id=1, source_target_pairs={{4,0},{8,4},{12,8},{16,12},{20,16},{24,20},{28,24},{32,28},{36,32}... | collective-permute-start | bytes 786440 | tf_op jit(solution)/shard_map/halo_4/ppermute | solution.py:293
  23.7 1.6 reshape.22
  25.3 1.3 copy.13
  27.4 15.7 %collective-permute-done.2.refs_1_ = f32[2,256,768]{2,1,0:T(8,128)S(1)} collective-permute-done((f32[2,256,768]{2,1,0:T(8,128)}, f32[2,256,768]{2,1,0:T(8,128)S(1)}, u32[]{:S(2)}, u32[]{:S(2)}) %collective-permute-start.2) | collective-permute-done | bytes 1572896 | tf_op jit(solution)/shard_map/halo_0/ppermute | solution.py:293
  43.1 1.1 copy-done.16
  44.4 2.2 copy-done.1
  46.6 1.4 copy-done.17
  48.0 2.2 copy-done.18
  54.3 3.8 %group_0.1 = (f32[2,4,256,128]{3,2,1,0:T(8,128)S(1)}, f32[2,4,256,128]{3,2,1,0:T(8,128)S(1)}, f32[2,2,512,128]{3,2,1,0:T(8,128)S(1)}, f32[2,2,256,256]{3,2,1,0:T(8,128)S(1)}) custom-call(s32[1]{0:T(128)S(6)} %copy.15.live, s32[16,2]{1,0:T(8,128)S(1)} %broadcast_subtract_fusion.off, f32[2,256,2048]{2,1,0:T(8,128)S(1)} %copy-done.1, ...), custom_call_target="tpu_custom_call" | custom-call | flops 17179869184 | bytes 4096 | tf_op jit(solution)/shard_map/group_0/pallas_call | solution.py:216
  58.1 1.9 collective-permute-start.6
  60.1 1.2 group_4.1
  61.4 19.0 %collective-permute-start.8 = (f32[2,3,256,128]{3,2,1,0:T(8,128)S(1)}, f32[2,3,256,128]{3,2,1,0:T(8,128)S(1)}, u32[]{:S(2)}, u32[]{:S(2)}) collective-permute-start(f32[2,3,256,128]{3,2,1,0:T(8,128)S(1)} %get-tuple-element.38), channel_id=1, source_target_pairs={{0,4},{4,8},{8,12},{12,16},{16,20},{20,24},{24,28},{28,32},{32,36}... | collective-permute-start | bytes 2359304 | tf_op jit(solution)/shard_map/grad_1/ppermute | solution.py:293
  80.5 1.9 collective-permute-start.3
  82.4 12.6 %collective-permute-done.6.refs_3_.refs_4_ = f32[2,4,256,128]{3,2,1,0:T(8,128)S(1)} collective-permute-done((f32[2,4,256,128]{3,2,1,0:T(8,128)S(1)}, f32[2,4,256,128]{3,2,1,0:T(8,128)S(1)}, u32[]{:S(2)}, u32[]{:S(2)}) %collective-permute-start.6) | collective-permute-done | bytes 1048608 | tf_op jit(solution)/shard_map/grad_0/ppermute | solution.py:293
  95.1 1.2 group_7.1
  96.4 2.2 collective-permute-start.7
  98.5 13.4 %collective-permute-done.8.refs_3_.refs_5_ = f32[2,3,256,128]{3,2,1,0:T(8,128)S(1)} collective-permute-done((f32[2,3,256,128]{3,2,1,0:T(8,128)S(1)}, f32[2,3,256,128]{3,2,1,0:T(8,128)S(1)}, u32[]{:S(2)}, u32[]{:S(2)}) %collective-permute-start.8) | collective-permute-done | bytes 786464 | tf_op jit(solution)/shard_map/grad_1/ppermute | solution.py:293
  111.9 4.5 %group_10.1 = (f32[2,3,256,128]{3,2,1,0:T(8,128)S(1)}, f32[2,3,256,128]{3,2,1,0:T(8,128)S(1)}, f32[2,2,512,128]{3,2,1,0:T(8,128)S(1)}, f32[2,2,256,256]{3,2,1,0:T(8,128)S(1)}) custom-call(s32[1]{0:T(128)S(6)} %copy.15.live, s32[16,2]{1,0:T(8,128)S(1)} %broadcast_subtract_fusion.off, f32[2,256,2048]{2,1,0:T(8,128)S(1)} %copy-done.1, ...), custom_call_target="tpu_custom_call" | custom-call | flops 17179869184 | bytes 4096 | tf_op jit(solution)/shard_map/group_10/pallas_call | solution.py:216
  117.3 21.9 %collective-permute-done.3.refs_3_ = f32[2,512,256]{2,1,0:T(8,128)S(1)} collective-permute-done((f32[2,512,256]{2,1,0:T(8,128)S(1)}, f32[2,512,256]{2,1,0:T(8,128)S(1)}, u32[]{:S(2)}, u32[]{:S(2)}) %collective-permute-start.3) | collective-permute-done | bytes 1048608 | tf_op jit(solution)/shard_map/corner/ppermute | solution.py:293
  139.2 1.4 group_13.1
  144.3 1.9 collective-permute-start.13
  146.2 2.4 fusion.2
  148.6 2.0 collective-permute-start.14
  150.7 1.3 bitcast_add_fusion
  153.5 1.7 collective-permute-start.10
  155.2 1.8 collective-permute-start.12
  157.0 18.0 %collective-permute-done.10 = f32[128,256]{1,0:T(8,128)S(1)} collective-permute-done((f32[128,256]{1,0:T(8,128)}, f32[128,256]{1,0:T(8,128)S(1)}, u32[]{:S(2)}, u32[]{:S(2)}) %collective-permute-start.10) | collective-permute-done | bytes 131104 | tf_op jit(solution)/shard_map/swap_y1/ppermute | solution.py:322
  175.0 10.2 %collective-permute-done.11 = f32[128,256]{1,0:T(8,128)} collective-permute-done((f32[128,256]{1,0:T(8,128)}, f32[128,256]{1,0:T(8,128)}, u32[]{:S(2)}, u32[]{:S(2)}) %collective-permute-start.11) | collective-permute-done | bytes 131104 | tf_op jit(solution)/shard_map/swap_y2/ppermute | solution.py:322
  186.4 5.5 %collective-permute-done.15 = f32[128,256]{1,0:T(8,128)S(1)} collective-permute-done((f32[128,256]{1,0:T(8,128)S(1)}, f32[128,256]{1,0:T(8,128)S(1)}, u32[]{:S(2)}, u32[]{:S(2)}) %collective-permute-start.15) | collective-permute-done | bytes 131104 | tf_op jit(solution)/shard_map/swap_x1/ppermute | solution.py:322
  192.0 6.5 %collective-permute-done.16 = f32[128,256]{1,0:T(8,128)S(1)} collective-permute-done((f32[128,256]{1,0:T(8,128)S(1)}, f32[128,256]{1,0:T(8,128)S(1)}, u32[]{:S(2)}, u32[]{:S(2)}) %collective-permute-start.16) | collective-permute-done | bytes 131104 | tf_op jit(solution)/shard_map/swap_x2/ppermute | solution.py:322
  198.5 5.9 %collective-permute-done.19 = f32[128,256]{1,0:T(8,128)S(1)} collective-permute-done((f32[128,256]{1,0:T(8,128)S(1)}, f32[128,256]{1,0:T(8,128)S(1)}, u32[]{:S(2)}, u32[]{:S(2)}) %collective-permute-start.19) | collective-permute-done | bytes 131104 | tf_op jit(solution)/shard_map/swap_z1/ppermute | solution.py:322
  204.6 6.5 %collective-permute-done.20 = f32[128,256]{1,0:T(8,128)S(1)} collective-permute-done((f32[128,256]{1,0:T(8,128)S(1)}, f32[128,256]{1,0:T(8,128)S(1)}, u32[]{:S(2)}, u32[]{:S(2)}) %collective-permute-start.20) | collective-permute-done | bytes 131104 | tf_op jit(solution)/shard_map/swap_z2/ppermute | solution.py:322
  211.1 4.2 %collective-permute-start.21 = (f32[128,256]{1,0:T(8,128)S(1)}, f32[128,256]{1,0:T(8,128)S(1)}, u32[]{:S(2)}, u32[]{:S(2)}) collective-permute-start(f32[128,256]{1,0:T(8,128)S(1)} %add_multiply_fusion), channel_id=1, source_target_pairs={{0,2},{1,3},{2,0},{3,1},{4,6},{5,7},{6,4},{7,5},{8,10},{9,11},{10,... | collective-permute-start | bytes 393224 | tf_op jit(solution)/shard_map/swap_y1/ppermute | solution.py:322
  215.2 2.6 %collective-permute-start.22 = (f32[128,256]{1,0:T(8,128)S(1)}, f32[128,256]{1,0:T(8,128)S(1)}, u32[]{:S(2)}, u32[]{:S(2)}) collective-permute-start(f32[128,256]{1,0:T(8,128)S(1)} %add_multiply_fusion), channel_id=1, source_target_pairs={{0,64},{1,65},{2,66},{3,67},{4,68},{5,69},{6,70},{7,71},{8,72},{9,... | collective-permute-start | bytes 393224 | tf_op jit(solution)/shard_map/swap_y2/ppermute | solution.py:322
  218.3 1.9 collective-permute-start.18
  220.3 2.5 collective-permute-start.17
  225.1 20.9 %collective-permute-done.18.refs_9_ = f32[2,2,256,128]{3,2,1,0:T(8,128)} collective-permute-done((f32[2,2,256,128]{3,2,1,0:T(8,128)}, f32[2,2,256,128]{3,2,1,0:T(8,128)}, u32[]{:S(2)}, u32[]{:S(2)}) %collective-permute-start.18) | collective-permute-done | bytes 524320 | tf_op jit(solution)/shard_map/over/ppermute | solution.py:293
  246.0 1.1 copy-done.7
  248.3 1.1 copy-done.11
  249.4 1.1 copy-done.13
  250.5 3.3 %finish_0.1.refs_2_ = f32[2,256,2048]{2,1,0:T(8,128)} custom-call(f32[2,4,256,128]{3,2,1,0:T(8,128)S(1)} %get-tuple-element.50.refs_0_, f32[2,3,256,128]{3,2,1,0:T(8,128)S(1)} %copy-done.5, f32[2,3,256,128]{3,2,1,0:T(8,128)S(1)} %copy-done.9, f32[2,3,256,128]{3,2,1,0:T(8,128)S(1)} %copy-done.13, ...), custom_call_target="tpu_custom_call" | custom-call | tf_op jit(solution)/shard_map/finish_0/pallas_call | solution.py:274
  253.9 2.2 finish_13.1
  (116 shorter events, 19.0 us)
Async XLA Ops:
  0.6 18.0 %copy-start = (f32[2,256,2048]{2,1,0:T(8,128)S(1)}, f32[2,256,2048]{2,1,0:T(8,128)}, u32[]{:S(2)}) copy-start(f32[2,256,2048]{2,1,0:T(8,128)} %refs_0_.9) | copy-start | bytes 12582916
  0.6 23.0 %copy-start.38 = (s32[16,2]{0,1:T(2,128)S(1)}, s32[16,2]{0,1:T(2,128)}, u32[]{:S(2)}) copy-start(s32[16,2]{0,1:T(2,128)} %param.12) | copy-start | bytes 388
  0.7 23.1 %copy-start.37 = (f32[2,2,256,256]{3,2,1,0:T(8,128)S(1)}, f32[2,2,256,256]{3,2,1,0:T(8,128)}, u32[]{:S(2)}) copy-start(f32[2,2,256,256]{3,2,1,0:T(8,128)} %param.10) | copy-start | bytes 3145732
  3.5 39.6 %collective-permute-start.2 = (f32[2,256,768]{2,1,0:T(8,128)}, f32[2,256,768]{2,1,0:T(8,128)S(1)}, u32[]{:S(2)}, u32[]{:S(2)}) collective-permute-start(f32[2,256,768]{2,1,0:T(8,128)} %slice.27), channel_id=1, source_target_pairs={{4,0},{8,4},{12,8},{16,12},{20,16},{24,20},{28,24},{32,28},{36,32}... | collective-permute-start | bytes 4718600 | tf_op jit(solution)/shard_map/halo_0/ppermute | solution.py:293
  11.0 49.0 %collective-permute-start.4 = (f32[2,256,384]{2,1,0:T(8,128)}, f32[2,256,384]{2,1,0:T(8,128)}, u32[]{:S(2)}, u32[]{:S(2)}) collective-permute-start(f32[2,256,384]{2,1,0:T(8,128)} %get-tuple-element.59), channel_id=1, source_target_pairs={{4,0},{8,4},{12,8},{16,12},{20,16},{24,20},{28,24},{32,28},{36,32}... | collective-permute-start | bytes 2359304 | tf_op jit(solution)/shard_map/halo_1/ppermute | solution.py:293
  13.8 66.7 %collective-permute-start.5 = (f32[2,256,384]{2,1,0:T(8,128)}, f32[2,256,384]{2,1,0:T(8,128)}, u32[]{:S(2)}, u32[]{:S(2)}) collective-permute-start(f32[2,256,384]{2,1,0:T(8,128)} %get-tuple-element.58), channel_id=1, source_target_pairs={{4,0},{8,4},{12,8},{16,12},{20,16},{24,20},{28,24},{32,28},{36,32}... | collective-permute-start | bytes 2359304 | tf_op jit(solution)/shard_map/halo_2/ppermute | solution.py:293
  16.2 82.3 %collective-permute-start = (f32[2,256,384]{2,1,0:T(8,128)}, f32[2,256,384]{2,1,0:T(8,128)}, u32[]{:S(2)}, u32[]{:S(2)}) collective-permute-start(f32[2,256,384]{2,1,0:T(8,128)} %get-tuple-element.60), channel_id=1, source_target_pairs={{4,0},{8,4},{12,8},{16,12},{20,16},{24,20},{28,24},{32,28},{36,32}... | collective-permute-start | bytes 2359304 | tf_op jit(solution)/shard_map/halo_3/ppermute | solution.py:293
  19.4 97.9 %collective-permute-start.1 = (f32[2,256,128]{2,1,0:T(8,128)}, f32[2,256,128]{2,1,0:T(8,128)S(1)}, u32[]{:S(2)}, u32[]{:S(2)}) collective-permute-start(f32[2,256,128]{2,1,0:T(8,128)} %slice.29), channel_id=1, source_target_pairs={{4,0},{8,4},{12,8},{16,12},{20,16},{24,20},{28,24},{32,28},{36,32}... | collective-permute-start | bytes 786440 | tf_op jit(solution)/shard_map/halo_4/ppermute | solution.py:293
  44.4 2.2 copy-start.1
  48.0 2.2 copy-start.18
  54.3 5.7 %copy-start.29 = (bf16[512,512]{1,0:T(8,128)(2,1)S(1)}, bf16[512,512]{1,0:T(8,128)(2,1)}, u32[]{:S(2)}) copy-start(bf16[512,512]{1,0:T(8,128)(2,1)} %constant.93.clone.refs_7_.refs_8_.refs_9_.refs_10_) | copy-start | bytes 1572868
  58.1 37.0 %collective-permute-start.6 = (f32[2,4,256,128]{3,2,1,0:T(8,128)S(1)}, f32[2,4,256,128]{3,2,1,0:T(8,128)S(1)}, u32[]{:S(2)}, u32[]{:S(2)}) collective-permute-start(f32[2,4,256,128]{3,2,1,0:T(8,128)S(1)} %get-tuple-element.32), channel_id=1, source_target_pairs={{0,4},{4,8},{8,12},{12,16},{16,20},{20,24},{24,28},{28,32},{32,36}... | collective-permute-start | bytes 3145736 | tf_op jit(solution)/shard_map/grad_0/ppermute | solution.py:293
  60.0 20.3 %slice-start = ((f32[2,256,2048]{2,1,0:T(8,128)}), f32[2,256,256]{2,1,0:T(8,128)S(1)}, s32[]{:S(2)}) async-start(f32[2,256,2048]{2,1,0:T(8,128)} %refs_0_.9), calls=%async_computation | async-start | bytes 1048576 | tf_op jit(solution)/shard_map/slice | solution.py:365
  60.1 20.3 %slice-start.1 = ((f32[2,256,768]{2,1,0:T(8,128)}), f32[2,256,256]{2,1,0:T(8,128)S(1)}, s32[]{:S(2)}) async-start(f32[2,256,768]{2,1,0:T(8,128)} %copy-done.16), calls=%async_computation.1 | async-start | bytes 1048576 | tf_op jit(solution)/shard_map/slice | solution.py:365
  60.1 35.0 %copy-start.19 = (f32[16,256,256]{2,1,0:T(8,128)S(1)}, f32[16,256,256]{2,1,0:T(8,128)}, u32[]{:S(2)}) copy-start(f32[16,256,256]{2,1,0:T(8,128)} %refs_5_.3) | copy-start | bytes 12582916
  60.1 35.0 %copy-start.23 = (bf16[512,512]{1,0:T(8,128)(2,1)S(1)}, bf16[512,512]{1,0:T(8,128)(2,1)}, u32[]{:S(2)}) copy-start(bf16[512,512]{1,0:T(8,128)(2,1)} %constant.90.clone.refs_4_.refs_5_.refs_6_.refs_7_) | copy-start | bytes 1572868
  60.1 35.0 %copy-start.25 = (bf16[512,512]{1,0:T(8,128)(2,1)S(1)}, bf16[512,512]{1,0:T(8,128)(2,1)}, u32[]{:S(2)}) copy-start(bf16[512,512]{1,0:T(8,128)(2,1)} %constant.91.clone.refs_5_.refs_6_.refs_7_.refs_8_) | copy-start | bytes 1572868
  60.1 35.0 %copy-start.27 = (bf16[512,512]{1,0:T(8,128)(2,1)S(1)}, bf16[512,512]{1,0:T(8,128)(2,1)}, u32[]{:S(2)}) copy-start(bf16[512,512]{1,0:T(8,128)(2,1)} %constant.92.clone.refs_6_.refs_7_.refs_8_.refs_9_) | copy-start | bytes 1572868
  61.4 33.7 %copy-start.4 = (f32[2,3,256,128]{3,2,1,0:T(8,128)}, f32[2,3,256,128]{3,2,1,0:T(8,128)S(1)}, u32[]{:S(2)}) copy-start(f32[2,3,256,128]{3,2,1,0:T(8,128)S(1)} %get-tuple-element.51.refs_1_) | copy-start | bytes 2359300
  61.4 50.5 %collective-permute-start.8 = (f32[2,3,256,128]{3,2,1,0:T(8,128)S(1)}, f32[2,3,256,128]{3,2,1,0:T(8,128)S(1)}, u32[]{:S(2)}, u32[]{:S(2)}) collective-permute-start(f32[2,3,256,128]{3,2,1,0:T(8,128)S(1)} %get-tuple-element.38), channel_id=1, source_target_pairs={{0,4},{4,8},{8,12},{12,16},{16,20},{20,24},{24,28},{28,32},{32,36}... | collective-permute-start | bytes 2359304 | tf_op jit(solution)/shard_map/grad_1/ppermute | solution.py:293
  80.5 58.7 %collective-permute-start.3 = (f32[2,512,256]{2,1,0:T(8,128)S(1)}, f32[2,512,256]{2,1,0:T(8,128)S(1)}, u32[]{:S(2)}, u32[]{:S(2)}) collective-permute-start(f32[2,512,256]{2,1,0:T(8,128)S(1)} %pad_maximum_fusion), channel_id=1, source_target_pairs={{1,0},{2,1},{3,2},{5,4},{6,5},{7,6},{9,8},{10,9},{11,10},{13,12},{... | collective-permute-start | bytes 3145736 | tf_op jit(solution)/shard_map/corner/ppermute | solution.py:293
  96.4 20.1 %copy-start.8 = (f32[2,3,256,128]{3,2,1,0:T(8,128)}, f32[2,3,256,128]{3,2,1,0:T(8,128)S(1)}, u32[]{:S(2)}) copy-start(f32[2,3,256,128]{3,2,1,0:T(8,128)S(1)} %get-tuple-element.52.refs_2_) | copy-start | bytes 2359300
  96.4 42.9 %collective-permute-start.7 = (f32[2,3,256,128]{3,2,1,0:T(8,128)S(1)}, f32[2,3,256,128]{3,2,1,0:T(8,128)S(1)}, u32[]{:S(2)}, u32[]{:S(2)}) collective-permute-start(f32[2,3,256,128]{3,2,1,0:T(8,128)S(1)} %get-tuple-element.37), channel_id=1, source_target_pairs={{0,4},{4,8},{8,12},{12,16},{16,20},{20,24},{24,28},{28,32},{32,36}... | collective-permute-start | bytes 2359304 | tf_op jit(solution)/shard_map/grad_2/ppermute | solution.py:293
  111.9 4.5 %copy-start.6 = (f32[2,3,256,128]{3,2,1,0:T(8,128)}, f32[2,3,256,128]{3,2,1,0:T(8,128)S(1)}, u32[]{:S(2)}) copy-start(f32[2,3,256,128]{3,2,1,0:T(8,128)S(1)} %collective-permute-done.8.refs_3_.refs_5_) | copy-start | bytes 2359300
  117.3 23.3 %copy-start.21 = (f32[2,3,256,128]{3,2,1,0:T(8,128)}, f32[2,3,256,128]{3,2,1,0:T(8,128)S(1)}, u32[]{:S(2)}) copy-start(f32[2,3,256,128]{3,2,1,0:T(8,128)S(1)} %get-tuple-element.45) | copy-start | bytes 2359300
  142.5 1.8 copy-start.14
  144.3 6.3 %collective-permute-start.9 = (f32[512,256]{1,0:T(8,128)}, f32[512,256]{1,0:T(8,128)}, u32[]{:S(2)}, u32[]{:S(2)}) collective-permute-start(f32[512,256]{1,0:T(8,128)} %dynamic-slice_bitcast_fusion), channel_id=1, source_target_pairs={{0,1},{1,0},{2,3},{3,2},{4,5},{5,4},{6,7},{7,6},{8,9},{9,8},{10,11... | collective-permute-start | bytes 1572872 | tf_op jit(solution)/shard_map/swap_c1/ppermute | solution.py:322
  144.3 42.0 %collective-permute-start.13 = (f32[2,3,256,128]{3,2,1,0:T(8,128)}, f32[2,3,256,128]{3,2,1,0:T(8,128)}, u32[]{:S(2)}, u32[]{:S(2)}) collective-permute-start(f32[2,3,256,128]{3,2,1,0:T(8,128)} %copy-done.21), channel_id=1, source_target_pairs={{0,4},{4,8},{8,12},{12,16},{16,20},{20,24},{24,28},{28,32},{32,36}... | collective-permute-start | bytes 2359304 | tf_op jit(solution)/shard_map/grad_3/ppermute | solution.py:293
  148.6 97.4 %copy-start.5 = (f32[2,3,256,128]{3,2,1,0:T(8,128)S(1)}, f32[2,3,256,128]{3,2,1,0:T(8,128)}, u32[]{:S(2)}) copy-start(f32[2,3,256,128]{3,2,1,0:T(8,128)} %copy-done.4) | copy-start | bytes 2359300
  148.6 37.7 %collective-permute-start.14 = (f32[2,2,256,128]{3,2,1,0:T(8,128)}, f32[2,2,256,128]{3,2,1,0:T(8,128)S(1)}, u32[]{:S(2)}, u32[]{:S(2)}) collective-permute-start(f32[2,2,256,128]{3,2,1,0:T(8,128)} %get-tuple-element.64), channel_id=1, source_target_pairs={{0,5},{1,6},{2,7},{4,9},{5,10},{6,11},{8,13},{9,14},{10,15},{12,17... | collective-permute-start | bytes 1572872 | tf_op jit(solution)/shard_map/slant/ppermute | solution.py:302
  153.5 21.5 %collective-permute-start.10 = (f32[128,256]{1,0:T(8,128)}, f32[128,256]{1,0:T(8,128)S(1)}, u32[]{:S(2)}, u32[]{:S(2)}) collective-permute-start(f32[128,256]{1,0:T(8,128)} %get-tuple-element.71), channel_id=1, source_target_pairs={{0,2},{1,3},{2,0},{3,1},{4,6},{5,7},{6,4},{7,5},{8,10},{9,11},{10,... | collective-permute-start | bytes 393224 | tf_op jit(solution)/shard_map/swap_y1/ppermute | solution.py:322
  155.2 30.0 %collective-permute-start.11 = (f32[128,256]{1,0:T(8,128)}, f32[128,256]{1,0:T(8,128)}, u32[]{:S(2)}, u32[]{:S(2)}) collective-permute-start(f32[128,256]{1,0:T(8,128)} %get-tuple-element.70), channel_id=1, source_target_pairs={{0,64},{1,65},{2,66},{3,67},{4,68},{5,69},{6,70},{7,71},{8,72},{9,... | collective-permute-start | bytes 393224 | tf_op jit(solution)/shard_map/swap_y2/ppermute | solution.py:322
  155.2 30.0 %collective-permute-start.12 = (f32[128,256]{1,0:T(8,128)}, f32[128,256]{1,0:T(8,128)}, u32[]{:S(2)}, u32[]{:S(2)}) collective-permute-start(f32[128,256]{1,0:T(8,128)} %get-tuple-element.69), channel_id=1, source_target_pairs={{0,66},{1,67},{2,64},{3,65},{4,70},{5,71},{6,68},{7,69},{8,74},{9,... | collective-permute-start | bytes 393224 | tf_op jit(solution)/shard_map/swap_y3/ppermute | solution.py:322
  186.3 5.6 %collective-permute-start.15 = (f32[128,256]{1,0:T(8,128)S(1)}, f32[128,256]{1,0:T(8,128)S(1)}, u32[]{:S(2)}, u32[]{:S(2)}) collective-permute-start(f32[128,256]{1,0:T(8,128)S(1)} %fusion), channel_id=1, source_target_pairs={{0,4},{1,5},{2,6},{3,7},{4,0},{5,1},{6,2},{7,3},{8,12},{9,13},{10,... | collective-permute-start | bytes 393224 | tf_op jit(solution)/shard_map/swap_x1/ppermute | solution.py:322
  191.9 6.6 %collective-permute-start.16 = (f32[128,256]{1,0:T(8,128)S(1)}, f32[128,256]{1,0:T(8,128)S(1)}, u32[]{:S(2)}, u32[]{:S(2)}) collective-permute-start(f32[128,256]{1,0:T(8,128)S(1)} %add.70), channel_id=1, source_target_pairs={{0,8},{1,9},{2,10},{3,11},{4,12},{5,13},{6,14},{7,15},{8,0},{9,1},... | collective-permute-start | bytes 393224 | tf_op jit(solution)/shard_map/swap_x2/ppermute | solution.py:322
  198.5 6.0 %collective-permute-start.19 = (f32[128,256]{1,0:T(8,128)S(1)}, f32[128,256]{1,0:T(8,128)S(1)}, u32[]{:S(2)}, u32[]{:S(2)}) collective-permute-start(f32[128,256]{1,0:T(8,128)S(1)} %add.71), channel_id=1, source_target_pairs={{0,16},{1,17},{2,18},{3,19},{4,20},{5,21},{6,22},{7,23},{8,24},{9,... | collective-permute-start | bytes 393224 | tf_op jit(solution)/shard_map/swap_z1/ppermute | solution.py:322
  204.5 6.6 %collective-permute-start.20 = (f32[128,256]{1,0:T(8,128)S(1)}, f32[128,256]{1,0:T(8,128)S(1)}, u32[]{:S(2)}, u32[]{:S(2)}) collective-permute-start(f32[128,256]{1,0:T(8,128)S(1)} %add.72), channel_id=1, source_target_pairs={{0,32},{1,33},{2,34},{3,35},{4,36},{5,37},{6,38},{7,39},{8,40},{9,... | collective-permute-start | bytes 393224 | tf_op jit(solution)/shard_map/swap_z2/ppermute | solution.py:322
  211.1 11.7 %collective-permute-start.21 = (f32[128,256]{1,0:T(8,128)S(1)}, f32[128,256]{1,0:T(8,128)S(1)}, u32[]{:S(2)}, u32[]{:S(2)}) collective-permute-start(f32[128,256]{1,0:T(8,128)S(1)} %add_multiply_fusion), channel_id=1, source_target_pairs={{0,2},{1,3},{2,0},{3,1},{4,6},{5,7},{6,4},{7,5},{8,10},{9,11},{10,... | collective-permute-start | bytes 393224 | tf_op jit(solution)/shard_map/swap_y1/ppermute | solution.py:322
  215.2 7.5 %collective-permute-start.22 = (f32[128,256]{1,0:T(8,128)S(1)}, f32[128,256]{1,0:T(8,128)S(1)}, u32[]{:S(2)}, u32[]{:S(2)}) collective-permute-start(f32[128,256]{1,0:T(8,128)S(1)} %add_multiply_fusion), channel_id=1, source_target_pairs={{0,64},{1,65},{2,66},{3,67},{4,68},{5,69},{6,70},{7,71},{8,72},{9,... | collective-permute-start | bytes 393224 | tf_op jit(solution)/shard_map/swap_y2/ppermute | solution.py:322
  217.9 5.7 %collective-permute-start.23 = (f32[128,256]{1,0:T(8,128)S(1)}, f32[128,256]{1,0:T(8,128)S(1)}, u32[]{:S(2)}, u32[]{:S(2)}) collective-permute-start(f32[128,256]{1,0:T(8,128)S(1)} %add_multiply_fusion), channel_id=1, source_target_pairs={{0,66},{1,67},{2,64},{3,65},{4,70},{5,71},{6,68},{7,69},{8,74},{9,... | collective-permute-start | bytes 393224 | tf_op jit(solution)/shard_map/swap_y3/ppermute | solution.py:322
  218.3 27.7 %collective-permute-start.18 = (f32[2,2,256,128]{3,2,1,0:T(8,128)}, f32[2,2,256,128]{3,2,1,0:T(8,128)}, u32[]{:S(2)}, u32[]{:S(2)}) collective-permute-start(f32[2,2,256,128]{3,2,1,0:T(8,128)} %get-tuple-element.56), channel_id=1, source_target_pairs={{0,1},{1,2},{2,3},{4,5},{5,6},{6,7},{8,9},{9,10},{10,11},{12,13},{... | collective-permute-start | bytes 1572872 | tf_op jit(solution)/shard_map/over/ppermute | solution.py:293
  220.3 33.6 %collective-permute-start.17 = (f32[2,3,256,128]{3,2,1,0:T(8,128)}, f32[2,3,256,128]{3,2,1,0:T(8,128)}, u32[]{:S(2)}, u32[]{:S(2)}) collective-permute-start(f32[2,3,256,128]{3,2,1,0:T(8,128)} %copy-done.20), channel_id=1, source_target_pairs={{0,4},{4,8},{8,12},{12,16},{16,20},{20,24},{24,28},{28,32},{32,36}... | collective-permute-start | bytes 2359304 | tf_op jit(solution)/shard_map/grad_last/ppermute | solution.py:293
  223.6 1.5 copy-start.33
  225.1 30.9 %collective-permute-start.24 = (f32[512,256]{1,0:T(8,128)}, f32[512,256]{1,0:T(8,128)}, u32[]{:S(2)}, u32[]{:S(2)}) collective-permute-start(f32[512,256]{1,0:T(8,128)} %pad_maximum_fusion.3), channel_id=1, source_target_pairs={{0,1},{1,0},{2,3},{3,2},{4,5},{5,4},{6,7},{7,6},{8,9},{9,8},{10,11... | collective-permute-start | bytes 1572872 | tf_op jit(solution)/shard_map/swap_c1/ppermute | solution.py:322
  250.5 3.3 %copy-start.15 = (f32[2,3,256,128]{3,2,1,0:T(8,128)S(1)}, f32[2,3,256,128]{3,2,1,0:T(8,128)}, u32[]{:S(2)}) copy-start(f32[2,3,256,128]{3,2,1,0:T(8,128)} %copy-done.14) | copy-start | bytes 2359300
  253.8 2.2 copy-start.32
  253.9 2.2 copy-start.34
  253.9 2.2 copy-start.36
  (18 other events, 19.3 us)

commit v3 on v2

v3 whole, which is shorter than its diff:
```python
import functools
import math

import jax
import jax.numpy as jnp
import ml_dtypes
import numpy as np
from jax import lax
from jax.experimental import pallas as pl
from jax.experimental.pallas import tpu as pltpu
from jax.sharding import PartitionSpec as P

SLOTS = 16
SIZE = 256
LANE = 128
CHUNK = 256
FLOOR = 0.5
AXES = ("scan", "mode")
f32 = jnp.float32
bf16 = jnp.bfloat16


def tables():
    n = SIZE
    place = np.arange(n)
    angles = (place[:, None] * place[None, :] % n) * (2.0 * math.pi / n)
    c = np.cos(angles) / math.sqrt(n)
    s = np.sin(angles) / math.sqrt(n)
    rows = np.concatenate([place[0 : n // 2 : 2], place[1 : n // 2 : 2]])

    def block(c, s):
        return np.block([[c, s], [-s, c]])

    def halves(c, s):
        return np.stack([block(c[rows, p::2], s[rows, p::2]) for p in (0, 1)])

    both = (halves(c, s), block(c, -s), halves(c, -s), block(c, s))
    return [t.astype(ml_dtypes.bfloat16) for t in both]


def stack(parts, axis):
    return jnp.concatenate(parts, axis)


def left_product(table, even, odd):
    dot = functools.partial(jnp.dot, preferred_element_type=f32)
    a = dot(table[0], even)
    b = dot(table[1], odd)
    return (a + b).astype(bf16), (a - b).astype(bf16)


def pattern(ext, grad, acc, probe, frame, tabs, r, c):
    left_fwd, right_fwd, left_bwd, right_bwd = tabs
    n = SIZE
    half, quarter = n // 2, n // 4
    block = c // LANE
    shift = c % LANE
    dot = functools.partial(jnp.dot, preferred_element_type=f32)

    def window(part):
        cols = []
        for j in range(3):
            view = ext.at[part, block + j]
            cols.append(stack([view[pl.ds(r + p, half, stride=2), :] for p in (0, 1)], 0))
        return pltpu.roll(stack(cols, 1), 3 * LANE - shift, 1)[:, :n]

    wr = window(0)
    wi = window(1)
    x_re = [probe[k, 0] * wr - probe[k, 1] * wi for k in (0, 1)]
    x_im = [probe[k, 0] * wi + probe[k, 1] * wr for k in (0, 1)]

    def rows_of(p):
        rows = slice(half * p, half * (p + 1))
        return stack([stack([x_re[k][rows], x_im[k][rows]], 0) for k in (0, 1)], 1).astype(bf16)

    sums = left_product(left_fwd, rows_of(0), rows_of(1))
    h = stack(
        [
            stack([t[:half, n * k : n * (k + 1)], t[half:, n * k : n * (k + 1)]], 1)
            for k in (0, 1)
            for t in sums
        ],
        0,
    )
    far = dot(h, right_fwd[...])
    sq = far * far
    intensity = (sq[:n, :n] + sq[:n, n:]) + (sq[n:, :n] + sq[n:, n:])
    amplitude = stack(
        [
            stack([frame.at[b][pl.ds(row, quarter, stride=2), :] for b in (0, 1)], 1)
            for row in (0, 1, half, half + 1)
        ],
        0,
    )
    factor = amplitude * lax.rsqrt(jnp.maximum(intensity, FLOOR)) - 1.0
    change = [
        [(far[n * k : n * (k + 1), n * p : n * (p + 1)] * factor).astype(bf16) for p in (0, 1)]
        for k in (0, 1)
    ]

    def quarters(q):
        return stack(
            [
                stack([change[k][p][at : at + quarter] for p in (0, 1) for at in (q, q + half)], 0)
                for k in (0, 1)
            ],
            1,
        )

    plus, minus = left_product(left_bwd, quarters(0), quarters(quarter))
    h = stack(
        [
            stack(
                [
                    t[at : at + quarter, n * k : n * (k + 1)],
                    t[half + at : half + at + quarter, n * k : n * (k + 1)],
                ],
                1,
            )
            for k in (0, 1)
            for t, at in ((plus, 0), (minus, 0), (plus, quarter), (minus, quarter))
        ],
        0,
    )
    delta = dot(h, right_bwd[...])
    terms = [None, None]
    for k in (0, 1):
        d_re = delta[n * k : n * k + n, :n]
        d_im = delta[n * k : n * k + n, n:]
        new = (
            probe[k, 0] * d_re + probe[k, 1] * d_im,
            probe[k, 0] * d_im - probe[k, 1] * d_re,
        )
        terms = [b if a is None else a + b for a, b in zip(terms, new)]
        acc[k, 0] += wr * d_re + wi * d_im
        acc[k, 1] += wr * d_im - wi * d_re
    blank = jnp.zeros((n, LANE), f32)
    for part, term in enumerate(terms):
        moved = pltpu.roll(stack([term, blank], 1), shift, 1)
        for j in range(3):
            view = grad.at[part, block + j]
            for p in (0, 1):
                rows = pl.ds(r + p, half, stride=2)
                view[rows, :] = view[rows, :] + moved[half * p : half * (p + 1), LANE * j : LANE * (j + 1)]


def group_kernel(first, count, homes, n_after, last, live, off, *refs):
    wide = count + 2
    refs = list(refs)
    sources = refs[: len(homes[2])]
    refs = refs[len(homes[2]) + n_after :]
    measured, probe, t0, t1, t2, t3, carry, acc_in = refs[:8]
    if last:
        upper, lower, over_upper, over_lower, acc = refs[8:13]
    else:
        upper, lower, carry_out, acc = refs[8:12]
    ext, grad, frame, picked, load_sem, frame_sem = refs[-6:]

    def pick(q, n):
        b = off[q, 1] // LANE - first
        picked[n] = q
        return n + jnp.where((b >= 0) & (b < count), 1, 0)

    n = lax.fori_loop(0, live[0], pick, jnp.int32(0))

    def loads():
        out = []
        for half in (0, 1):
            for b in range(wide):
                which, row, at = homes[half][b]
                src = sources[which].at[:, row : row + SIZE, at : at + LANE]
                dst = ext.at[:, b, SIZE * half : SIZE * (half + 1), :]
                out.append(pltpu.make_async_copy(src, dst, load_sem.at[2 * b + half]))
        return out

    def frame_copies(i):
        slot = i % 2
        return [
            pltpu.make_async_copy(
                measured.at[picked[i], :, LANE * b : LANE * (b + 1)],
                frame.at[slot, b],
                frame_sem.at[2 * slot + b],
            )
            for b in (0, 1)
        ]

    @pl.when(n > 0)
    def _():
        for copy in loads():
            copy.start()
        for copy in frame_copies(0):
            copy.start()

    grad[:, 0:2] = carry[...]
    grad[:, 2:] = jnp.zeros((2, count, 2 * SIZE, LANE), f32)
    acc[...] = acc_in[...]

    @pl.when(n > 0)
    def _():
        for copy in loads():
            copy.wait()

    def step(i, _):
        @pl.when(i + 1 < n)
        def _():
            for copy in frame_copies(i + 1):
                copy.start()

        for copy in frame_copies(i):
            copy.wait()
        q = picked[i]
        pattern(
            ext, grad, acc, probe, frame.at[i % 2], (t0, t1, t2, t3), off[q, 0], off[q, 1] - first * LANE
        )
        return 0

    lax.fori_loop(0, n, step, 0)
    upper[...] = grad[:, 0:count, :SIZE]
    lower[...] = grad[:, 0:count, SIZE:]
    if not last:
        carry_out[...] = grad[:, count:]
    else:
        over_upper[...] = grad[:, count:, :SIZE]
        over_lower[...] = grad[:, count:, SIZE:]
        for k in (0, 1):
            for part in (0, 1):
                for b in (0, 1):
                    view = ext.at[part, 2 * k + b]
                    at = slice(LANE * b, LANE * (b + 1))
                    for p in (0, 1):
                        rows = pl.ds(p, SIZE // 2, stride=2)
                        view[rows, :] = acc[k, part, LANE * p : LANE * (p + 1), at]
                    acc[k, part, :, at] = view[0:SIZE, :]


IN_HBM = pl.BlockSpec(memory_space=pltpu.HBM)
IN_SMEM = pl.BlockSpec(memory_space=pltpu.SMEM)
IN_VMEM = pl.BlockSpec(memory_space=pltpu.VMEM)


def run_group(first, count, bounds, live, off, field, halos, corner, measured, probe, tabs, carry, acc, after):
    wide = count + 2
    arrays, homes = [], [[], []]

    def index_in(array):
        for i, other in enumerate(arrays):
            if other is array:
                return i
        arrays.append(array)
        return len(arrays) - 1

    for b in range(first, first + wide):
        if b < bounds[-1]:
            chunk = next(i for i, end in enumerate(bounds) if b < end)
            begin = bounds[chunk - 1] if chunk else 0
            homes[0].append((index_in(field), 0, b * LANE))
            homes[1].append((index_in(halos[chunk]), 0, (b - begin) * LANE))
        else:
            at = (b - bounds[-1]) * LANE
            homes[0].append((index_in(corner), 0, at))
            homes[1].append((index_in(corner), SIZE, at))
    homes.append(arrays)
    args = [live, off, *arrays, *after, measured, probe, *tabs, carry, acc]
    specs = [IN_SMEM] * 2 + [IN_HBM] * (1 + len(arrays) + len(after)) + [IN_VMEM] * 7
    part = jax.ShapeDtypeStruct((2, count, SIZE, LANE), f32)
    last = first + count == bounds[-1]
    edge = jax.ShapeDtypeStruct((2, 2, SIZE, LANE), f32)
    whole = jax.ShapeDtypeStruct((2, 2, 2 * SIZE, LANE), f32)
    out_shape = (part, part) + ((edge, edge) if last else (whole,))
    out_shape += (jax.ShapeDtypeStruct((2, 2, SIZE, SIZE), f32),)
    return pl.pallas_call(
        functools.partial(group_kernel, first, count, (homes[0], homes[1], [None] * len(arrays)),
            len(after), last),
        out_shape=out_shape,
        in_specs=specs,
        out_specs=(IN_VMEM,) * len(out_shape),
        scratch_shapes=[
            pltpu.VMEM((2, wide, 2 * SIZE, LANE), f32),
            pltpu.VMEM((2, wide, 2 * SIZE, LANE), f32),
            pltpu.VMEM((2, 2, SIZE, LANE), f32),
            pltpu.SMEM((SLOTS + 1,), jnp.int32),
            pltpu.SemaphoreType.DMA((2 * wide,)),
            pltpu.SemaphoreType.DMA((4,)),
        ],
        compiler_params=pltpu.CompilerParams(vmem_limit_bytes=30 * 2**20),
        cost_estimate=pl.CostEstimate(flops=2**34, bytes_accessed=2**12, transcendentals=0),
        name=f"group_{first}",
    )(*args)


def finish_kernel(blocks, terms, *refs):
    out, buf, sem = refs[-3:]
    copies = []
    for at, (block, many) in enumerate(zip(blocks, terms)):
        value = None
        for which, b in many:
            term = refs[which][:, b]
            value = term if value is None else value + term
        buf[at] = value
        copy = pltpu.make_async_copy(
            buf.at[at], out.at[:, :, block * LANE : (block + 1) * LANE], sem.at[at]
        )
        copy.start()
        copies.append(copy)
    for copy in copies:
        copy.wait()


def finish(blocks, sources, shape, onto):
    args = [array for _, array in sources]
    terms = tuple(
        tuple(
            (i, block - first)
            for i, (first, array) in enumerate(sources)
            if first <= block < first + array.shape[1]
        )
        for block in blocks
    )
    specs = [IN_VMEM] * len(args)
    aliases = {}
    if onto is not None:
        aliases = {len(args): 0}
        args.append(onto)
        specs.append(IN_HBM)
    return pl.pallas_call(
        functools.partial(finish_kernel, tuple(blocks), terms),
        out_shape=jax.ShapeDtypeStruct(shape, f32),
        in_specs=specs,
        out_specs=IN_HBM,
        scratch_shapes=[
            pltpu.VMEM((len(blocks), 2, SIZE, LANE), f32),
            pltpu.SemaphoreType.DMA((len(blocks),)),
        ],
        input_output_aliases=aliases,
        compiler_params=pltpu.CompilerParams(vmem_limit_bytes=24 * 2**20),
        name=f"finish_{blocks[0]}",
    )(*args)


def shifted(array, axis, by, name):
    count = lax.axis_size(axis)
    pairs = [(i, i + by) for i in range(count) if 0 <= i + by < count]
    with jax.named_scope(name):
        return lax.ppermute(array, axis, pairs)


def shifted_both(array):
    rows, cols = (lax.axis_size(a) for a in AXES)
    pairs = [
        (i * cols + j, (i + 1) * cols + j + 1) for i in range(rows - 1) for j in range(cols - 1)
    ]
    with jax.named_scope("slant"):
        return lax.ppermute(array, AXES, pairs)


def place_of(index):
    s, m = divmod(index, 4)
    return [m % 2, (s // 16) * 2 + m // 2, (s // 4) % 4, s % 4]


def index_of(place):
    core, y, z, x = place
    return ((y // 2) * 16 + z * 4 + x) * 4 + (y % 2) * 2 + core


def swapped(array, axis, bits):
    pairs = []
    for i in range(128):
        place = place_of(i)
        place[axis] ^= bits
        pairs.append((i, index_of(place)))
    with jax.named_scope("swap_" + "cyzx"[axis] + str(bits)):
        return lax.ppermute(array, AXES, pairs)


def halved_sum(v, axis, here, pieces):
    v = v.reshape(pieces, -1, v.shape[-1])
    pick = functools.partial(lax.dynamic_index_in_dim, axis=0, keepdims=False)
    got = [swapped(pick(v, here ^ k), axis, k) for k in range(1, pieces)]
    if pieces == 2:
        return pick(v, here) + got[0]
    return (pick(v, here) + got[0]) + (got[1] + got[2])


def exchanged_sum(v, axis):
    a, b, c = [swapped(v, axis, k) for k in (1, 2, 3)]
    return (v + a) + (b + c)


def gathered(v, axis, here, pieces):
    parts = [v] + [swapped(v, axis, k) for k in range(1, pieces)]

    def part_of(i):
        which = here ^ i
        if pieces == 2:
            return jnp.where(which == 0, parts[0], parts[1])
        return jnp.where(
            which < 2,
            jnp.where(which == 0, parts[0], parts[1]),
            jnp.where(which == 2, parts[2], parts[3]),
        )

    return jnp.concatenate([part_of(i) for i in range(pieces)], 0)


BOUNDS = (3, 6, 9, 12, 15, 16)


def shards(field, probe, measured, offsets, live):
    rows, cols = field.shape[1:]
    base = jnp.stack([lax.axis_index("scan") * rows, lax.axis_index("mode") * cols])
    off = offsets - base[None, :]
    tabs = [jnp.asarray(t) for t in tables()]
    probe_rows = probe.reshape(2, 2, 128, 2, 256).transpose(0, 1, 3, 2, 4).reshape(probe.shape)
    tie = lax.optimization_barrier
    halos = []
    left_over = field
    for i, (a, b) in enumerate(zip((0,) + BOUNDS[:-1], BOUNDS)):
        part, left_over = tie((left_over[:, :, LANE * a : LANE * b], left_over))
        if i >= 4:
            part, halos[i - 4] = tie((part, halos[i - 4]))
        halos.append(shifted(part, "scan", -1, f"halo_{i}"))
    beside = jnp.concatenate([field[:, :, :SIZE], halos[0][:, :, :SIZE]], 1)
    corner = shifted(beside, "mode", -1, "corner")
    carry = jnp.zeros((2, 2, 2 * SIZE, LANE), f32)
    acc = jnp.zeros(probe.shape, f32)
    ends = [b - 2 for b in BOUNDS[:-1]] + [BOUNDS[-1]]
    plan = [(a, b - a) for a, b in zip([0] + ends[:-1], ends)]
    needed = {3: (0, 1), 4: (2,), 5: (3,)}
    uppers, lowers, comings = [], [], []
    for i, (first, count) in enumerate(plan):
        after = [comings[j] for j in needed.get(i, ())]
        *parts, acc = run_group(
            first, count, BOUNDS, live, off, field, halos, corner, measured, probe_rows, tabs, carry, acc, after
        )
        uppers.append(parts[0])
        lowers.append(parts[1])
        if i + 1 < len(plan):
            carry = parts[2]
        comings.append(shifted(lowers[i], "scan", 1, f"grad_{i}"))
    over_upper, over_lower = parts[2:]
    s, m = lax.axis_index("scan"), lax.axis_index("mode")
    core, y = m % 2, (s // 16) * 2 + m // 2
    v = halved_sum(acc.reshape(1024, 256), 0, core, 2)
    over = shifted(over_upper, "mode", 1, "over")
    v, comings[4] = tie((v, comings[4]))
    v = halved_sum(v, 1, y, 4)
    v, over = tie((v, over))
    v = exchanged_sum(v, 2)
    v, comings[5] = tie((v, comings[5]))
    v = exchanged_sum(v, 3)
    slots_all = lax.axis_size("scan") * lax.axis_size("mode") * SLOTS
    v = v * (1.0 / math.sqrt(slots_all))
    sources = [(first, array) for (first, _), pair in zip(plan, zip(uppers, comings)) for array in pair]
    step = finish(range(2, 13), sources[2:10], field.shape, None)
    v, over_lower, step = tie((v, over_lower, step))
    slant = shifted_both(over_lower)
    v = gathered(v, 1, y, 4)
    v, slant = tie((v, slant))
    probe_step = gathered(v, 0, core, 2).reshape(probe.shape)
    rest = sources[:4] + sources[10:] + [(0, over), (0, slant)]
    step = finish([0, 1, 13, 14, 15], rest, field.shape, step)
    return (step, probe_step)


def solution(mesh):
    in_specs = (
        P(None, "scan", "mode"),
        P(),
        P(AXES, None, None),
        P(AXES, None),
        P(AXES),
    )
    out_specs = (P(None, "scan", "mode"), P())
    return jax.shard_map(shards, mesh=mesh, in_specs=in_specs, out_specs=out_specs, check_vma=False)
```

time: 257 us -> 224 us (0.87)
  the two profiles are of different devices: /device:TPU:104 before, /device:TPU:1 now
where the time goes in v3:
time: 224 us; the launch traced here: 221 us
  starting transfers between devices  71.7 us (32%)
  waiting for transfers between devices  55.6 us (25%)
  Pallas kernels  50.3 us (22%)
  local copies, waits for them, and re-layouts  34.7 us (15%)
  other arithmetic  6.73 us (3%)
    pallas_call x6, Pallas kernels, run_group(): pl.pallas_call(functools.partial(group_kernel, first, count, (homes[0], h...  45 us
    ppermute x14, starting transfers between devices, swapped(): return lax.ppermute(array, AXES, pairs)  38.9 us
    ppermute x14, waiting for transfers between devices, shifted(): return lax.ppermute(array, axis, pairs)  32.1 us
    ppermute x14, starting transfers between devices, shifted(): return lax.ppermute(array, axis, pairs)  29.9 us
    ppermute x14, waiting for transfers between devices, swapped(): return lax.ppermute(array, AXES, pairs)  23.5 us
    unnamed x73, local copies, waits for them, and re-layouts  18.8 us
    slice x6, local copies, waits for them, and re-layouts, shards(): part, left_over = tie((left_over[:, :, LANE * a:LANE * b], left_over))  11.2 us
    pallas_call x2, Pallas kernels, finish(): pl.pallas_call(functools.partial(finish_kernel, tuple(blocks), terms), ou...  5.28 us
  transfers between devices with their start and end apart: 29, of which 13 were waited for; matrix products, arithmetic and copies ran while one was open for 8% of the time, Pallas kernels for 23%

profile of v3, /device:TPU:1, one launch (start us, length us, event | category | flops | bytes accessed | tf_op | source)
XLA Modules:
  0.0 220.8 jit_solution(6721685979640095605)
XLA Ops:
  0.7 2.2 %slice.24 = f32[2,256,384]{2,1,0:T(8,128)} slice(f32[2,256,2048]{2,1,0:T(8,128)} %refs_0_.11), slice={[0:2], [0:256], [0:384]} | slice | bytes 1572864 | tf_op jit(solution)/shard_map/slice | solution.py:419
  2.9 1.3 collective-permute-start
  4.2 2.1 slice.25
  6.2 1.3 collective-permute-start.2
  7.5 2.1 slice.26
  9.6 1.3 collective-permute-start.7
  11.9 1.3 collective-permute-start.8
  14.0 2.2 slice.28
  16.1 1.6 reshape.17
  17.7 1.3 copy.13
  19.0 1.7 slice.29
  20.8 3.0 %collective-permute-done.refs_1_ = f32[2,256,384]{2,1,0:T(8,128)S(1)} collective-permute-done((f32[2,256,384]{2,1,0:T(8,128)}, f32[2,256,384]{2,1,0:T(8,128)S(1)}, u32[]{:S(2)}, u32[]{:S(2)}) %collective-permute-start) | collective-permute-done | bytes 786464 | tf_op jit(solution)/shard_map/halo_0/ppermute | solution.py:344
  24.0 2.2 copy-done.1
  26.1 2.2 copy-done.17
  30.3 5.3 %group_0.1 = (f32[2,1,256,128]{3,2,1,0:T(8,128)S(1)}, f32[2,1,256,128]{3,2,1,0:T(8,128)S(1)}, f32[2,2,512,128]{3,2,1,0:T(8,128)S(1)}, f32[2,2,256,256]{3,2,1,0:T(8,128)S(1)}) custom-call(s32[1]{0:T(128)S(6)} %copy.15.live, s32[16,2]{1,0:T(8,128)S(1)} %broadcast_subtract_fusion.off, f32[2,256,2048]{2,1,0:T(8,128)S(1)} %copy-done.1, ...), custom_call_target="tpu_custom_call" | custom-call | flops 17179869184 | bytes 4096 | tf_op jit(solution)/shard_map/group_0/pallas_call | solution.py:271
  36.3 1.4 collective-permute-start.1
  37.7 2.9 %collective-permute-done.2.refs_2_.refs_1_ = f32[2,256,384]{2,1,0:T(8,128)S(1)} collective-permute-done((f32[2,256,384]{2,1,0:T(8,128)}, f32[2,256,384]{2,1,0:T(8,128)S(1)}, u32[]{:S(2)}, u32[]{:S(2)}) %collective-permute-start.2) | collective-permute-done | bytes 786464 | tf_op jit(solution)/shard_map/halo_1/ppermute | solution.py:344
  40.7 3.6 %group_1.1 = (f32[2,3,256,128]{3,2,1,0:T(8,128)S(1)}, f32[2,3,256,128]{3,2,1,0:T(8,128)S(1)}, f32[2,2,512,128]{3,2,1,0:T(8,128)S(1)}, f32[2,2,256,256]{3,2,1,0:T(8,128)S(1)}) custom-call(s32[1]{0:T(128)S(6)} %copy.15.live, s32[16,2]{1,0:T(8,128)S(1)} %broadcast_subtract_fusion.off, f32[2,256,2048]{2,1,0:T(8,128)S(1)} %copy-done.1, ...), custom_call_target="tpu_custom_call" | custom-call | flops 17179869184 | bytes 4096 | tf_op jit(solution)/shard_map/group_1/pallas_call | solution.py:271
  44.3 2.2 collective-permute-start.3
  46.5 1.3 collective-permute-start.4
  47.8 9.8 %collective-permute-done.7.refs_2_.refs_1_ = f32[2,256,384]{2,1,0:T(8,128)} collective-permute-done((f32[2,256,384]{2,1,0:T(8,128)}, f32[2,256,384]{2,1,0:T(8,128)}, u32[]{:S(2)}, u32[]{:S(2)}) %collective-permute-start.7) | collective-permute-done | bytes 786464 | tf_op jit(solution)/shard_map/halo_2/ppermute | solution.py:344
  57.6 1.3 collective-permute-start.5
  60.0 6.4 %group_4.1 = (f32[2,3,256,128]{3,2,1,0:T(8,128)S(1)}, f32[2,3,256,128]{3,2,1,0:T(8,128)S(1)}, f32[2,2,512,128]{3,2,1,0:T(8,128)S(1)}, f32[2,2,256,256]{3,2,1,0:T(8,128)S(1)}) custom-call(s32[1]{0:T(128)S(6)} %copy.15.live, s32[16,2]{1,0:T(8,128)S(1)} %broadcast_subtract_fusion.off, f32[2,256,2048]{2,1,0:T(8,128)S(1)} %copy-done.1, ...), custom_call_target="tpu_custom_call" | custom-call | flops 17179869184 | bytes 4096 | tf_op jit(solution)/shard_map/group_4/pallas_call | solution.py:271
  66.5 7.9 %collective-permute-done.8.refs_2_.refs_1_ = f32[2,256,384]{2,1,0:T(8,128)} collective-permute-done((f32[2,256,384]{2,1,0:T(8,128)}, f32[2,256,384]{2,1,0:T(8,128)}, u32[]{:S(2)}, u32[]{:S(2)}) %collective-permute-start.8) | collective-permute-done | bytes 786464 | tf_op jit(solution)/shard_map/halo_3/ppermute | solution.py:344
  74.4 5.0 %collective-permute-start.6 = (f32[2,512,256]{2,1,0:T(8,128)S(1)}, f32[2,512,256]{2,1,0:T(8,128)S(1)}, u32[]{:S(2)}, u32[]{:S(2)}) collective-permute-start(f32[2,512,256]{2,1,0:T(8,128)S(1)} %pad_maximum_fusion), channel_id=1, source_target_pairs={{1,0},{2,1},{3,2},{5,4},{6,5},{7,6},{9,8},{10,9},{11,10},{13,12},{... | collective-permute-start | bytes 3145736 | tf_op jit(solution)/shard_map/corner/ppermute | solution.py:344
  79.4 3.2 %collective-permute-start.10 = (f32[2,3,256,128]{3,2,1,0:T(8,128)S(1)}, f32[2,3,256,128]{3,2,1,0:T(8,128)S(1)}, u32[]{:S(2)}, u32[]{:S(2)}) collective-permute-start(f32[2,3,256,128]{3,2,1,0:T(8,128)S(1)} %get-tuple-element.79), channel_id=1, source_target_pairs={{0,4},{4,8},{8,12},{12,16},{16,20},{20,24},{24,28},{28,32},{32,36}... | collective-permute-start | bytes 2359304 | tf_op jit(solution)/shard_map/grad_2/ppermute | solution.py:344
  82.7 6.5 %group_7.1 = (f32[2,3,256,128]{3,2,1,0:T(8,128)S(1)}, f32[2,3,256,128]{3,2,1,0:T(8,128)S(1)}, f32[2,2,512,128]{3,2,1,0:T(8,128)S(1)}, f32[2,2,256,256]{3,2,1,0:T(8,128)S(1)}) custom-call(s32[1]{0:T(128)S(6)} %copy.15.live, s32[16,2]{1,0:T(8,128)S(1)} %broadcast_subtract_fusion.off, f32[2,256,2048]{2,1,0:T(8,128)S(1)} %copy-done.1, ...), custom_call_target="tpu_custom_call" | custom-call | flops 17179869184 | bytes 4096 | tf_op jit(solution)/shard_map/group_7/pallas_call | solution.py:271
  90.1 1.3 collective-permute-start.9
  91.5 8.5 %collective-permute-done.10.refs_3_ = f32[2,3,256,128]{3,2,1,0:T(8,128)S(1)} collective-permute-done((f32[2,3,256,128]{3,2,1,0:T(8,128)S(1)}, f32[2,3,256,128]{3,2,1,0:T(8,128)S(1)}, u32[]{:S(2)}, u32[]{:S(2)}) %collective-permute-start.10) | collective-permute-done | bytes 786464 | tf_op jit(solution)/shard_map/grad_2/ppermute | solution.py:344
  100.0 14.9 %group_10.1 = (f32[2,3,256,128]{3,2,1,0:T(8,128)S(1)}, f32[2,3,256,128]{3,2,1,0:T(8,128)}, f32[2,2,512,128]{3,2,1,0:T(8,128)S(1)}, f32[2,2,256,256]{3,2,1,0:T(8,128)S(1)}) custom-call(s32[1]{0:T(128)S(6)} %copy.15.live, s32[16,2]{1,0:T(8,128)S(1)} %broadcast_subtract_fusion.off, f32[2,256,2048]{2,1,0:T(8,128)S(1)} %copy-done.1, ...), custom_call_target="tpu_custom_call" | custom-call | flops 17179869184 | bytes 4096 | tf_op jit(solution)/shard_map/group_10/pallas_call | solution.py:271
  115.8 2.2 collective-permute-start.12
  118.0 8.3 %group_13.1 = (f32[2,3,256,128]{3,2,1,0:T(8,128)S(1)}, f32[2,3,256,128]{3,2,1,0:T(8,128)S(1)}, f32[2,2,256,128]{3,2,1,0:T(8,128)S(1)}, f32[2,2,256,128]{3,2,1,0:T(8,128)}, f32[2,2,256,256]{3,2,1,0:T(8,128)S(1)}) custom-call(s32[1]{0:T(128)S(6)} %copy.15.live, s32[16,2]{1,0:T(8,128)S(1)} %broadcast_subtract_fusion.off, f32[2,256,2048]{2,1,0:T(8,128)S(1)} %copy-done.1, ...), custom_call_target="tpu_custom_call" | custom-call | flops 17179869184 | bytes 4096 | tf_op jit(solution)/shard_map/group_13/pallas_call | solution.py:271
  129.0 2.0 collective-permute-start.16
  131.0 5.0 %collective-permute-start.20 = (f32[2,3,256,128]{3,2,1,0:T(8,128)}, f32[2,3,256,128]{3,2,1,0:T(8,128)}, u32[]{:S(2)}, u32[]{:S(2)}) collective-permute-start(f32[2,3,256,128]{3,2,1,0:T(8,128)} %copy-done.18), channel_id=1, source_target_pairs={{0,4},{4,8},{8,12},{12,16},{16,20},{20,24},{24,28},{28,32},{32,36}... | collective-permute-start | bytes 2359304 | tf_op jit(solution)/shard_map/grad_5/ppermute | solution.py:344
  138.8 11.3 %collective-permute-start.14 = (f32[128,256]{1,0:T(8,128)S(1)}, f32[128,256]{1,0:T(8,128)}, u32[]{:S(2)}, u32[]{:S(2)}) collective-permute-start(f32[128,256]{1,0:T(8,128)S(1)} %get-tuple-element.111), channel_id=1, source_target_pairs={{0,64},{1,65},{2,66},{3,67},{4,68},{5,69},{6,70},{7,71},{8,72},{9,... | collective-permute-start | bytes 393224 | tf_op jit(solution)/shard_map/swap_y2/ppermute | solution.py:373
  150.1 6.6 %collective-permute-done.14 = f32[128,256]{1,0:T(8,128)} collective-permute-done((f32[128,256]{1,0:T(8,128)S(1)}, f32[128,256]{1,0:T(8,128)}, u32[]{:S(2)}, u32[]{:S(2)}) %collective-permute-start.14) | collective-permute-done | bytes 131104 | tf_op jit(solution)/shard_map/swap_y2/ppermute | solution.py:373
  156.7 2.8 %collective-permute-done.15 = f32[128,256]{1,0:T(8,128)} collective-permute-done((f32[128,256]{1,0:T(8,128)S(1)}, f32[128,256]{1,0:T(8,128)}, u32[]{:S(2)}, u32[]{:S(2)}) %collective-permute-start.15) | collective-permute-done | bytes 131104 | tf_op jit(solution)/shard_map/swap_y3/ppermute | solution.py:373
  160.7 19.3 %collective-permute-start.19 = (f32[128,256]{1,0:T(8,128)S(1)}, f32[128,256]{1,0:T(8,128)S(1)}, u32[]{:S(2)}, u32[]{:S(2)}) collective-permute-start(f32[128,256]{1,0:T(8,128)S(1)} %fusion), channel_id=1, source_target_pairs={{0,48},{1,49},{2,50},{3,51},{4,52},{5,53},{6,54},{7,55},{8,56},{9,... | collective-permute-start | bytes 393224 | tf_op jit(solution)/shard_map/swap_z3/ppermute | solution.py:373
  180.5 1.9 collective-permute-done.18
  182.4 1.3 collective-permute-done.19
  185.5 1.8 collective-permute-start.21
  191.9 2.9 %finish_2.1.refs_8_ = f32[2,256,2048]{2,1,0:T(8,128)} custom-call(f32[2,3,256,128]{3,2,1,0:T(8,128)S(1)} %get-tuple-element.68.refs_0_.refs_2_, f32[2,3,256,128]{3,2,1,0:T(8,128)S(1)} %collective-permute-done.3.refs_4_.refs_1_.refs_3_, f32[2,3,256,128]{3,2,1,0:T(8,128)S(1)} %copy-done.4, f32[2,3,256,128]{3,2,1,0:T(8,128)S(1)} %copy-done.6, ...), custom_call_target="tpu_custom_call" | custom-call | tf_op jit(solution)/shard_map/finish_2/pallas_call | solution.py:325
  194.9 2.8 %collective-permute-start.27 = (f32[2,2,256,128]{3,2,1,0:T(8,128)}, f32[2,2,256,128]{3,2,1,0:T(8,128)S(1)}, u32[]{:S(2)}, u32[]{:S(2)}) collective-permute-start(f32[2,2,256,128]{3,2,1,0:T(8,128)} %get-tuple-element.100), channel_id=1, source_target_pairs={{0,5},{1,6},{2,7},{4,9},{5,10},{6,11},{8,13},{9,14},{10,15},{12,17... | collective-permute-start | bytes 1572872 | tf_op jit(solution)/shard_map/slant/ppermute | solution.py:353
  197.7 5.0 %collective-permute-start.25 = (f32[128,256]{1,0:T(8,128)S(1)}, f32[128,256]{1,0:T(8,128)S(1)}, u32[]{:S(2)}, u32[]{:S(2)}) collective-permute-start(f32[128,256]{1,0:T(8,128)S(1)} %add_multiply_fusion), channel_id=1, source_target_pairs={{0,64},{1,65},{2,66},{3,67},{4,68},{5,69},{6,70},{7,71},{8,72},{9,... | collective-permute-start | bytes 393224 | tf_op jit(solution)/shard_map/swap_y2/ppermute | solution.py:373
  202.6 5.4 %collective-permute-done.25 = f32[128,256]{1,0:T(8,128)S(1)} collective-permute-done((f32[128,256]{1,0:T(8,128)S(1)}, f32[128,256]{1,0:T(8,128)S(1)}, u32[]{:S(2)}, u32[]{:S(2)}) %collective-permute-start.25) | collective-permute-done | bytes 131104 | tf_op jit(solution)/shard_map/swap_y2/ppermute | solution.py:373
  208.9 4.4 %collective-permute-done.24 = f32[128,256]{1,0:T(8,128)} collective-permute-done((f32[128,256]{1,0:T(8,128)S(1)}, f32[128,256]{1,0:T(8,128)}, u32[]{:S(2)}, u32[]{:S(2)}) %collective-permute-start.24) | collective-permute-done | bytes 131104 | tf_op jit(solution)/shard_map/swap_y1/ppermute | solution.py:373
  216.1 2.4 %finish_0.1 = f32[2,256,2048]{2,1,0:T(8,128)} custom-call(f32[2,1,256,128]{3,2,1,0:T(8,128)S(1)} %copy-done.14, f32[2,1,256,128]{3,2,1,0:T(8,128)S(1)} %copy-done.16, f32[2,3,256,128]{3,2,1,0:T(8,128)S(1)} %get-tuple-element.68.refs_0_.refs_2_, f32[2,3,256,128]{3,2,1,0:T(8,128)S(1)} %collective-permute-done.3.refs_4_.refs_1_.refs_3_, ...), custom_call_target="tpu_custom_call", output_to_operand_aliasing={{}: (8, {})} | custom-call | tf_op jit(solution)/shard_map/finish_0/pallas_call | solution.py:325
  218.5 1.3 broadcast_select_fusion.1
  (117 shorter events, 25.3 us)
Async XLA Ops:
  0.6 10.3 %copy-start = (f32[2,256,2048]{2,1,0:T(8,128)S(1)}, f32[2,256,2048]{2,1,0:T(8,128)}, u32[]{:S(2)}) copy-start(f32[2,256,2048]{2,1,0:T(8,128)} %refs_0_.11) | copy-start | bytes 12582916
  0.6 13.2 %copy-start.35 = (s32[16,2]{0,1:T(2,128)S(1)}, s32[16,2]{0,1:T(2,128)}, u32[]{:S(2)}) copy-start(s32[16,2]{0,1:T(2,128)} %param.12) | copy-start | bytes 388
  0.7 15.5 %copy-start.31 = (f32[2,2,256,256]{3,2,1,0:T(8,128)S(1)}, f32[2,2,256,256]{3,2,1,0:T(8,128)}, u32[]{:S(2)}) copy-start(f32[2,2,256,256]{3,2,1,0:T(8,128)} %param.10) | copy-start | bytes 3145732
  2.9 20.9 %collective-permute-start = (f32[2,256,384]{2,1,0:T(8,128)}, f32[2,256,384]{2,1,0:T(8,128)S(1)}, u32[]{:S(2)}, u32[]{:S(2)}) collective-permute-start(f32[2,256,384]{2,1,0:T(8,128)} %slice.24), channel_id=1, source_target_pairs={{4,0},{8,4},{12,8},{16,12},{20,16},{24,20},{28,24},{32,28},{36,32}... | collective-permute-start | bytes 2359304 | tf_op jit(solution)/shard_map/halo_0/ppermute | solution.py:344
  6.2 34.4 %collective-permute-start.2 = (f32[2,256,384]{2,1,0:T(8,128)}, f32[2,256,384]{2,1,0:T(8,128)S(1)}, u32[]{:S(2)}, u32[]{:S(2)}) collective-permute-start(f32[2,256,384]{2,1,0:T(8,128)} %slice.25), channel_id=1, source_target_pairs={{4,0},{8,4},{12,8},{16,12},{20,16},{24,20},{28,24},{32,28},{36,32}... | collective-permute-start | bytes 2359304 | tf_op jit(solution)/shard_map/halo_1/ppermute | solution.py:344
  9.6 48.0 %collective-permute-start.7 = (f32[2,256,384]{2,1,0:T(8,128)}, f32[2,256,384]{2,1,0:T(8,128)}, u32[]{:S(2)}, u32[]{:S(2)}) collective-permute-start(f32[2,256,384]{2,1,0:T(8,128)} %slice.26), channel_id=1, source_target_pairs={{4,0},{8,4},{12,8},{16,12},{20,16},{24,20},{28,24},{32,28},{36,32}... | collective-permute-start | bytes 2359304 | tf_op jit(solution)/shard_map/halo_2/ppermute | solution.py:344
  11.9 62.5 %collective-permute-start.8 = (f32[2,256,384]{2,1,0:T(8,128)}, f32[2,256,384]{2,1,0:T(8,128)}, u32[]{:S(2)}, u32[]{:S(2)}) collective-permute-start(f32[2,256,384]{2,1,0:T(8,128)} %slice.27), channel_id=1, source_target_pairs={{4,0},{8,4},{12,8},{16,12},{20,16},{24,20},{28,24},{32,28},{36,32}... | collective-permute-start | bytes 2359304 | tf_op jit(solution)/shard_map/halo_3/ppermute | solution.py:344
  14.0 10.0 %copy-start.22 = (bf16[512,512]{1,0:T(8,128)(2,1)S(1)}, bf16[512,512]{1,0:T(8,128)(2,1)}, u32[]{:S(2)}) copy-start(bf16[512,512]{1,0:T(8,128)(2,1)} %constant.82.clone.refs_5_.refs_6_.refs_8_.refs_7_) | copy-start | bytes 1572868
  14.0 10.0 %copy-start.26 = (bf16[2,256,256]{2,1,0:T(8,128)(2,1)S(1)}, bf16[2,256,256]{2,1,0:T(8,128)(2,1)}, u32[]{:S(2)}) copy-start(bf16[2,256,256]{2,1,0:T(8,128)(2,1)} %constant.81.clone.refs_4_.refs_5_.refs_7_.refs_6_) | copy-start | bytes 786436
  30.3 10.3 %copy-start.23 = (bf16[512,512]{1,0:T(8,128)(2,1)S(1)}, bf16[512,512]{1,0:T(8,128)(2,1)}, u32[]{:S(2)}) copy-start(bf16[512,512]{1,0:T(8,128)(2,1)} %constant.82.clone.refs_5_.refs_6_.refs_8_.refs_7_) | copy-start | bytes 1572868
  30.3 10.3 %copy-start.25 = (bf16[512,512]{1,0:T(8,128)(2,1)S(1)}, bf16[512,512]{1,0:T(8,128)(2,1)}, u32[]{:S(2)}) copy-start(bf16[512,512]{1,0:T(8,128)(2,1)} %constant.84.clone.refs_7_.refs_8_.refs_10_.refs_9_) | copy-start | bytes 1572868
  30.3 10.3 %copy-start.27 = (bf16[2,256,256]{2,1,0:T(8,128)(2,1)S(1)}, bf16[2,256,256]{2,1,0:T(8,128)(2,1)}, u32[]{:S(2)}) copy-start(bf16[2,256,256]{2,1,0:T(8,128)(2,1)} %constant.81.clone.refs_4_.refs_5_.refs_7_.refs_6_) | copy-start | bytes 786436
  30.3 10.3 %copy-start.29 = (bf16[2,256,256]{2,1,0:T(8,128)(2,1)S(1)}, bf16[2,256,256]{2,1,0:T(8,128)(2,1)}, u32[]{:S(2)}) copy-start(bf16[2,256,256]{2,1,0:T(8,128)(2,1)} %constant.83.clone.refs_6_.refs_7_.refs_9_.refs_8_) | copy-start | bytes 786436
  36.3 43.1 %collective-permute-start.1 = (f32[2,1,256,128]{3,2,1,0:T(8,128)S(1)}, f32[2,1,256,128]{3,2,1,0:T(8,128)S(1)}, u32[]{:S(2)}, u32[]{:S(2)}) collective-permute-start(f32[2,1,256,128]{3,2,1,0:T(8,128)S(1)} %get-tuple-element.61), channel_id=1, source_target_pairs={{0,4},{4,8},{8,12},{12,16},{16,20},{20,24},{24,28},{28,32},{32,36}... | collective-permute-start | bytes 786440 | tf_op jit(solution)/shard_map/grad_0/ppermute | solution.py:344
  40.6 3.7 %copy-start.19 = (f32[2,256,384]{2,1,0:T(8,128)}, f32[2,256,384]{2,1,0:T(8,128)S(1)}, u32[]{:S(2)}) copy-start(f32[2,256,384]{2,1,0:T(8,128)S(1)} %collective-permute-done.2.refs_2_.refs_1_) | copy-start | bytes 2359300
  40.7 5.8 %copy-start.32 = (f32[2,256,384]{2,1,0:T(8,128)S(1)}, f32[2,256,384]{2,1,0:T(8,128)}, u32[]{:S(2)}) copy-start(f32[2,256,384]{2,1,0:T(8,128)} %slice.28) | copy-start | bytes 2359300
  40.7 16.9 %copy-start.33 = (f32[2,256,128]{2,1,0:T(8,128)S(1)}, f32[2,256,128]{2,1,0:T(8,128)}, u32[]{:S(2)}) copy-start(f32[2,256,128]{2,1,0:T(8,128)} %slice.29) | copy-start | bytes 786436
  44.3 38.3 %collective-permute-start.3 = (f32[2,3,256,128]{3,2,1,0:T(8,128)S(1)}, f32[2,3,256,128]{3,2,1,0:T(8,128)S(1)}, u32[]{:S(2)}, u32[]{:S(2)}) collective-permute-start(f32[2,3,256,128]{3,2,1,0:T(8,128)S(1)} %get-tuple-element.69), channel_id=1, source_target_pairs={{0,4},{4,8},{8,12},{12,16},{16,20},{20,24},{24,28},{28,32},{32,36}... | collective-permute-start | bytes 2359304 | tf_op jit(solution)/shard_map/grad_1/ppermute | solution.py:344
  46.5 45.0 %collective-permute-start.4 = (f32[2,256,384]{2,1,0:T(8,128)S(1)}, f32[2,256,384]{2,1,0:T(8,128)S(1)}, u32[]{:S(2)}, u32[]{:S(2)}) collective-permute-start(f32[2,256,384]{2,1,0:T(8,128)S(1)} %copy-done.32), channel_id=1, source_target_pairs={{4,0},{8,4},{12,8},{16,12},{20,16},{24,20},{28,24},{32,28},{36,32}... | collective-permute-start | bytes 2359304 | tf_op jit(solution)/shard_map/halo_4/ppermute | solution.py:344
  57.6 60.4 %collective-permute-start.5 = (f32[2,256,128]{2,1,0:T(8,128)S(1)}, f32[2,256,128]{2,1,0:T(8,128)S(1)}, u32[]{:S(2)}, u32[]{:S(2)}) collective-permute-start(f32[2,256,128]{2,1,0:T(8,128)S(1)} %copy-done.33), channel_id=1, source_target_pairs={{4,0},{8,4},{12,8},{16,12},{20,16},{24,20},{28,24},{32,28},{36,32}... | collective-permute-start | bytes 786440 | tf_op jit(solution)/shard_map/halo_5/ppermute | solution.py:344
  60.0 6.4 %slice-start = ((f32[2,256,2048]{2,1,0:T(8,128)}), f32[2,256,256]{2,1,0:T(8,128)S(1)}, s32[]{:S(2)}) async-start(f32[2,256,2048]{2,1,0:T(8,128)} %refs_0_.11), calls=%async_computation | async-start | bytes 1048576 | tf_op jit(solution)/shard_map/slice | solution.py:423
  66.4 22.9 %copy-start.3 = (f32[2,3,256,128]{3,2,1,0:T(8,128)}, f32[2,3,256,128]{3,2,1,0:T(8,128)S(1)}, u32[]{:S(2)}) copy-start(f32[2,3,256,128]{3,2,1,0:T(8,128)S(1)} %get-tuple-element.95.refs_2_) | copy-start | bytes 2359300
  74.4 43.6 %collective-permute-start.6 = (f32[2,512,256]{2,1,0:T(8,128)S(1)}, f32[2,512,256]{2,1,0:T(8,128)S(1)}, u32[]{:S(2)}, u32[]{:S(2)}) collective-permute-start(f32[2,512,256]{2,1,0:T(8,128)S(1)} %pad_maximum_fusion), channel_id=1, source_target_pairs={{1,0},{2,1},{3,2},{5,4},{6,5},{7,6},{9,8},{10,9},{11,10},{13,12},{... | collective-permute-start | bytes 3145736 | tf_op jit(solution)/shard_map/corner/ppermute | solution.py:344
  79.4 9.8 %copy-start.15 = (f32[2,1,256,128]{3,2,1,0:T(8,128)}, f32[2,1,256,128]{3,2,1,0:T(8,128)S(1)}, u32[]{:S(2)}) copy-start(f32[2,1,256,128]{3,2,1,0:T(8,128)S(1)} %collective-permute-done.1.refs_3_.refs_1_) | copy-start | bytes 786436
  79.4 20.5 %collective-permute-start.10 = (f32[2,3,256,128]{3,2,1,0:T(8,128)S(1)}, f32[2,3,256,128]{3,2,1,0:T(8,128)S(1)}, u32[]{:S(2)}, u32[]{:S(2)}) collective-permute-start(f32[2,3,256,128]{3,2,1,0:T(8,128)S(1)} %get-tuple-element.79), channel_id=1, source_target_pairs={{0,4},{4,8},{8,12},{12,16},{16,20},{20,24},{24,28},{28,32},{32,36}... | collective-permute-start | bytes 2359304 | tf_op jit(solution)/shard_map/grad_2/ppermute | solution.py:344
  90.1 27.9 %collective-permute-start.9 = (f32[2,3,256,128]{3,2,1,0:T(8,128)S(1)}, f32[2,3,256,128]{3,2,1,0:T(8,128)S(1)}, u32[]{:S(2)}, u32[]{:S(2)}) collective-permute-start(f32[2,3,256,128]{3,2,1,0:T(8,128)S(1)} %get-tuple-element.78), channel_id=1, source_target_pairs={{0,4},{4,8},{8,12},{12,16},{16,20},{20,24},{24,28},{28,32},{32,36}... | collective-permute-start | bytes 2359304 | tf_op jit(solution)/shard_map/grad_3/ppermute | solution.py:344
  100.0 15.0 %copy-start.5 = (f32[2,3,256,128]{3,2,1,0:T(8,128)}, f32[2,3,256,128]{3,2,1,0:T(8,128)S(1)}, u32[]{:S(2)}) copy-start(f32[2,3,256,128]{3,2,1,0:T(8,128)S(1)} %collective-permute-done.10.refs_3_) | copy-start | bytes 2359300
  115.8 21.5 %collective-permute-start.12 = (f32[2,3,256,128]{3,2,1,0:T(8,128)}, f32[2,3,256,128]{3,2,1,0:T(8,128)}, u32[]{:S(2)}, u32[]{:S(2)}) collective-permute-start(f32[2,3,256,128]{3,2,1,0:T(8,128)} %get-tuple-element.86), channel_id=1, source_target_pairs={{0,4},{4,8},{8,12},{12,16},{16,20},{20,24},{24,28},{28,32},{32,36}... | collective-permute-start | bytes 2359304 | tf_op jit(solution)/shard_map/grad_4/ppermute | solution.py:344
  118.0 8.3 %copy-start.9 = (f32[2,3,256,128]{3,2,1,0:T(8,128)}, f32[2,3,256,128]{3,2,1,0:T(8,128)S(1)}, u32[]{:S(2)}) copy-start(f32[2,3,256,128]{3,2,1,0:T(8,128)S(1)} %collective-permute-done.9.refs_4_.refs_5_) | copy-start | bytes 2359300
  127.2 60.2 %copy-start.4 = (f32[2,3,256,128]{3,2,1,0:T(8,128)S(1)}, f32[2,3,256,128]{3,2,1,0:T(8,128)}, u32[]{:S(2)}) copy-start(f32[2,3,256,128]{3,2,1,0:T(8,128)} %copy-done.3) | copy-start | bytes 2359300
  129.0 7.0 %collective-permute-start.11 = (f32[512,256]{1,0:T(8,128)}, f32[512,256]{1,0:T(8,128)}, u32[]{:S(2)}, u32[]{:S(2)}) collective-permute-start(f32[512,256]{1,0:T(8,128)} %dynamic-slice_bitcast_fusion), channel_id=1, source_target_pairs={{0,1},{1,0},{2,3},{3,2},{4,5},{5,4},{6,7},{7,6},{8,9},{9,8},{10,11... | collective-permute-start | bytes 1572872 | tf_op jit(solution)/shard_map/swap_c1/ppermute | solution.py:373
  129.0 31.6 %collective-permute-start.16 = (f32[2,2,256,128]{3,2,1,0:T(8,128)}, f32[2,2,256,128]{3,2,1,0:T(8,128)}, u32[]{:S(2)}, u32[]{:S(2)}) collective-permute-start(f32[2,2,256,128]{3,2,1,0:T(8,128)} %copy-done.21), channel_id=1, source_target_pairs={{0,1},{1,2},{2,3},{4,5},{5,6},{6,7},{8,9},{9,10},{10,11},{12,13},{... | collective-permute-start | bytes 1572872 | tf_op jit(solution)/shard_map/over/ppermute | solution.py:344
  131.0 53.6 %collective-permute-start.20 = (f32[2,3,256,128]{3,2,1,0:T(8,128)}, f32[2,3,256,128]{3,2,1,0:T(8,128)}, u32[]{:S(2)}, u32[]{:S(2)}) collective-permute-start(f32[2,3,256,128]{3,2,1,0:T(8,128)} %copy-done.18), channel_id=1, source_target_pairs={{0,4},{4,8},{8,12},{12,16},{16,20},{20,24},{24,28},{28,32},{32,36}... | collective-permute-start | bytes 2359304 | tf_op jit(solution)/shard_map/grad_5/ppermute | solution.py:344
  138.8 11.4 %collective-permute-start.13 = (f32[128,256]{1,0:T(8,128)}, f32[128,256]{1,0:T(8,128)S(1)}, u32[]{:S(2)}, u32[]{:S(2)}) collective-permute-start(f32[128,256]{1,0:T(8,128)} %get-tuple-element.112), channel_id=1, source_target_pairs={{0,2},{1,3},{2,0},{3,1},{4,6},{5,7},{6,4},{7,5},{8,10},{9,11},{10,... | collective-permute-start | bytes 393224 | tf_op jit(solution)/shard_map/swap_y1/ppermute | solution.py:373
  138.8 17.9 %collective-permute-start.14 = (f32[128,256]{1,0:T(8,128)S(1)}, f32[128,256]{1,0:T(8,128)}, u32[]{:S(2)}, u32[]{:S(2)}) collective-permute-start(f32[128,256]{1,0:T(8,128)S(1)} %get-tuple-element.111), channel_id=1, source_target_pairs={{0,64},{1,65},{2,66},{3,67},{4,68},{5,69},{6,70},{7,71},{8,72},{9,... | collective-permute-start | bytes 393224 | tf_op jit(solution)/shard_map/swap_y2/ppermute | solution.py:373
  150.1 9.4 %collective-permute-start.15 = (f32[128,256]{1,0:T(8,128)S(1)}, f32[128,256]{1,0:T(8,128)}, u32[]{:S(2)}, u32[]{:S(2)}) collective-permute-start(f32[128,256]{1,0:T(8,128)S(1)} %get-tuple-element.110), channel_id=1, source_target_pairs={{0,66},{1,67},{2,64},{3,65},{4,70},{5,71},{6,68},{7,69},{8,74},{9,... | collective-permute-start | bytes 393224 | tf_op jit(solution)/shard_map/swap_y3/ppermute | solution.py:373
  160.6 21.8 %collective-permute-start.18 = (f32[128,256]{1,0:T(8,128)S(1)}, f32[128,256]{1,0:T(8,128)S(1)}, u32[]{:S(2)}, u32[]{:S(2)}) collective-permute-start(f32[128,256]{1,0:T(8,128)S(1)} %fusion), channel_id=1, source_target_pairs={{0,32},{1,33},{2,34},{3,35},{4,36},{5,37},{6,38},{7,39},{8,40},{9,... | collective-permute-start | bytes 393224 | tf_op jit(solution)/shard_map/swap_z2/ppermute | solution.py:373
  160.7 23.0 %collective-permute-start.19 = (f32[128,256]{1,0:T(8,128)S(1)}, f32[128,256]{1,0:T(8,128)S(1)}, u32[]{:S(2)}, u32[]{:S(2)}) collective-permute-start(f32[128,256]{1,0:T(8,128)S(1)} %fusion), channel_id=1, source_target_pairs={{0,48},{1,49},{2,50},{3,51},{4,52},{5,53},{6,54},{7,55},{8,56},{9,... | collective-permute-start | bytes 393224 | tf_op jit(solution)/shard_map/swap_z3/ppermute | solution.py:373
  180.0 4.6 %collective-permute-start.17 = (f32[128,256]{1,0:T(8,128)S(1)}, f32[128,256]{1,0:T(8,128)S(1)}, u32[]{:S(2)}, u32[]{:S(2)}) collective-permute-start(f32[128,256]{1,0:T(8,128)S(1)} %fusion), channel_id=1, source_target_pairs={{0,16},{1,17},{2,18},{3,19},{4,20},{5,21},{6,22},{7,23},{8,24},{9,... | collective-permute-start | bytes 393224 | tf_op jit(solution)/shard_map/swap_z1/ppermute | solution.py:373
  184.7 10.1 %collective-permute-start.22 = (f32[128,256]{1,0:T(8,128)S(1)}, f32[128,256]{1,0:T(8,128)S(1)}, u32[]{:S(2)}, u32[]{:S(2)}) collective-permute-start(f32[128,256]{1,0:T(8,128)S(1)} %add_add_fusion), channel_id=1, source_target_pairs={{0,8},{1,9},{2,10},{3,11},{4,12},{5,13},{6,14},{7,15},{8,0},{9,1},... | collective-permute-start | bytes 393224 | tf_op jit(solution)/shard_map/swap_x2/ppermute | solution.py:373
  184.8 10.1 %collective-permute-start.23 = (f32[128,256]{1,0:T(8,128)S(1)}, f32[128,256]{1,0:T(8,128)S(1)}, u32[]{:S(2)}, u32[]{:S(2)}) collective-permute-start(f32[128,256]{1,0:T(8,128)S(1)} %add_add_fusion), channel_id=1, source_target_pairs={{0,12},{1,13},{2,14},{3,15},{4,8},{5,9},{6,10},{7,11},{8,4},{9,5},... | collective-permute-start | bytes 393224 | tf_op jit(solution)/shard_map/swap_x3/ppermute | solution.py:373
  185.5 9.3 %collective-permute-start.21 = (f32[128,256]{1,0:T(8,128)S(1)}, f32[128,256]{1,0:T(8,128)S(1)}, u32[]{:S(2)}, u32[]{:S(2)}) collective-permute-start(f32[128,256]{1,0:T(8,128)S(1)} %add_add_fusion), channel_id=1, source_target_pairs={{0,4},{1,5},{2,6},{3,7},{4,0},{5,1},{6,2},{7,3},{8,12},{9,13},{10,... | collective-permute-start | bytes 393224 | tf_op jit(solution)/shard_map/swap_x1/ppermute | solution.py:373
  191.9 23.2 %copy-start.14 = (f32[2,1,256,128]{3,2,1,0:T(8,128)S(1)}, f32[2,1,256,128]{3,2,1,0:T(8,128)}, u32[]{:S(2)}) copy-start(f32[2,1,256,128]{3,2,1,0:T(8,128)} %copy-done.13) | copy-start | bytes 786436
  194.9 20.3 %collective-permute-start.27 = (f32[2,2,256,128]{3,2,1,0:T(8,128)}, f32[2,2,256,128]{3,2,1,0:T(8,128)S(1)}, u32[]{:S(2)}, u32[]{:S(2)}) collective-permute-start(f32[2,2,256,128]{3,2,1,0:T(8,128)} %get-tuple-element.100), channel_id=1, source_target_pairs={{0,5},{1,6},{2,7},{4,9},{5,10},{6,11},{8,13},{9,14},{10,15},{12,17... | collective-permute-start | bytes 1572872 | tf_op jit(solution)/shard_map/slant/ppermute | solution.py:353
  197.7 10.4 %collective-permute-start.25 = (f32[128,256]{1,0:T(8,128)S(1)}, f32[128,256]{1,0:T(8,128)S(1)}, u32[]{:S(2)}, u32[]{:S(2)}) collective-permute-start(f32[128,256]{1,0:T(8,128)S(1)} %add_multiply_fusion), channel_id=1, source_target_pairs={{0,64},{1,65},{2,66},{3,67},{4,68},{5,69},{6,70},{7,71},{8,72},{9,... | collective-permute-start | bytes 393224 | tf_op jit(solution)/shard_map/swap_y2/ppermute | solution.py:373
  202.6 5.6 %collective-permute-start.26 = (f32[128,256]{1,0:T(8,128)S(1)}, f32[128,256]{1,0:T(8,128)S(1)}, u32[]{:S(2)}, u32[]{:S(2)}) collective-permute-start(f32[128,256]{1,0:T(8,128)S(1)} %add_multiply_fusion), channel_id=1, source_target_pairs={{0,66},{1,67},{2,64},{3,65},{4,70},{5,71},{6,68},{7,69},{8,74},{9,... | collective-permute-start | bytes 393224 | tf_op jit(solution)/shard_map/swap_y3/ppermute | solution.py:373
  202.6 10.6 %collective-permute-start.24 = (f32[128,256]{1,0:T(8,128)S(1)}, f32[128,256]{1,0:T(8,128)}, u32[]{:S(2)}, u32[]{:S(2)}) collective-permute-start(f32[128,256]{1,0:T(8,128)S(1)} %add_multiply_fusion), channel_id=1, source_target_pairs={{0,2},{1,3},{2,0},{3,1},{4,6},{5,7},{6,4},{7,5},{8,10},{9,11},{10,... | collective-permute-start | bytes 393224 | tf_op jit(solution)/shard_map/swap_y1/ppermute | solution.py:373
  215.1 3.4 %collective-permute-start.28 = (f32[512,256]{1,0:T(8,128)}, f32[512,256]{1,0:T(8,128)}, u32[]{:S(2)}, u32[]{:S(2)}) collective-permute-start(f32[512,256]{1,0:T(8,128)} %pad_maximum_fusion.2), channel_id=1, source_target_pairs={{0,1},{1,0},{2,3},{3,2},{4,5},{5,4},{6,7},{7,6},{8,9},{9,8},{10,11... | collective-permute-start | bytes 1572872 | tf_op jit(solution)/shard_map/swap_c1/ppermute | solution.py:373
  (18 other events, 20.6 us)

commit v4 on v3

--- a/solution.py
+++ b/solution.py
@@ -150,10 +150,7 @@
     sources = refs[: len(homes[2])]
     refs = refs[len(homes[2]) + n_after :]
     measured, probe, t0, t1, t2, t3, carry, acc_in = refs[:8]
-    if last:
-        upper, lower, over_upper, over_lower, acc = refs[8:13]
-    else:
-        upper, lower, carry_out, acc = refs[8:12]
+    upper, lower, carry_out, acc = refs[8:12]
     ext, grad, frame, picked, load_sem, frame_sem = refs[-6:]
 
     def pick(q, n):
@@ -217,11 +214,8 @@
     lax.fori_loop(0, n, step, 0)
     upper[...] = grad[:, 0:count, :SIZE]
     lower[...] = grad[:, 0:count, SIZE:]
-    if not last:
-        carry_out[...] = grad[:, count:]
-    else:
-        over_upper[...] = grad[:, count:, :SIZE]
-        over_lower[...] = grad[:, count:, SIZE:]
+    carry_out[...] = grad[:, count:]
+    if last:
         for k in (0, 1):
             for part in (0, 1):
                 for b in (0, 1):
@@ -264,9 +258,8 @@
     specs = [IN_SMEM] * 2 + [IN_HBM] * (1 + len(arrays) + len(after)) + [IN_VMEM] * 7
     part = jax.ShapeDtypeStruct((2, count, SIZE, LANE), f32)
     last = first + count == bounds[-1]
-    edge = jax.ShapeDtypeStruct((2, 2, SIZE, LANE), f32)
     whole = jax.ShapeDtypeStruct((2, 2, 2 * SIZE, LANE), f32)
-    out_shape = (part, part) + ((edge, edge) if last else (whole,))
+    out_shape = (part, part, whole)
     out_shape += (jax.ShapeDtypeStruct((2, 2, SIZE, SIZE), f32),)
     return pl.pallas_call(
         functools.partial(group_kernel, first, count, (homes[0], homes[1], [None] * len(arrays)),
@@ -283,7 +276,7 @@
             pltpu.SemaphoreType.DMA((4,)),
         ],
         compiler_params=pltpu.CompilerParams(vmem_limit_bytes=30 * 2**20),
-        cost_estimate=pl.CostEstimate(flops=2**34, bytes_accessed=2**12, transcendentals=0),
+        cost_estimate=pl.CostEstimate(flops=2**32, bytes_accessed=2**12, transcendentals=0),
         name=f"group_{first}",
     )(*args)
 
@@ -294,7 +287,7 @@
     for at, (block, many) in enumerate(zip(blocks, terms)):
         value = None
         for which, b in many:
-            term = refs[which][:, b]
+            term = refs[which][:, b, :SIZE]
             value = term if value is None else value + term
         buf[at] = value
         copy = pltpu.make_async_copy(
@@ -344,15 +337,6 @@
         return lax.ppermute(array, axis, pairs)
 
 
-def shifted_both(array):
-    rows, cols = (lax.axis_size(a) for a in AXES)
-    pairs = [
-        (i * cols + j, (i + 1) * cols + j + 1) for i in range(rows - 1) for j in range(cols - 1)
-    ]
-    with jax.named_scope("slant"):
-        return lax.ppermute(array, AXES, pairs)
-
-
 def place_of(index):
     s, m = divmod(index, 4)
     return [m % 2, (s // 16) * 2 + m // 2, (s // 4) % 4, s % 4]
@@ -403,7 +387,7 @@
     return jnp.concatenate([part_of(i) for i in range(pieces)], 0)
 
 
-BOUNDS = (3, 6, 9, 12, 15, 16)
+BOUNDS = (4, 7, 10, 12, 15, 16)
 
 
 def shards(field, probe, measured, offsets, live):
@@ -413,52 +397,49 @@
     tabs = [jnp.asarray(t) for t in tables()]
     probe_rows = probe.reshape(2, 2, 128, 2, 256).transpose(0, 1, 3, 2, 4).reshape(probe.shape)
     tie = lax.optimization_barrier
-    halos = []
-    left_over = field
-    for i, (a, b) in enumerate(zip((0,) + BOUNDS[:-1], BOUNDS)):
-        part, left_over = tie((left_over[:, :, LANE * a : LANE * b], left_over))
-        if i >= 4:
-            part, halos[i - 4] = tie((part, halos[i - 4]))
-        halos.append(shifted(part, "scan", -1, f"halo_{i}"))
+    head, rest = tie((field[:, :, : LANE * BOUNDS[0]], field))
+    halos = [shifted(head, "scan", -1, "halo_0")]
+    for i, (a, b) in enumerate(zip(BOUNDS[:-1], BOUNDS[1:])):
+        part = rest[:, :, LANE * a : LANE * b]
+        halos.append(shifted(part, "scan", -1, f"halo_{i + 1}"))
     beside = jnp.concatenate([field[:, :, :SIZE], halos[0][:, :, :SIZE]], 1)
     corner = shifted(beside, "mode", -1, "corner")
     carry = jnp.zeros((2, 2, 2 * SIZE, LANE), f32)
     acc = jnp.zeros(probe.shape, f32)
     ends = [b - 2 for b in BOUNDS[:-1]] + [BOUNDS[-1]]
     plan = [(a, b - a) for a, b in zip([0] + ends[:-1], ends)]
-    needed = {3: (0, 1), 4: (2,), 5: (3,)}
     uppers, lowers, comings = [], [], []
     for i, (first, count) in enumerate(plan):
-        after = [comings[j] for j in needed.get(i, ())]
-        *parts, acc = run_group(
+        after = {3: (corner, 1), 4: (2,), 5: (3,)}.get(i, ())
+        after = [comings[j] if isinstance(j, int) else j for j in after]
+        upper, lower, carry, acc = run_group(
             first, count, BOUNDS, live, off, field, halos, corner, measured, probe_rows, tabs, carry, acc, after
         )
-        uppers.append(parts[0])
-        lowers.append(parts[1])
-        if i + 1 < len(plan):
-            carry = parts[2]
-        comings.append(shifted(lowers[i], "scan", 1, f"grad_{i}"))
-    over_upper, over_lower = parts[2:]
+        uppers.append(upper)
+        lowers.append(lower)
+        early = 0 < i < len(plan) - 1
+        comings.append(shifted(lower, "scan", 1, f"grad_{i}") if early else None)
     s, m = lax.axis_index("scan"), lax.axis_index("mode")
     core, y = m % 2, (s // 16) * 2 + m // 2
     v = halved_sum(acc.reshape(1024, 256), 0, core, 2)
-    over = shifted(over_upper, "mode", 1, "over")
-    v, comings[4] = tie((v, comings[4]))
+    v, comings[4], final = tie((v, comings[4], lowers[5]))
+    comings[5] = shifted(final, "scan", 1, "grad_5")
     v = halved_sum(v, 1, y, 4)
-    v, over = tie((v, over))
+    v, carry = tie((v, carry))
+    over = shifted(carry, "mode", 1, "over")
     v = exchanged_sum(v, 2)
-    v, comings[5] = tie((v, comings[5]))
+    sources = [(first, array) for (first, _), pair in zip(plan, zip(uppers, comings)) for array in pair]
+    step = finish(range(2, 13), sources[2:10], field.shape, None)
+    v, comings[5], step = tie((v, comings[5], step))
     v = exchanged_sum(v, 3)
     slots_all = lax.axis_size("scan") * lax.axis_size("mode") * SLOTS
     v = v * (1.0 / math.sqrt(slots_all))
-    sources = [(first, array) for (first, _), pair in zip(plan, zip(uppers, comings)) for array in pair]
-    step = finish(range(2, 13), sources[2:10], field.shape, None)
-    v, over_lower, step = tie((v, over_lower, step))
-    slant = shifted_both(over_lower)
+    v, over = tie((v, over))
+    comings[0] = shifted(lowers[0] + over[:, :, SIZE:], "scan", 1, "grad_0")
     v = gathered(v, 1, y, 4)
-    v, slant = tie((v, slant))
+    v, comings[0] = tie((v, comings[0]))
     probe_step = gathered(v, 0, core, 2).reshape(probe.shape)
-    rest = sources[:4] + sources[10:] + [(0, over), (0, slant)]
+    rest = [(0, uppers[0]), (0, comings[0]), (0, over), (13, uppers[5]), (13, comings[5])]
     step = finish([0, 1, 13, 14, 15], rest, field.shape, step)
     return (step, probe_step)
 

time: 224 us -> 236 us (1.054)
  starting transfers between devices: 71.7 us -> 96.9 us
  Pallas kernels: 50.3 us -> 33.7 us
  local copies, waits for them, and re-layouts: 34.7 us -> 37.6 us
    pallas_call x6, Pallas kernels: 45 us -> 28.4 us  [run_group(): pl.pallas_call(functools.partial(group_kernel, first, count, (homes[0], h...]
    ppermute x14, starting transfers between devices: 38.9 us -> 54.7 us  [swapped(): return lax.ppermute(array, AXES, pairs)]
    ppermute x14, starting transfers between devices: 29.9 us -> 42.3 us  [shifted(): return lax.ppermute(array, axis, pairs)]
    unnamed x73 -> x89, local copies, waits for them, and re-layouts: 18.8 us -> 28 us
    slice x6 -> x4, local copies, waits for them, and re-layouts: 11.2 us -> 6.2 us  [the longest x3 3.84 us: shards(): part = rest[:, :, LANE * a:LANE * b]]
    ppermute x14, waiting for transfers between devices: 23.5 us -> 26.8 us  [swapped(): return lax.ppermute(array, AXES, pairs)]
    ppermute x1 -> x0, starting transfers between devices: 2.77 us -> none  [shifted_both(): return lax.ppermute(array, AXES, pairs)]
  transfers between devices with their start and end apart: 29 -> 28, of which waited for: 13 -> 13; matrix products, arithmetic and copies ran while one was open for 8% -> 4% of each run, Pallas kernels for 23% -> 14%
where the time goes in v4:
time: 236 us; the launch traced here: 234 us
  starting transfers between devices  96.9 us (41%)
  waiting for transfers between devices  56.6 us (24%)
  local copies, waits for them, and re-layouts  37.6 us (16%)
  Pallas kernels  33.7 us (14%)
  other arithmetic  6.34 us (3%)
  between operations  2.38 us (1%)
    ppermute x14, starting transfers between devices, swapped(): return lax.ppermute(array, AXES, pairs)  54.7 us
    ppermute x14, starting transfers between devices, shifted(): return lax.ppermute(array, axis, pairs)  42.3 us
    ppermute x14, waiting for transfers between devices, shifted(): return lax.ppermute(array, axis, pairs)  29.8 us
    pallas_call x6, Pallas kernels, run_group(): pl.pallas_call(functools.partial(group_kernel, first, count, (homes[0], h...  28.4 us
    unnamed x89, local copies, waits for them, and re-layouts  28 us
    ppermute x14, waiting for transfers between devices, swapped(): return lax.ppermute(array, AXES, pairs)  26.8 us
    pallas_call x2, Pallas kernels, finish(): pl.pallas_call(functools.partial(finish_kernel, tuple(blocks), terms), ou...  5.28 us
  transfers between devices with their start and end apart: 28, of which 13 were waited for; matrix products, arithmetic and copies ran while one was open for 4% of the time, Pallas kernels for 14%

profile of v4, /device:TPU:1, one launch (start us, length us, event | category | flops | bytes accessed | tf_op | source)
XLA Modules:
  0.0 233.5 jit_solution(7386760774396758483)
XLA Ops:
  0.6 2.4 %slice.27 = f32[2,256,512]{2,1,0:T(8,128)} slice(f32[2,256,2048]{2,1,0:T(8,128)} %refs_0_.11), slice={[0:2], [0:256], [0:512]} | slice | bytes 2097152 | tf_op jit(solution)/shard_map/slice | solution.py:400
  3.0 1.3 collective-permute-start
  4.3 3.1 %fusion.1 = (f32[2,256,384]{2,1,0:T(8,128)}, f32[2,256,384]{2,1,0:T(8,128)}, f32[2,256,384]{2,1,0:T(8,128)}) fusion(f32[2,256,2048]{2,1,0:T(8,128)} %refs_0_.11), kind=kLoop, calls=%fused_computation.21 | loop fusion | bytes 4718592 | tf_op jit(solution)/shard_map/slice | solution.py:403
  7.4 1.4 collective-permute-start.6
  8.8 1.3 collective-permute-start.4
  10.2 1.6 reshape.17
  11.9 1.5 copy.13
  14.5 15.0 %collective-permute-done.refs_1_ = f32[2,256,512]{2,1,0:T(8,128)S(1)} collective-permute-done((f32[2,256,512]{2,1,0:T(8,128)}, f32[2,256,512]{2,1,0:T(8,128)S(1)}, u32[]{:S(2)}, u32[]{:S(2)}) %collective-permute-start) | collective-permute-done | bytes 1048608 | tf_op jit(solution)/shard_map/halo_0/ppermute | solution.py:337
  30.6 5.0 %collective-permute-start.3 = (f32[2,512,256]{2,1,0:T(8,128)S(1)}, f32[2,512,256]{2,1,0:T(8,128)S(1)}, u32[]{:S(2)}, u32[]{:S(2)}) collective-permute-start(f32[2,512,256]{2,1,0:T(8,128)S(1)} %pad_maximum_fusion), channel_id=1, source_target_pairs={{1,0},{2,1},{3,2},{5,4},{6,5},{7,6},{9,8},{10,9},{11,10},{13,12},{... | collective-permute-start | bytes 3145736 | tf_op jit(solution)/shard_map/corner/ppermute | solution.py:337
  35.8 2.2 copy-done.2
  39.2 5.5 %group_0.1 = (f32[2,2,256,128]{3,2,1,0:T(8,128)S(1)}, f32[2,2,256,128]{3,2,1,0:T(8,128)S(1)}, f32[2,2,512,128]{3,2,1,0:T(8,128)S(1)}, f32[2,2,256,256]{3,2,1,0:T(8,128)S(1)}) custom-call(s32[1]{0:T(128)S(6)} %copy.15.live, s32[16,2]{1,0:T(8,128)S(1)} %broadcast_subtract_fusion.off, f32[2,256,2048]{2,1,0:T(8,128)S(1)} %copy-done, ...), custom_call_target="tpu_custom_call" | custom-call | flops 4294967296 | bytes 4096 | tf_op jit(solution)/shard_map/group_0/pallas_call | solution.py:264
  46.5 6.4 %group_2.1 = (f32[2,3,256,128]{3,2,1,0:T(8,128)S(1)}, f32[2,3,256,128]{3,2,1,0:T(8,128)S(1)}, f32[2,2,512,128]{3,2,1,0:T(8,128)S(1)}, f32[2,2,256,256]{3,2,1,0:T(8,128)S(1)}) custom-call(s32[1]{0:T(128)S(6)} %copy.15.live, s32[16,2]{1,0:T(8,128)S(1)} %broadcast_subtract_fusion.off, f32[2,256,2048]{2,1,0:T(8,128)S(1)} %copy-done, ...), custom_call_target="tpu_custom_call" | custom-call | flops 4294967296 | bytes 4096 | tf_op jit(solution)/shard_map/group_2/pallas_call | solution.py:264
  52.9 1.3 collective-permute-start.7
  54.3 1.3 collective-permute-start.5
  55.6 1.3 collective-permute-start.1
  56.9 6.5 %collective-permute-done.4.refs_2_.refs_1_ = f32[2,256,384]{2,1,0:T(8,128)} collective-permute-done((f32[2,256,384]{2,1,0:T(8,128)}, f32[2,256,384]{2,1,0:T(8,128)}, u32[]{:S(2)}, u32[]{:S(2)}) %collective-permute-start.4) | collective-permute-done | bytes 786464 | tf_op jit(solution)/shard_map/halo_2/ppermute | solution.py:337
  63.3 2.1 group_5.1
  65.5 7.5 %collective-permute-start.9 = (f32[2,3,256,128]{3,2,1,0:T(8,128)}, f32[2,3,256,128]{3,2,1,0:T(8,128)}, u32[]{:S(2)}, u32[]{:S(2)}) collective-permute-start(f32[2,3,256,128]{3,2,1,0:T(8,128)} %get-tuple-element.51), channel_id=1, source_target_pairs={{0,4},{4,8},{8,12},{12,16},{16,20},{20,24},{24,28},{28,32},{32,36}... | collective-permute-start | bytes 2359304 | tf_op jit(solution)/shard_map/grad_2/ppermute | solution.py:337
  73.0 1.5 collective-permute-done.5.refs_2_.refs_1_
  74.5 4.9 %group_8.1 = (f32[2,2,256,128]{3,2,1,0:T(8,128)S(1)}, f32[2,2,256,128]{3,2,1,0:T(8,128)}, f32[2,2,512,128]{3,2,1,0:T(8,128)S(1)}, f32[2,2,256,256]{3,2,1,0:T(8,128)S(1)}) custom-call(s32[1]{0:T(128)S(6)} %copy.15.live, s32[16,2]{1,0:T(8,128)S(1)} %broadcast_subtract_fusion.off, f32[2,256,2048]{2,1,0:T(8,128)S(1)} %copy-done, ...), custom_call_target="tpu_custom_call" | custom-call | flops 4294967296 | bytes 4096 | tf_op jit(solution)/shard_map/group_8/pallas_call | solution.py:264
  81.3 1.3 collective-permute-start.8
  83.4 1.3 collective-permute-start.2
  84.7 6.7 %collective-permute-done.1.refs_2_.refs_1_ = f32[2,256,384]{2,1,0:T(8,128)} collective-permute-done((f32[2,256,384]{2,1,0:T(8,128)}, f32[2,256,384]{2,1,0:T(8,128)}, u32[]{:S(2)}, u32[]{:S(2)}) %collective-permute-start.1) | collective-permute-done | bytes 786464 | tf_op jit(solution)/shard_map/halo_4/ppermute | solution.py:337
  91.4 2.2 copy-done.1
  93.6 2.2 copy-done.3
  103.3 5.1 %group_10.1 = (f32[2,3,256,128]{3,2,1,0:T(8,128)S(1)}, f32[2,3,256,128]{3,2,1,0:T(8,128)}, f32[2,2,512,128]{3,2,1,0:T(8,128)S(1)}, f32[2,2,256,256]{3,2,1,0:T(8,128)S(1)}) custom-call(s32[1]{0:T(128)S(6)} %copy.15.live, s32[16,2]{1,0:T(8,128)S(1)} %broadcast_subtract_fusion.off, f32[2,256,2048]{2,1,0:T(8,128)S(1)} %copy-done.1, ...), custom_call_target="tpu_custom_call" | custom-call | flops 4294967296 | bytes 4096 | tf_op jit(solution)/shard_map/group_10/pallas_call | solution.py:264
  109.3 2.2 collective-permute-start.11
  111.5 4.4 %group_13.1 = (f32[2,3,256,128]{3,2,1,0:T(8,128)S(1)}, f32[2,3,256,128]{3,2,1,0:T(8,128)S(1)}, f32[2,2,512,128]{3,2,1,0:T(8,128)S(1)}, f32[2,2,256,256]{3,2,1,0:T(8,128)S(1)}) custom-call(s32[1]{0:T(128)S(6)} %copy.15.live, s32[16,2]{1,0:T(8,128)S(1)} %broadcast_subtract_fusion.off, f32[2,256,2048]{2,1,0:T(8,128)S(1)} %copy-done.1, ...), custom_call_target="tpu_custom_call" | custom-call | flops 4294967296 | bytes 4096 | tf_op jit(solution)/shard_map/group_13/pallas_call | solution.py:264
  119.1 9.1 %collective-permute-start.10 = (f32[512,256]{1,0:T(8,128)S(1)}, f32[512,256]{1,0:T(8,128)S(1)}, u32[]{:S(2)}, u32[]{:S(2)}) collective-permute-start(f32[512,256]{1,0:T(8,128)S(1)} %dynamic-slice_bitcast_fusion), channel_id=1, source_target_pairs={{0,1},{1,0},{2,3},{3,2},{4,5},{5,4},{6,7},{7,6},{8,9},{9,8},{10,11... | collective-permute-start | bytes 1572872 | tf_op jit(solution)/shard_map/swap_c1/ppermute | solution.py:357
  128.2 1.5 collective-permute-done.10
  130.9 2.1 collective-permute-start.12
  133.0 16.3 %collective-permute-start.13 = (f32[128,256]{1,0:T(8,128)S(1)}, f32[128,256]{1,0:T(8,128)S(1)}, u32[]{:S(2)}, u32[]{:S(2)}) collective-permute-start(f32[128,256]{1,0:T(8,128)S(1)} %get-tuple-element.88), channel_id=1, source_target_pairs={{0,64},{1,65},{2,66},{3,67},{4,68},{5,69},{6,70},{7,71},{8,72},{9,... | collective-permute-start | bytes 393224 | tf_op jit(solution)/shard_map/swap_y2/ppermute | solution.py:357
  149.2 13.0 %collective-permute-start.18 = (f32[2,3,256,128]{3,2,1,0:T(8,128)}, f32[2,3,256,128]{3,2,1,0:T(8,128)S(1)}, u32[]{:S(2)}, u32[]{:S(2)}) collective-permute-start(f32[2,3,256,128]{3,2,1,0:T(8,128)} %copy-done.41), channel_id=1, source_target_pairs={{0,4},{4,8},{8,12},{12,16},{16,20},{20,24},{24,28},{28,32},{32,36}... | collective-permute-start | bytes 2359304 | tf_op jit(solution)/shard_map/grad_5/ppermute | solution.py:337
  162.4 1.9 collective-permute-start.22
  164.3 16.0 %collective-permute-start.15 = (f32[128,256]{1,0:T(8,128)S(1)}, f32[128,256]{1,0:T(8,128)S(1)}, u32[]{:S(2)}, u32[]{:S(2)}) collective-permute-start(f32[128,256]{1,0:T(8,128)S(1)} %fusion), channel_id=1, source_target_pairs={{0,16},{1,17},{2,18},{3,19},{4,20},{5,21},{6,22},{7,23},{8,24},{9,... | collective-permute-start | bytes 393224 | tf_op jit(solution)/shard_map/swap_z1/ppermute | solution.py:357
  180.3 2.5 %collective-permute-start.17 = (f32[128,256]{1,0:T(8,128)S(1)}, f32[128,256]{1,0:T(8,128)S(1)}, u32[]{:S(2)}, u32[]{:S(2)}) collective-permute-start(f32[128,256]{1,0:T(8,128)S(1)} %fusion), channel_id=1, source_target_pairs={{0,48},{1,49},{2,50},{3,51},{4,52},{5,53},{6,54},{7,55},{8,56},{9,... | collective-permute-start | bytes 393224 | tf_op jit(solution)/shard_map/swap_z3/ppermute | solution.py:357
  186.1 3.1 %finish_2.1.refs_5_ = f32[2,256,2048]{2,1,0:T(8,128)} custom-call(f32[2,3,256,128]{3,2,1,0:T(8,128)S(1)} %copy-done.8, f32[2,3,256,128]{3,2,1,0:T(8,128)S(1)} %collective-permute-done.7.refs_4_.refs_1_, f32[2,3,256,128]{3,2,1,0:T(8,128)S(1)} %copy-done.10, f32[2,3,256,128]{3,2,1,0:T(8,128)} %collective-permute-done.9.refs_3_, ...), custom_call_target="tpu_custom_call" | custom-call | tf_op jit(solution)/shard_map/finish_2/pallas_call | solution.py:318
  189.2 10.4 %collective-permute-done.15 = f32[128,256]{1,0:T(8,128)S(1)} collective-permute-done((f32[128,256]{1,0:T(8,128)S(1)}, f32[128,256]{1,0:T(8,128)S(1)}, u32[]{:S(2)}, u32[]{:S(2)}) %collective-permute-start.15) | collective-permute-done | bytes 131104 | tf_op jit(solution)/shard_map/swap_z1/ppermute | solution.py:357
  199.6 2.8 %collective-permute-done.16 = f32[128,256]{1,0:T(8,128)S(1)} collective-permute-done((f32[128,256]{1,0:T(8,128)S(1)}, f32[128,256]{1,0:T(8,128)S(1)}, u32[]{:S(2)}, u32[]{:S(2)}) %collective-permute-start.16) | collective-permute-done | bytes 131104 | tf_op jit(solution)/shard_map/swap_z2/ppermute | solution.py:357
  203.4 3.9 %collective-permute-start.21 = (f32[128,256]{1,0:T(8,128)S(1)}, f32[128,256]{1,0:T(8,128)S(1)}, u32[]{:S(2)}, u32[]{:S(2)}) collective-permute-start(f32[128,256]{1,0:T(8,128)S(1)} %add_add_fusion), channel_id=1, source_target_pairs={{0,12},{1,13},{2,14},{3,15},{4,8},{5,9},{6,10},{7,11},{8,4},{9,5},... | collective-permute-start | bytes 393224 | tf_op jit(solution)/shard_map/swap_x3/ppermute | solution.py:357
  208.0 1.5 collective-permute-done.20
  209.5 3.7 %collective-permute-done.21 = f32[128,256]{1,0:T(8,128)S(1)} collective-permute-done((f32[128,256]{1,0:T(8,128)S(1)}, f32[128,256]{1,0:T(8,128)S(1)}, u32[]{:S(2)}, u32[]{:S(2)}) %collective-permute-start.21) | collective-permute-done | bytes 131104 | tf_op jit(solution)/shard_map/swap_x3/ppermute | solution.py:357
  214.0 2.1 collective-permute-start.26
  216.1 1.5 collective-permute-start.24
  217.6 2.4 %collective-permute-start.25 = (f32[128,256]{1,0:T(8,128)S(1)}, f32[128,256]{1,0:T(8,128)}, u32[]{:S(2)}, u32[]{:S(2)}) collective-permute-start(f32[128,256]{1,0:T(8,128)S(1)} %add_multiply_fusion), channel_id=1, source_target_pairs={{0,66},{1,67},{2,64},{3,65},{4,70},{5,71},{6,68},{7,69},{8,74},{9,... | collective-permute-start | bytes 393224 | tf_op jit(solution)/shard_map/swap_y3/ppermute | solution.py:357
  220.0 3.5 %collective-permute-done.24 = f32[128,256]{1,0:T(8,128)S(1)} collective-permute-done((f32[128,256]{1,0:T(8,128)S(1)}, f32[128,256]{1,0:T(8,128)S(1)}, u32[]{:S(2)}, u32[]{:S(2)}) %collective-permute-start.24) | collective-permute-done | bytes 131104 | tf_op jit(solution)/shard_map/swap_y2/ppermute | solution.py:357
  223.5 2.7 %collective-permute-done.25 = f32[128,256]{1,0:T(8,128)} collective-permute-done((f32[128,256]{1,0:T(8,128)S(1)}, f32[128,256]{1,0:T(8,128)}, u32[]{:S(2)}, u32[]{:S(2)}) %collective-permute-start.25) | collective-permute-done | bytes 131104 | tf_op jit(solution)/shard_map/swap_y3/ppermute | solution.py:357
  229.0 2.2 finish_0.1
  (130 shorter events, 30.8 us)
Async XLA Ops:
  0.6 9.5 %copy-start.43 = (s32[16,2]{0,1:T(2,128)S(1)}, s32[16,2]{0,1:T(2,128)}, u32[]{:S(2)}) copy-start(s32[16,2]{0,1:T(2,128)} %param.12) | copy-start | bytes 388
  0.6 9.6 %copy-start.42 = (f32[2,2,256,256]{3,2,1,0:T(8,128)S(1)}, f32[2,2,256,256]{3,2,1,0:T(8,128)}, u32[]{:S(2)}) copy-start(f32[2,2,256,256]{3,2,1,0:T(8,128)} %param.10) | copy-start | bytes 3145732
  3.0 26.5 %collective-permute-start = (f32[2,256,512]{2,1,0:T(8,128)}, f32[2,256,512]{2,1,0:T(8,128)S(1)}, u32[]{:S(2)}, u32[]{:S(2)}) collective-permute-start(f32[2,256,512]{2,1,0:T(8,128)} %slice.27), channel_id=1, source_target_pairs={{4,0},{8,4},{12,8},{16,12},{20,16},{24,20},{28,24},{32,28},{36,32}... | collective-permute-start | bytes 3145736 | tf_op jit(solution)/shard_map/halo_0/ppermute | solution.py:337
  7.4 23.1 %slice-start = ((f32[2,256,2048]{2,1,0:T(8,128)}), f32[2,256,256]{2,1,0:T(8,128)S(1)}, s32[]{:S(2)}) async-start(f32[2,256,2048]{2,1,0:T(8,128)} %refs_0_.11), calls=%async_computation | async-start | bytes 1048576 | tf_op jit(solution)/shard_map/slice | solution.py:405
  7.4 39.1 %collective-permute-start.6 = (f32[2,256,384]{2,1,0:T(8,128)}, f32[2,256,384]{2,1,0:T(8,128)}, u32[]{:S(2)}, u32[]{:S(2)}) collective-permute-start(f32[2,256,384]{2,1,0:T(8,128)} %get-tuple-element.78), channel_id=1, source_target_pairs={{4,0},{8,4},{12,8},{16,12},{20,16},{24,20},{28,24},{32,28},{36,32}... | collective-permute-start | bytes 2359304 | tf_op jit(solution)/shard_map/halo_1/ppermute | solution.py:337
  8.8 54.6 %collective-permute-start.4 = (f32[2,256,384]{2,1,0:T(8,128)}, f32[2,256,384]{2,1,0:T(8,128)}, u32[]{:S(2)}, u32[]{:S(2)}) collective-permute-start(f32[2,256,384]{2,1,0:T(8,128)} %get-tuple-element.79), channel_id=1, source_target_pairs={{4,0},{8,4},{12,8},{16,12},{20,16},{24,20},{28,24},{32,28},{36,32}... | collective-permute-start | bytes 2359304 | tf_op jit(solution)/shard_map/halo_2/ppermute | solution.py:337
  11.8 23.9 %copy-start = (f32[2,256,2048]{2,1,0:T(8,128)S(1)}, f32[2,256,2048]{2,1,0:T(8,128)}, u32[]{:S(2)}) copy-start(f32[2,256,2048]{2,1,0:T(8,128)} %refs_0_.11) | copy-start | bytes 12582916
  11.8 23.9 %copy-start.23 = (bf16[512,512]{1,0:T(8,128)(2,1)S(1)}, bf16[512,512]{1,0:T(8,128)(2,1)}, u32[]{:S(2)}) copy-start(bf16[512,512]{1,0:T(8,128)(2,1)} %constant.82.clone.refs_5_.refs_6_.refs_8_.refs_7_) | copy-start | bytes 1572868
  11.8 23.9 %copy-start.25 = (bf16[512,512]{1,0:T(8,128)(2,1)S(1)}, bf16[512,512]{1,0:T(8,128)(2,1)}, u32[]{:S(2)}) copy-start(bf16[512,512]{1,0:T(8,128)(2,1)} %constant.84.clone.refs_7_.refs_8_.refs_10_.refs_9_) | copy-start | bytes 1572868
  11.8 23.9 %copy-start.29 = (bf16[2,256,256]{2,1,0:T(8,128)(2,1)S(1)}, bf16[2,256,256]{2,1,0:T(8,128)(2,1)}, u32[]{:S(2)}) copy-start(bf16[2,256,256]{2,1,0:T(8,128)(2,1)} %constant.81.clone.refs_4_.refs_5_.refs_7_.refs_6_) | copy-start | bytes 786436
  11.8 23.9 %copy-start.32 = (bf16[2,256,256]{2,1,0:T(8,128)(2,1)S(1)}, bf16[2,256,256]{2,1,0:T(8,128)(2,1)}, u32[]{:S(2)}) copy-start(bf16[2,256,256]{2,1,0:T(8,128)(2,1)} %constant.83.clone.refs_6_.refs_7_.refs_9_.refs_8_) | copy-start | bytes 786436
  30.6 43.9 %collective-permute-start.3 = (f32[2,512,256]{2,1,0:T(8,128)S(1)}, f32[2,512,256]{2,1,0:T(8,128)S(1)}, u32[]{:S(2)}, u32[]{:S(2)}) collective-permute-start(f32[2,512,256]{2,1,0:T(8,128)S(1)} %pad_maximum_fusion), channel_id=1, source_target_pairs={{1,0},{2,1},{3,2},{5,4},{6,5},{7,6},{9,8},{10,9},{11,10},{13,12},{... | collective-permute-start | bytes 3145736 | tf_op jit(solution)/shard_map/corner/ppermute | solution.py:337
  35.8 2.2 copy-start.2
  52.9 10.5 %copy-start.7 = (f32[2,3,256,128]{3,2,1,0:T(8,128)}, f32[2,3,256,128]{3,2,1,0:T(8,128)S(1)}, u32[]{:S(2)}) copy-start(f32[2,3,256,128]{3,2,1,0:T(8,128)S(1)} %get-tuple-element.63.refs_0_) | copy-start | bytes 2359300
  52.9 21.6 %collective-permute-start.7 = (f32[2,3,256,128]{3,2,1,0:T(8,128)S(1)}, f32[2,3,256,128]{3,2,1,0:T(8,128)S(1)}, u32[]{:S(2)}, u32[]{:S(2)}) collective-permute-start(f32[2,3,256,128]{3,2,1,0:T(8,128)S(1)} %get-tuple-element.45), channel_id=1, source_target_pairs={{0,4},{4,8},{8,12},{12,16},{16,20},{20,24},{24,28},{28,32},{32,36}... | collective-permute-start | bytes 2359304 | tf_op jit(solution)/shard_map/grad_1/ppermute | solution.py:337
  54.3 20.2 %collective-permute-start.5 = (f32[2,256,256]{2,1,0:T(8,128)S(1)}, f32[2,256,256]{2,1,0:T(8,128)S(1)}, u32[]{:S(2)}, u32[]{:S(2)}) collective-permute-start(f32[2,256,256]{2,1,0:T(8,128)S(1)} %slice.33), channel_id=1, source_target_pairs={{4,0},{8,4},{12,8},{16,12},{20,16},{24,20},{28,24},{32,28},{36,32}... | collective-permute-start | bytes 1572872 | tf_op jit(solution)/shard_map/halo_3/ppermute | solution.py:337
  55.6 35.9 %collective-permute-start.1 = (f32[2,256,384]{2,1,0:T(8,128)}, f32[2,256,384]{2,1,0:T(8,128)}, u32[]{:S(2)}, u32[]{:S(2)}) collective-permute-start(f32[2,256,384]{2,1,0:T(8,128)} %get-tuple-element.80), channel_id=1, source_target_pairs={{4,0},{8,4},{12,8},{16,12},{20,16},{24,20},{28,24},{32,28},{36,32}... | collective-permute-start | bytes 2359304 | tf_op jit(solution)/shard_map/halo_4/ppermute | solution.py:337
  65.5 13.9 %copy-start.9 = (f32[2,3,256,128]{3,2,1,0:T(8,128)}, f32[2,3,256,128]{3,2,1,0:T(8,128)S(1)}, u32[]{:S(2)}) copy-start(f32[2,3,256,128]{3,2,1,0:T(8,128)S(1)} %get-tuple-element.64.refs_2_) | copy-start | bytes 2359300
  65.5 25.9 %collective-permute-start.9 = (f32[2,3,256,128]{3,2,1,0:T(8,128)}, f32[2,3,256,128]{3,2,1,0:T(8,128)}, u32[]{:S(2)}, u32[]{:S(2)}) collective-permute-start(f32[2,3,256,128]{3,2,1,0:T(8,128)} %get-tuple-element.51), channel_id=1, source_target_pairs={{0,4},{4,8},{8,12},{12,16},{16,20},{20,24},{24,28},{28,32},{32,36}... | collective-permute-start | bytes 2359304 | tf_op jit(solution)/shard_map/grad_2/ppermute | solution.py:337
  74.5 4.9 %copy-start.27 = (f32[2,256,256]{2,1,0:T(8,128)}, f32[2,256,256]{2,1,0:T(8,128)S(1)}, u32[]{:S(2)}) copy-start(f32[2,256,256]{2,1,0:T(8,128)S(1)} %collective-permute-done.5.refs_2_.refs_1_) | copy-start | bytes 1572868
  81.3 30.2 %collective-permute-start.8 = (f32[2,2,256,128]{3,2,1,0:T(8,128)}, f32[2,2,256,128]{3,2,1,0:T(8,128)S(1)}, u32[]{:S(2)}, u32[]{:S(2)}) collective-permute-start(f32[2,2,256,128]{3,2,1,0:T(8,128)} %get-tuple-element.50), channel_id=1, source_target_pairs={{0,4},{4,8},{8,12},{12,16},{16,20},{20,24},{24,28},{28,32},{32,36}... | collective-permute-start | bytes 1572872 | tf_op jit(solution)/shard_map/grad_3/ppermute | solution.py:337
  83.4 28.1 %collective-permute-start.2 = (f32[2,256,128]{2,1,0:T(8,128)}, f32[2,256,128]{2,1,0:T(8,128)}, u32[]{:S(2)}, u32[]{:S(2)}) collective-permute-start(f32[2,256,128]{2,1,0:T(8,128)} %slice.29), channel_id=1, source_target_pairs={{4,0},{8,4},{12,8},{16,12},{20,16},{24,20},{28,24},{32,28},{36,32}... | collective-permute-start | bytes 786440 | tf_op jit(solution)/shard_map/halo_5/ppermute | solution.py:337
  103.3 8.3 %copy-start.31 = (bf16[2,256,256]{2,1,0:T(8,128)(2,1)S(1)}, bf16[2,256,256]{2,1,0:T(8,128)(2,1)}, u32[]{:S(2)}) copy-start(bf16[2,256,256]{2,1,0:T(8,128)(2,1)} %constant.81.clone.refs_4_.refs_5_.refs_7_.refs_6_) | copy-start | bytes 786436
  109.3 21.5 %collective-permute-start.11 = (f32[2,3,256,128]{3,2,1,0:T(8,128)}, f32[2,3,256,128]{3,2,1,0:T(8,128)}, u32[]{:S(2)}, u32[]{:S(2)}) collective-permute-start(f32[2,3,256,128]{3,2,1,0:T(8,128)} %get-tuple-element.57), channel_id=1, source_target_pairs={{0,4},{4,8},{8,12},{12,16},{16,20},{20,24},{24,28},{28,32},{32,36}... | collective-permute-start | bytes 2359304 | tf_op jit(solution)/shard_map/grad_4/ppermute | solution.py:337
  111.5 4.5 %copy-start.21 = (f32[2,2,256,128]{3,2,1,0:T(8,128)}, f32[2,2,256,128]{3,2,1,0:T(8,128)S(1)}, u32[]{:S(2)}) copy-start(f32[2,2,256,128]{3,2,1,0:T(8,128)S(1)} %collective-permute-done.8.refs_4_.refs_5_) | copy-start | bytes 1572868
  117.9 64.9 %copy-start.8 = (f32[2,3,256,128]{3,2,1,0:T(8,128)S(1)}, f32[2,3,256,128]{3,2,1,0:T(8,128)}, u32[]{:S(2)}) copy-start(f32[2,3,256,128]{3,2,1,0:T(8,128)} %copy-done.7) | copy-start | bytes 2359300
  117.9 64.9 %copy-start.20 = (f32[2,2,256,128]{3,2,1,0:T(8,128)S(1)}, f32[2,2,256,128]{3,2,1,0:T(8,128)}, u32[]{:S(2)}) copy-start(f32[2,2,256,128]{3,2,1,0:T(8,128)} %copy-done.19) | copy-start | bytes 1572868
  119.1 10.6 %collective-permute-start.10 = (f32[512,256]{1,0:T(8,128)S(1)}, f32[512,256]{1,0:T(8,128)S(1)}, u32[]{:S(2)}, u32[]{:S(2)}) collective-permute-start(f32[512,256]{1,0:T(8,128)S(1)} %dynamic-slice_bitcast_fusion), channel_id=1, source_target_pairs={{0,1},{1,0},{2,3},{3,2},{4,5},{5,4},{6,7},{7,6},{8,9},{9,8},{10,11... | collective-permute-start | bytes 1572872 | tf_op jit(solution)/shard_map/swap_c1/ppermute | solution.py:357
  130.9 31.4 %collective-permute-start.12 = (f32[128,256]{1,0:T(8,128)S(1)}, f32[128,256]{1,0:T(8,128)S(1)}, u32[]{:S(2)}, u32[]{:S(2)}) collective-permute-start(f32[128,256]{1,0:T(8,128)S(1)} %get-tuple-element.89), channel_id=1, source_target_pairs={{0,2},{1,3},{2,0},{3,1},{4,6},{5,7},{6,4},{7,5},{8,10},{9,11},{10,... | collective-permute-start | bytes 393224 | tf_op jit(solution)/shard_map/swap_y1/ppermute | solution.py:357
  133.0 29.3 %collective-permute-start.13 = (f32[128,256]{1,0:T(8,128)S(1)}, f32[128,256]{1,0:T(8,128)S(1)}, u32[]{:S(2)}, u32[]{:S(2)}) collective-permute-start(f32[128,256]{1,0:T(8,128)S(1)} %get-tuple-element.88), channel_id=1, source_target_pairs={{0,64},{1,65},{2,66},{3,67},{4,68},{5,69},{6,70},{7,71},{8,72},{9,... | collective-permute-start | bytes 393224 | tf_op jit(solution)/shard_map/swap_y2/ppermute | solution.py:357
  149.2 13.1 %collective-permute-start.14 = (f32[128,256]{1,0:T(8,128)S(1)}, f32[128,256]{1,0:T(8,128)S(1)}, u32[]{:S(2)}, u32[]{:S(2)}) collective-permute-start(f32[128,256]{1,0:T(8,128)S(1)} %get-tuple-element.87), channel_id=1, source_target_pairs={{0,66},{1,67},{2,64},{3,65},{4,70},{5,71},{6,68},{7,69},{8,74},{9,... | collective-permute-start | bytes 393224 | tf_op jit(solution)/shard_map/swap_y3/ppermute | solution.py:357
  149.2 53.2 %collective-permute-start.18 = (f32[2,3,256,128]{3,2,1,0:T(8,128)}, f32[2,3,256,128]{3,2,1,0:T(8,128)S(1)}, u32[]{:S(2)}, u32[]{:S(2)}) collective-permute-start(f32[2,3,256,128]{3,2,1,0:T(8,128)} %copy-done.41), channel_id=1, source_target_pairs={{0,4},{4,8},{8,12},{12,16},{16,20},{20,24},{24,28},{28,32},{32,36}... | collective-permute-start | bytes 2359304 | tf_op jit(solution)/shard_map/grad_5/ppermute | solution.py:337
  162.4 50.8 %collective-permute-start.22 = (f32[2,2,512,128]{3,2,1,0:T(8,128)}, f32[2,2,512,128]{3,2,1,0:T(8,128)S(1)}, u32[]{:S(2)}, u32[]{:S(2)}) collective-permute-start(f32[2,2,512,128]{3,2,1,0:T(8,128)} %copy-done.36), channel_id=1, source_target_pairs={{0,1},{1,2},{2,3},{4,5},{5,6},{6,7},{8,9},{9,10},{10,11},{12,13},{... | collective-permute-start | bytes 3145736 | tf_op jit(solution)/shard_map/over/ppermute | solution.py:337
  164.3 35.3 %collective-permute-start.15 = (f32[128,256]{1,0:T(8,128)S(1)}, f32[128,256]{1,0:T(8,128)S(1)}, u32[]{:S(2)}, u32[]{:S(2)}) collective-permute-start(f32[128,256]{1,0:T(8,128)S(1)} %fusion), channel_id=1, source_target_pairs={{0,16},{1,17},{2,18},{3,19},{4,20},{5,21},{6,22},{7,23},{8,24},{9,... | collective-permute-start | bytes 393224 | tf_op jit(solution)/shard_map/swap_z1/ppermute | solution.py:357
  180.3 22.1 %collective-permute-start.16 = (f32[128,256]{1,0:T(8,128)S(1)}, f32[128,256]{1,0:T(8,128)S(1)}, u32[]{:S(2)}, u32[]{:S(2)}) collective-permute-start(f32[128,256]{1,0:T(8,128)S(1)} %fusion), channel_id=1, source_target_pairs={{0,32},{1,33},{2,34},{3,35},{4,36},{5,37},{6,38},{7,39},{8,40},{9,... | collective-permute-start | bytes 393224 | tf_op jit(solution)/shard_map/swap_z2/ppermute | solution.py:357
  180.3 22.1 %collective-permute-start.17 = (f32[128,256]{1,0:T(8,128)S(1)}, f32[128,256]{1,0:T(8,128)S(1)}, u32[]{:S(2)}, u32[]{:S(2)}) collective-permute-start(f32[128,256]{1,0:T(8,128)S(1)} %fusion), channel_id=1, source_target_pairs={{0,48},{1,49},{2,50},{3,51},{4,52},{5,53},{6,54},{7,55},{8,56},{9,... | collective-permute-start | bytes 393224 | tf_op jit(solution)/shard_map/swap_z3/ppermute | solution.py:357
  186.1 27.1 %copy-start.18 = (f32[2,2,256,128]{3,2,1,0:T(8,128)S(1)}, f32[2,2,256,128]{3,2,1,0:T(8,128)}, u32[]{:S(2)}) copy-start(f32[2,2,256,128]{3,2,1,0:T(8,128)} %copy-done.17) | copy-start | bytes 1572868
  189.2 39.8 %copy-start.6 = (f32[2,3,256,128]{3,2,1,0:T(8,128)S(1)}, f32[2,3,256,128]{3,2,1,0:T(8,128)}, u32[]{:S(2)}) copy-start(f32[2,3,256,128]{3,2,1,0:T(8,128)} %copy-done.5) | copy-start | bytes 2359300
  189.2 39.8 %copy-start.16 = (f32[2,2,256,128]{3,2,1,0:T(8,128)S(1)}, f32[2,2,256,128]{3,2,1,0:T(8,128)}, u32[]{:S(2)}) copy-start(f32[2,2,256,128]{3,2,1,0:T(8,128)} %copy-done.15) | copy-start | bytes 1572868
  203.4 4.6 %collective-permute-start.19 = (f32[128,256]{1,0:T(8,128)S(1)}, f32[128,256]{1,0:T(8,128)S(1)}, u32[]{:S(2)}, u32[]{:S(2)}) collective-permute-start(f32[128,256]{1,0:T(8,128)S(1)} %add_add_fusion), channel_id=1, source_target_pairs={{0,4},{1,5},{2,6},{3,7},{4,0},{5,1},{6,2},{7,3},{8,12},{9,13},{10,... | collective-permute-start | bytes 393224 | tf_op jit(solution)/shard_map/swap_x1/ppermute | solution.py:357
  203.4 25.6 %copy-start.14 = (f32[2,3,256,128]{3,2,1,0:T(8,128)S(1)}, f32[2,3,256,128]{3,2,1,0:T(8,128)}, u32[]{:S(2)}) copy-start(f32[2,3,256,128]{3,2,1,0:T(8,128)} %copy-done.13) | copy-start | bytes 2359300
  203.4 6.1 %collective-permute-start.20 = (f32[128,256]{1,0:T(8,128)S(1)}, f32[128,256]{1,0:T(8,128)S(1)}, u32[]{:S(2)}, u32[]{:S(2)}) collective-permute-start(f32[128,256]{1,0:T(8,128)S(1)} %add_add_fusion), channel_id=1, source_target_pairs={{0,8},{1,9},{2,10},{3,11},{4,12},{5,13},{6,14},{7,15},{8,0},{9,1},... | collective-permute-start | bytes 393224 | tf_op jit(solution)/shard_map/swap_x2/ppermute | solution.py:357
  203.4 9.7 %collective-permute-start.21 = (f32[128,256]{1,0:T(8,128)S(1)}, f32[128,256]{1,0:T(8,128)S(1)}, u32[]{:S(2)}, u32[]{:S(2)}) collective-permute-start(f32[128,256]{1,0:T(8,128)S(1)} %add_add_fusion), channel_id=1, source_target_pairs={{0,12},{1,13},{2,14},{3,15},{4,8},{5,9},{6,10},{7,11},{8,4},{9,5},... | collective-permute-start | bytes 393224 | tf_op jit(solution)/shard_map/swap_x3/ppermute | solution.py:357
  214.0 14.0 %collective-permute-start.26 = (f32[2,2,256,128]{3,2,1,0:T(8,128)}, f32[2,2,256,128]{3,2,1,0:T(8,128)}, u32[]{:S(2)}, u32[]{:S(2)}) collective-permute-start(f32[2,2,256,128]{3,2,1,0:T(8,128)} %slice_add_fusion), channel_id=1, source_target_pairs={{0,4},{4,8},{8,12},{12,16},{16,20},{20,24},{24,28},{28,32},{32,36}... | collective-permute-start | bytes 1572872 | tf_op jit(solution)/shard_map/grad_0/ppermute | solution.py:337
  216.1 3.9 %collective-permute-start.23 = (f32[128,256]{1,0:T(8,128)S(1)}, f32[128,256]{1,0:T(8,128)S(1)}, u32[]{:S(2)}, u32[]{:S(2)}) collective-permute-start(f32[128,256]{1,0:T(8,128)S(1)} %add_multiply_fusion), channel_id=1, source_target_pairs={{0,2},{1,3},{2,0},{3,1},{4,6},{5,7},{6,4},{7,5},{8,10},{9,11},{10,... | collective-permute-start | bytes 393224 | tf_op jit(solution)/shard_map/swap_y1/ppermute | solution.py:357
  216.1 7.4 %collective-permute-start.24 = (f32[128,256]{1,0:T(8,128)S(1)}, f32[128,256]{1,0:T(8,128)S(1)}, u32[]{:S(2)}, u32[]{:S(2)}) collective-permute-start(f32[128,256]{1,0:T(8,128)S(1)} %add_multiply_fusion), channel_id=1, source_target_pairs={{0,64},{1,65},{2,66},{3,67},{4,68},{5,69},{6,70},{7,71},{8,72},{9,... | collective-permute-start | bytes 393224 | tf_op jit(solution)/shard_map/swap_y2/ppermute | solution.py:357
  217.6 8.6 %collective-permute-start.25 = (f32[128,256]{1,0:T(8,128)S(1)}, f32[128,256]{1,0:T(8,128)}, u32[]{:S(2)}, u32[]{:S(2)}) collective-permute-start(f32[128,256]{1,0:T(8,128)S(1)} %add_multiply_fusion), channel_id=1, source_target_pairs={{0,66},{1,67},{2,64},{3,65},{4,70},{5,71},{6,68},{7,69},{8,74},{9,... | collective-permute-start | bytes 393224 | tf_op jit(solution)/shard_map/swap_y3/ppermute | solution.py:357
  228.0 3.2 %collective-permute-start.27 = (f32[512,256]{1,0:T(8,128)}, f32[512,256]{1,0:T(8,128)}, u32[]{:S(2)}, u32[]{:S(2)}) collective-permute-start(f32[512,256]{1,0:T(8,128)} %pad_maximum_fusion.2), channel_id=1, source_target_pairs={{0,1},{1,0},{2,3},{3,2},{4,5},{5,4},{6,7},{7,6},{8,9},{9,8},{10,11... | collective-permute-start | bytes 1572872 | tf_op jit(solution)/shard_map/swap_c1/ppermute | solution.py:357
  (25 other events, 28.9 us)

commit v5 on v4

--- a/solution.py
+++ b/solution.py
@@ -232,7 +232,7 @@
 IN_VMEM = pl.BlockSpec(memory_space=pltpu.VMEM)
 
 
-def run_group(first, count, bounds, live, off, field, halos, corner, measured, probe, tabs, carry, acc, after):
+def run_group(first, count, bounds, live, off, field, halos, right, corner, measured, probe, tabs, carry, acc, after):
     wide = count + 2
     arrays, homes = [], [[], []]
 
@@ -251,8 +251,8 @@
             homes[1].append((index_in(halos[chunk]), 0, (b - begin) * LANE))
         else:
             at = (b - bounds[-1]) * LANE
-            homes[0].append((index_in(corner), 0, at))
-            homes[1].append((index_in(corner), SIZE, at))
+            homes[0].append((index_in(right), 0, at))
+            homes[1].append((index_in(corner), 0, at))
     homes.append(arrays)
     args = [live, off, *arrays, *after, measured, probe, *tabs, carry, acc]
     specs = [IN_SMEM] * 2 + [IN_HBM] * (1 + len(arrays) + len(after)) + [IN_VMEM] * 7
@@ -275,7 +275,7 @@
             pltpu.SemaphoreType.DMA((2 * wide,)),
             pltpu.SemaphoreType.DMA((4,)),
         ],
-        compiler_params=pltpu.CompilerParams(vmem_limit_bytes=30 * 2**20),
+        compiler_params=pltpu.CompilerParams(vmem_limit_bytes=44 * 2**20),
         cost_estimate=pl.CostEstimate(flops=2**32, bytes_accessed=2**12, transcendentals=0),
         name=f"group_{first}",
     )(*args)
@@ -402,18 +402,18 @@
     for i, (a, b) in enumerate(zip(BOUNDS[:-1], BOUNDS[1:])):
         part = rest[:, :, LANE * a : LANE * b]
         halos.append(shifted(part, "scan", -1, f"halo_{i + 1}"))
-    beside = jnp.concatenate([field[:, :, :SIZE], halos[0][:, :, :SIZE]], 1)
-    corner = shifted(beside, "mode", -1, "corner")
+    right = shifted(field[:, :, :SIZE], "mode", -1, "right")
+    corner = shifted(halos[0][:, :, :SIZE], "mode", -1, "corner")
     carry = jnp.zeros((2, 2, 2 * SIZE, LANE), f32)
     acc = jnp.zeros(probe.shape, f32)
     ends = [b - 2 for b in BOUNDS[:-1]] + [BOUNDS[-1]]
     plan = [(a, b - a) for a, b in zip([0] + ends[:-1], ends)]
     uppers, lowers, comings = [], [], []
     for i, (first, count) in enumerate(plan):
-        after = {3: (corner, 1), 4: (2,), 5: (3,)}.get(i, ())
+        after = {2: (right,), 3: (1,), 4: (2,), 5: (3,)}.get(i, ())
         after = [comings[j] if isinstance(j, int) else j for j in after]
         upper, lower, carry, acc = run_group(
-            first, count, BOUNDS, live, off, field, halos, corner, measured, probe_rows, tabs, carry, acc, after
+            first, count, BOUNDS, live, off, field, halos, right, corner, measured, probe_rows, tabs, carry, acc, after
         )
         uppers.append(upper)
         lowers.append(lower)

time: 236 us -> 238 us (level)
  starting transfers between devices: 96.9 us -> 109 us
  Pallas kernels: 33.7 us -> 27.6 us
  waiting for transfers between devices: 56.6 us -> 54.1 us
    ppermute x14, starting transfers between devices: 54.7 us -> 65.2 us  [swapped(): return lax.ppermute(array, AXES, pairs)]
    pallas_call x6, Pallas kernels: 28.4 us -> 22.6 us  [run_group(): pl.pallas_call(functools.partial(group_kernel, first, count, (homes[0], h...]
    unnamed x89 -> x85, local copies, waits for them, and re-layouts: 28 us -> 25 us
    slice x3 -> x2, local copies, waits for them, and re-layouts: 0.04 us -> 2.74 us  [the longest x1 1.86 us: shards(): right = shifted(field[:, :, :SIZE], 'mode', -1, 'right')]
    ppermute x14 -> x15, waiting for transfers between devices: 29.8 us -> 27.8 us  [shifted(): return lax.ppermute(array, axis, pairs)]
    ppermute x14 -> x15, starting transfers between devices: 42.3 us -> 43.8 us  [shifted(): return lax.ppermute(array, axis, pairs)]
  transfers between devices with their start and end apart: 28 -> 29, of which waited for: 13 -> 12; matrix products, arithmetic and copies ran while one was open for 4% -> 6% of each run, Pallas kernels for 14% -> 12%
where the time goes in v5:
time: 238 us; the launch traced here: 237 us
  starting transfers between devices  109 us (46%)
  waiting for transfers between devices  54.1 us (23%)
  local copies, waits for them, and re-layouts  37.9 us (16%)
  Pallas kernels  27.6 us (12%)
  other arithmetic  6.95 us (3%)
    ppermute x14, starting transfers between devices, swapped(): return lax.ppermute(array, AXES, pairs)  65.2 us
    ppermute x15, starting transfers between devices, shifted(): return lax.ppermute(array, axis, pairs)  43.8 us
    ppermute x15, waiting for transfers between devices, shifted(): return lax.ppermute(array, axis, pairs)  27.8 us
    ppermute x14, waiting for transfers between devices, swapped(): return lax.ppermute(array, AXES, pairs)  26.3 us
    unnamed x85, local copies, waits for them, and re-layouts  25 us
    pallas_call x6, Pallas kernels, run_group(): pl.pallas_call(functools.partial(group_kernel, first, count, (homes[0], h...  22.6 us
    slice x3, local copies, waits for them, and re-layouts, shards(): part = rest[:, :, LANE * a:LANE * b]  5.83 us
    pallas_call x2, Pallas kernels, finish(): pl.pallas_call(functools.partial(finish_kernel, tuple(blocks), terms), ou...  5.05 us
  transfers between devices with their start and end apart: 29, of which 12 were waited for; matrix products, arithmetic and copies ran while one was open for 6% of the time, Pallas kernels for 12%

profile of v5, /device:TPU:1, one launch (start us, length us, event | category | flops | bytes accessed | tf_op | source)
XLA Modules:
  0.0 237.4 jit_solution(4413709742185630450)
XLA Ops:
  0.6 2.4 slice.27
  3.0 1.3 collective-permute-start
  4.3 3.1 %fusion.1 = (f32[2,256,384]{2,1,0:T(8,128)}, f32[2,256,384]{2,1,0:T(8,128)}, f32[2,256,384]{2,1,0:T(8,128)}) fusion(f32[2,256,2048]{2,1,0:T(8,128)} %refs_0_.11), kind=kLoop, calls=%fused_computation.20 | loop fusion | bytes 4718592 | tf_op jit(solution)/shard_map/slice | solution.py:403
  7.4 1.4 collective-permute-start.7
  8.8 1.3 collective-permute-start.5
  10.1 1.9 slice.30
  11.9 3.3 %collective-permute-start.3 = (f32[2,256,256]{2,1,0:T(8,128)}, f32[2,256,256]{2,1,0:T(8,128)}, u32[]{:S(2)}, u32[]{:S(2)}) collective-permute-start(f32[2,256,256]{2,1,0:T(8,128)} %slice.30), channel_id=1, source_target_pairs={{1,0},{2,1},{3,2},{5,4},{6,5},{7,6},{9,8},{10,9},{11,10},{13,12},{... | collective-permute-start | bytes 1572872 | tf_op jit(solution)/shard_map/right/ppermute | solution.py:337
  16.8 12.7 %collective-permute-done.refs_1_ = f32[2,256,512]{2,1,0:T(8,128)S(1)} collective-permute-done((f32[2,256,512]{2,1,0:T(8,128)}, f32[2,256,512]{2,1,0:T(8,128)S(1)}, u32[]{:S(2)}, u32[]{:S(2)}) %collective-permute-start) | collective-permute-done | bytes 1048608 | tf_op jit(solution)/shard_map/halo_0/ppermute | solution.py:337
  32.7 1.2 group_0.1
  33.9 12.5 %collective-permute-done.7.refs_2_.refs_1_ = f32[2,256,384]{2,1,0:T(8,128)} collective-permute-done((f32[2,256,384]{2,1,0:T(8,128)}, f32[2,256,384]{2,1,0:T(8,128)}, u32[]{:S(2)}, u32[]{:S(2)}) %collective-permute-start.7) | collective-permute-done | bytes 786464 | tf_op jit(solution)/shard_map/halo_1/ppermute | solution.py:337
  46.5 8.4 %group_2.1 = (f32[2,3,256,128]{3,2,1,0:T(8,128)S(1)}, f32[2,3,256,128]{3,2,1,0:T(8,128)S(1)}, f32[2,2,512,128]{3,2,1,0:T(8,128)S(1)}, f32[2,2,256,256]{3,2,1,0:T(8,128)S(1)}) custom-call(s32[1]{0:T(128)S(6)} %copy.15.live, s32[16,2]{1,0:T(8,128)S(1)} %broadcast_subtract_fusion.off, f32[2,256,2048]{2,1,0:T(8,128)} %refs_0_.11, ...), custom_call_target="tpu_custom_call" | custom-call | flops 4294967296 | bytes 4096 | tf_op jit(solution)/shard_map/group_2/pallas_call | solution.py:264
  55.8 1.3 collective-permute-start.8
  58.2 1.3 collective-permute-start.6
  59.5 1.3 collective-permute-start.1
  60.8 2.5 %collective-permute-done.5.refs_2_.refs_1_ = f32[2,256,384]{2,1,0:T(8,128)} collective-permute-done((f32[2,256,384]{2,1,0:T(8,128)}, f32[2,256,384]{2,1,0:T(8,128)}, u32[]{:S(2)}, u32[]{:S(2)}) %collective-permute-start.5) | collective-permute-done | bytes 786464 | tf_op jit(solution)/shard_map/halo_2/ppermute | solution.py:337
  63.3 6.1 %group_5.1 = (f32[2,3,256,128]{3,2,1,0:T(8,128)S(1)}, f32[2,3,256,128]{3,2,1,0:T(8,128)}, f32[2,2,512,128]{3,2,1,0:T(8,128)S(1)}, f32[2,2,256,256]{3,2,1,0:T(8,128)S(1)}) custom-call(s32[1]{0:T(128)S(6)} %copy.15.live, s32[16,2]{1,0:T(8,128)S(1)} %broadcast_subtract_fusion.off, f32[2,256,2048]{2,1,0:T(8,128)} %refs_0_.11, ...), custom_call_target="tpu_custom_call" | custom-call | flops 4294967296 | bytes 4096 | tf_op jit(solution)/shard_map/group_5/pallas_call | solution.py:264
  69.4 3.6 %collective-permute-start.10 = (f32[2,3,256,128]{3,2,1,0:T(8,128)}, f32[2,3,256,128]{3,2,1,0:T(8,128)S(1)}, u32[]{:S(2)}, u32[]{:S(2)}) collective-permute-start(f32[2,3,256,128]{3,2,1,0:T(8,128)} %get-tuple-element.51), channel_id=1, source_target_pairs={{0,4},{4,8},{8,12},{12,16},{16,20},{20,24},{24,28},{28,32},{32,36}... | collective-permute-start | bytes 2359304 | tf_op jit(solution)/shard_map/grad_2/ppermute | solution.py:337
  73.9 8.2 %collective-permute-start.4 = (f32[2,256,256]{2,1,0:T(8,128)}, f32[2,256,256]{2,1,0:T(8,128)}, u32[]{:S(2)}, u32[]{:S(2)}) collective-permute-start(f32[2,256,256]{2,1,0:T(8,128)} %slice.36), channel_id=1, source_target_pairs={{1,0},{2,1},{3,2},{5,4},{6,5},{7,6},{9,8},{10,9},{11,10},{13,12},{... | collective-permute-start | bytes 1572872 | tf_op jit(solution)/shard_map/corner/ppermute | solution.py:337
  82.1 2.0 group_8.1
  86.1 1.6 collective-permute-start.9
  87.7 1.7 slice.29
  89.4 1.3 collective-permute-start.2
  90.7 1.3 copy-done.20
  96.0 1.2 copy-done.37
  97.2 2.9 %group_10.1 = (f32[2,3,256,128]{3,2,1,0:T(8,128)S(1)}, f32[2,3,256,128]{3,2,1,0:T(8,128)}, f32[2,2,512,128]{3,2,1,0:T(8,128)S(1)}, f32[2,2,256,256]{3,2,1,0:T(8,128)S(1)}) custom-call(s32[1]{0:T(128)S(6)} %copy.15.live, s32[16,2]{1,0:T(8,128)S(1)} %broadcast_subtract_fusion.off, f32[2,256,2048]{2,1,0:T(8,128)} %refs_0_.11, f32[2,256,256]{2,1,0:T(8,128)S(1)} %copy-done.20, ...), custom_call_target="tpu_custom_call" | custom-call | flops 4294967296 | bytes 4096 | tf_op jit(solution)/shard_map/group_10/pallas_call | solution.py:264
  101.2 11.8 %collective-permute-start.12 = (f32[2,3,256,128]{3,2,1,0:T(8,128)}, f32[2,3,256,128]{3,2,1,0:T(8,128)}, u32[]{:S(2)}, u32[]{:S(2)}) collective-permute-start(f32[2,3,256,128]{3,2,1,0:T(8,128)} %get-tuple-element.57), channel_id=1, source_target_pairs={{0,4},{4,8},{8,12},{12,16},{16,20},{20,24},{24,28},{28,32},{32,36}... | collective-permute-start | bytes 2359304 | tf_op jit(solution)/shard_map/grad_4/ppermute | solution.py:337
  114.8 2.0 group_13.1
  118.8 15.2 %collective-permute-start.11 = (f32[512,256]{1,0:T(8,128)S(1)}, f32[512,256]{1,0:T(8,128)S(1)}, u32[]{:S(2)}, u32[]{:S(2)}) collective-permute-start(f32[512,256]{1,0:T(8,128)S(1)} %dynamic-slice_bitcast_fusion), channel_id=1, source_target_pairs={{0,1},{1,0},{2,3},{3,2},{4,5},{5,4},{6,7},{7,6},{8,9},{9,8},{10,11... | collective-permute-start | bytes 1572872 | tf_op jit(solution)/shard_map/swap_c1/ppermute | solution.py:357
  134.0 1.5 collective-permute-done.11
  137.5 34.4 %collective-permute-start.14 = (f32[128,256]{1,0:T(8,128)S(1)}, f32[128,256]{1,0:T(8,128)S(1)}, u32[]{:S(2)}, u32[]{:S(2)}) collective-permute-start(f32[128,256]{1,0:T(8,128)S(1)} %get-tuple-element.88), channel_id=1, source_target_pairs={{0,64},{1,65},{2,66},{3,67},{4,68},{5,69},{6,70},{7,71},{8,72},{9,... | collective-permute-start | bytes 393224 | tf_op jit(solution)/shard_map/swap_y2/ppermute | solution.py:357
  171.9 1.4 collective-permute-start.19
  173.4 4.9 %collective-permute-done.14 = f32[128,256]{1,0:T(8,128)S(1)} collective-permute-done((f32[128,256]{1,0:T(8,128)S(1)}, f32[128,256]{1,0:T(8,128)S(1)}, u32[]{:S(2)}, u32[]{:S(2)}) %collective-permute-start.14) | collective-permute-done | bytes 131104 | tf_op jit(solution)/shard_map/swap_y2/ppermute | solution.py:357
  178.3 2.5 %collective-permute-done.15 = f32[128,256]{1,0:T(8,128)S(1)} collective-permute-done((f32[128,256]{1,0:T(8,128)S(1)}, f32[128,256]{1,0:T(8,128)S(1)}, u32[]{:S(2)}, u32[]{:S(2)}) %collective-permute-start.15) | collective-permute-done | bytes 131104 | tf_op jit(solution)/shard_map/swap_y3/ppermute | solution.py:357
  181.7 1.9 collective-permute-start.23
  184.8 2.8 %collective-permute-start.18 = (f32[128,256]{1,0:T(8,128)S(1)}, f32[128,256]{1,0:T(8,128)S(1)}, u32[]{:S(2)}, u32[]{:S(2)}) collective-permute-start(f32[128,256]{1,0:T(8,128)S(1)} %fusion), channel_id=1, source_target_pairs={{0,48},{1,49},{2,50},{3,51},{4,52},{5,53},{6,54},{7,55},{8,56},{9,... | collective-permute-start | bytes 393224 | tf_op jit(solution)/shard_map/swap_z3/ppermute | solution.py:357
  195.4 2.9 %finish_2.1.refs_5_ = f32[2,256,2048]{2,1,0:T(8,128)} custom-call(f32[2,3,256,128]{3,2,1,0:T(8,128)S(1)} %copy-done.1, f32[2,3,256,128]{3,2,1,0:T(8,128)S(1)} %copy-done.3, f32[2,3,256,128]{3,2,1,0:T(8,128)S(1)} %copy-done.5, f32[2,3,256,128]{3,2,1,0:T(8,128)S(1)} %copy-done.7, f32[2,2,256,128]{3,2,1,0:T(8,128)S(1)} %copy-done.13, ...), custom_call_target="tpu_custom_call" | custom-call | tf_op jit(solution)/shard_map/finish_2/pallas_call | solution.py:318
  198.2 2.7 %collective-permute-done.17 = f32[128,256]{1,0:T(8,128)S(1)} collective-permute-done((f32[128,256]{1,0:T(8,128)S(1)}, f32[128,256]{1,0:T(8,128)S(1)}, u32[]{:S(2)}, u32[]{:S(2)}) %collective-permute-start.17) | collective-permute-done | bytes 131104 | tf_op jit(solution)/shard_map/swap_z2/ppermute | solution.py:357
  201.1 2.4 %collective-permute-start.21 = (f32[128,256]{1,0:T(8,128)S(1)}, f32[128,256]{1,0:T(8,128)S(1)}, u32[]{:S(2)}, u32[]{:S(2)}) collective-permute-start(f32[128,256]{1,0:T(8,128)S(1)} %add_add_fusion), channel_id=1, source_target_pairs={{0,8},{1,9},{2,10},{3,11},{4,12},{5,13},{6,14},{7,15},{8,0},{9,1},... | collective-permute-start | bytes 393224 | tf_op jit(solution)/shard_map/swap_x2/ppermute | solution.py:357
  203.5 1.5 collective-permute-start.22
  205.7 2.6 %collective-permute-done.21 = f32[128,256]{1,0:T(8,128)S(1)} collective-permute-done((f32[128,256]{1,0:T(8,128)S(1)}, f32[128,256]{1,0:T(8,128)S(1)}, u32[]{:S(2)}, u32[]{:S(2)}) %collective-permute-start.21) | collective-permute-done | bytes 131104 | tf_op jit(solution)/shard_map/swap_x2/ppermute | solution.py:357
  208.4 2.9 %collective-permute-done.22 = f32[128,256]{1,0:T(8,128)S(1)} collective-permute-done((f32[128,256]{1,0:T(8,128)S(1)}, f32[128,256]{1,0:T(8,128)S(1)}, u32[]{:S(2)}, u32[]{:S(2)}) %collective-permute-start.22) | collective-permute-done | bytes 131104 | tf_op jit(solution)/shard_map/swap_x3/ppermute | solution.py:357
  212.1 2.9 %collective-permute-start.27 = (f32[2,2,256,128]{3,2,1,0:T(8,128)}, f32[2,2,256,128]{3,2,1,0:T(8,128)}, u32[]{:S(2)}, u32[]{:S(2)}) collective-permute-start(f32[2,2,256,128]{3,2,1,0:T(8,128)} %slice_add_fusion), channel_id=1, source_target_pairs={{0,4},{4,8},{8,12},{12,16},{16,20},{20,24},{24,28},{28,32},{32,36}... | collective-permute-start | bytes 1572872 | tf_op jit(solution)/shard_map/grad_0/ppermute | solution.py:337
  215.0 6.5 %collective-permute-start.25 = (f32[128,256]{1,0:T(8,128)S(1)}, f32[128,256]{1,0:T(8,128)S(1)}, u32[]{:S(2)}, u32[]{:S(2)}) collective-permute-start(f32[128,256]{1,0:T(8,128)S(1)} %add_multiply_fusion), channel_id=1, source_target_pairs={{0,64},{1,65},{2,66},{3,67},{4,68},{5,69},{6,70},{7,71},{8,72},{9,... | collective-permute-start | bytes 393224 | tf_op jit(solution)/shard_map/swap_y2/ppermute | solution.py:357
  221.6 5.7 %collective-permute-done.25 = f32[128,256]{1,0:T(8,128)S(1)} collective-permute-done((f32[128,256]{1,0:T(8,128)S(1)}, f32[128,256]{1,0:T(8,128)S(1)}, u32[]{:S(2)}, u32[]{:S(2)}) %collective-permute-start.25) | collective-permute-done | bytes 131104 | tf_op jit(solution)/shard_map/swap_y2/ppermute | solution.py:357
  227.3 2.6 %collective-permute-done.26 = f32[128,256]{1,0:T(8,128)} collective-permute-done((f32[128,256]{1,0:T(8,128)S(1)}, f32[128,256]{1,0:T(8,128)}, u32[]{:S(2)}, u32[]{:S(2)}) %collective-permute-start.26) | collective-permute-done | bytes 131104 | tf_op jit(solution)/shard_map/swap_y3/ppermute | solution.py:357
  231.8 1.2 collective-permute-start.28
  232.9 2.2 finish_0.1
  235.1 1.3 broadcast_select_fusion.1
  (126 shorter events, 34.1 us)
Async XLA Ops:
  0.6 14.7 %copy-start.41 = (s32[16,2]{0,1:T(2,128)S(1)}, s32[16,2]{0,1:T(2,128)}, u32[]{:S(2)}) copy-start(s32[16,2]{0,1:T(2,128)} %param.12) | copy-start | bytes 388
  0.6 14.7 %copy-start.40 = (f32[2,2,256,256]{3,2,1,0:T(8,128)S(1)}, f32[2,2,256,256]{3,2,1,0:T(8,128)}, u32[]{:S(2)}) copy-start(f32[2,2,256,256]{3,2,1,0:T(8,128)} %param.10) | copy-start | bytes 3145732
  3.0 26.5 %collective-permute-start = (f32[2,256,512]{2,1,0:T(8,128)}, f32[2,256,512]{2,1,0:T(8,128)S(1)}, u32[]{:S(2)}, u32[]{:S(2)}) collective-permute-start(f32[2,256,512]{2,1,0:T(8,128)} %slice.27), channel_id=1, source_target_pairs={{4,0},{8,4},{12,8},{16,12},{20,16},{24,20},{28,24},{32,28},{36,32}... | collective-permute-start | bytes 3145736 | tf_op jit(solution)/shard_map/halo_0/ppermute | solution.py:337
  7.4 22.3 %copy-start.29 = (bf16[2,256,256]{2,1,0:T(8,128)(2,1)S(1)}, bf16[2,256,256]{2,1,0:T(8,128)(2,1)}, u32[]{:S(2)}) copy-start(bf16[2,256,256]{2,1,0:T(8,128)(2,1)} %constant.81.clone.refs_4_.refs_5_.refs_6_.refs_8_) | copy-start | bytes 786436
  7.4 39.1 %collective-permute-start.7 = (f32[2,256,384]{2,1,0:T(8,128)}, f32[2,256,384]{2,1,0:T(8,128)}, u32[]{:S(2)}, u32[]{:S(2)}) collective-permute-start(f32[2,256,384]{2,1,0:T(8,128)} %get-tuple-element.78), channel_id=1, source_target_pairs={{4,0},{8,4},{12,8},{16,12},{20,16},{24,20},{28,24},{32,28},{36,32}... | collective-permute-start | bytes 2359304 | tf_op jit(solution)/shard_map/halo_1/ppermute | solution.py:337
  8.8 54.6 %collective-permute-start.5 = (f32[2,256,384]{2,1,0:T(8,128)}, f32[2,256,384]{2,1,0:T(8,128)}, u32[]{:S(2)}, u32[]{:S(2)}) collective-permute-start(f32[2,256,384]{2,1,0:T(8,128)} %get-tuple-element.79), channel_id=1, source_target_pairs={{4,0},{8,4},{12,8},{16,12},{20,16},{24,20},{28,24},{32,28},{36,32}... | collective-permute-start | bytes 2359304 | tf_op jit(solution)/shard_map/halo_2/ppermute | solution.py:337
  11.9 48.9 %collective-permute-start.3 = (f32[2,256,256]{2,1,0:T(8,128)}, f32[2,256,256]{2,1,0:T(8,128)}, u32[]{:S(2)}, u32[]{:S(2)}) collective-permute-start(f32[2,256,256]{2,1,0:T(8,128)} %slice.30), channel_id=1, source_target_pairs={{1,0},{2,1},{3,2},{5,4},{6,5},{7,6},{9,8},{10,9},{11,10},{13,12},{... | collective-permute-start | bytes 1572872 | tf_op jit(solution)/shard_map/right/ppermute | solution.py:337
  32.7 13.8 %copy-start.22 = (bf16[512,512]{1,0:T(8,128)(2,1)S(1)}, bf16[512,512]{1,0:T(8,128)(2,1)}, u32[]{:S(2)}) copy-start(bf16[512,512]{1,0:T(8,128)(2,1)} %constant.82.clone.refs_5_.refs_6_.refs_7_.refs_9_) | copy-start | bytes 1572868
  32.7 13.8 %copy-start.26 = (bf16[512,512]{1,0:T(8,128)(2,1)S(1)}, bf16[512,512]{1,0:T(8,128)(2,1)}, u32[]{:S(2)}) copy-start(bf16[512,512]{1,0:T(8,128)(2,1)} %constant.84.clone.refs_7_.refs_8_.refs_9_.refs_11_) | copy-start | bytes 1572868
  33.9 20.9 %copy-start.10 = (f32[2,2,256,128]{3,2,1,0:T(8,128)}, f32[2,2,256,128]{3,2,1,0:T(8,128)S(1)}, u32[]{:S(2)}) copy-start(f32[2,2,256,128]{3,2,1,0:T(8,128)S(1)} %get-tuple-element.71) | copy-start | bytes 1572868
  46.5 16.9 %copy-start.30 = (bf16[2,256,256]{2,1,0:T(8,128)(2,1)S(1)}, bf16[2,256,256]{2,1,0:T(8,128)(2,1)}, u32[]{:S(2)}) copy-start(bf16[2,256,256]{2,1,0:T(8,128)(2,1)} %constant.81.clone.refs_4_.refs_5_.refs_6_.refs_8_) | copy-start | bytes 786436
  46.5 16.9 %copy-start.33 = (bf16[2,256,256]{2,1,0:T(8,128)(2,1)S(1)}, bf16[2,256,256]{2,1,0:T(8,128)(2,1)}, u32[]{:S(2)}) copy-start(bf16[2,256,256]{2,1,0:T(8,128)(2,1)} %constant.83.clone.refs_6_.refs_7_.refs_8_.refs_10_) | copy-start | bytes 786436
  55.8 7.6 %copy-start.39 = (f32[2,2,256,256]{3,2,1,0:T(8,128)}, f32[2,2,256,256]{3,2,1,0:T(8,128)S(1)}, u32[]{:S(2)}) copy-start(f32[2,2,256,256]{3,2,1,0:T(8,128)S(1)} %get-tuple-element.47.refs_11_) | copy-start | bytes 3145732
  55.8 26.3 %collective-permute-start.8 = (f32[2,3,256,128]{3,2,1,0:T(8,128)S(1)}, f32[2,3,256,128]{3,2,1,0:T(8,128)S(1)}, u32[]{:S(2)}, u32[]{:S(2)}) collective-permute-start(f32[2,3,256,128]{3,2,1,0:T(8,128)S(1)} %get-tuple-element.45), channel_id=1, source_target_pairs={{0,4},{4,8},{8,12},{12,16},{16,20},{20,24},{24,28},{28,32},{32,36}... | collective-permute-start | bytes 2359304 | tf_op jit(solution)/shard_map/grad_1/ppermute | solution.py:337
  58.2 23.9 %collective-permute-start.6 = (f32[2,256,256]{2,1,0:T(8,128)S(1)}, f32[2,256,256]{2,1,0:T(8,128)S(1)}, u32[]{:S(2)}, u32[]{:S(2)}) collective-permute-start(f32[2,256,256]{2,1,0:T(8,128)S(1)} %slice.33), channel_id=1, source_target_pairs={{4,0},{8,4},{12,8},{16,12},{20,16},{24,20},{28,24},{32,28},{36,32}... | collective-permute-start | bytes 1572872 | tf_op jit(solution)/shard_map/halo_3/ppermute | solution.py:337
  59.5 31.2 %collective-permute-start.1 = (f32[2,256,384]{2,1,0:T(8,128)}, f32[2,256,384]{2,1,0:T(8,128)}, u32[]{:S(2)}, u32[]{:S(2)}) collective-permute-start(f32[2,256,384]{2,1,0:T(8,128)} %get-tuple-element.80), channel_id=1, source_target_pairs={{4,0},{8,4},{12,8},{16,12},{20,16},{24,20},{28,24},{32,28},{36,32}... | collective-permute-start | bytes 2359304 | tf_op jit(solution)/shard_map/halo_4/ppermute | solution.py:337
  69.4 12.7 %copy-start.4 = (f32[2,3,256,128]{3,2,1,0:T(8,128)}, f32[2,3,256,128]{3,2,1,0:T(8,128)S(1)}, u32[]{:S(2)}) copy-start(f32[2,3,256,128]{3,2,1,0:T(8,128)S(1)} %get-tuple-element.64.refs_2_) | copy-start | bytes 2359300
  69.4 21.2 %collective-permute-start.10 = (f32[2,3,256,128]{3,2,1,0:T(8,128)}, f32[2,3,256,128]{3,2,1,0:T(8,128)S(1)}, u32[]{:S(2)}, u32[]{:S(2)}) collective-permute-start(f32[2,3,256,128]{3,2,1,0:T(8,128)} %get-tuple-element.51), channel_id=1, source_target_pairs={{0,4},{4,8},{8,12},{12,16},{16,20},{20,24},{24,28},{28,32},{32,36}... | collective-permute-start | bytes 2359304 | tf_op jit(solution)/shard_map/grad_2/ppermute | solution.py:337
  73.9 39.0 %collective-permute-start.4 = (f32[2,256,256]{2,1,0:T(8,128)}, f32[2,256,256]{2,1,0:T(8,128)}, u32[]{:S(2)}, u32[]{:S(2)}) collective-permute-start(f32[2,256,256]{2,1,0:T(8,128)} %slice.36), channel_id=1, source_target_pairs={{1,0},{2,1},{3,2},{5,4},{6,5},{7,6},{9,8},{10,9},{11,10},{13,12},{... | collective-permute-start | bytes 1572872 | tf_op jit(solution)/shard_map/corner/ppermute | solution.py:337
  82.1 2.0 copy-start.19
  82.1 2.0 copy-start.2
  86.1 14.1 %copy-start.12 = (f32[2,2,256,128]{3,2,1,0:T(8,128)}, f32[2,2,256,128]{3,2,1,0:T(8,128)S(1)}, u32[]{:S(2)}) copy-start(f32[2,2,256,128]{3,2,1,0:T(8,128)S(1)} %get-tuple-element.65.refs_4_) | copy-start | bytes 1572868
  86.1 26.8 %collective-permute-start.9 = (f32[2,2,256,128]{3,2,1,0:T(8,128)}, f32[2,2,256,128]{3,2,1,0:T(8,128)S(1)}, u32[]{:S(2)}, u32[]{:S(2)}) collective-permute-start(f32[2,2,256,128]{3,2,1,0:T(8,128)} %get-tuple-element.50), channel_id=1, source_target_pairs={{0,4},{4,8},{8,12},{12,16},{16,20},{20,24},{24,28},{28,32},{32,36}... | collective-permute-start | bytes 1572872 | tf_op jit(solution)/shard_map/grad_3/ppermute | solution.py:337
  89.4 23.6 %collective-permute-start.2 = (f32[2,256,128]{2,1,0:T(8,128)}, f32[2,256,128]{2,1,0:T(8,128)}, u32[]{:S(2)}, u32[]{:S(2)}) collective-permute-start(f32[2,256,128]{2,1,0:T(8,128)} %slice.29), channel_id=1, source_target_pairs={{4,0},{8,4},{12,8},{16,12},{20,16},{24,20},{28,24},{32,28},{36,32}... | collective-permute-start | bytes 786440 | tf_op jit(solution)/shard_map/halo_5/ppermute | solution.py:337
  90.7 9.5 %copy-start.6 = (f32[2,3,256,128]{3,2,1,0:T(8,128)}, f32[2,3,256,128]{3,2,1,0:T(8,128)S(1)}, u32[]{:S(2)}) copy-start(f32[2,3,256,128]{3,2,1,0:T(8,128)S(1)} %collective-permute-done.10.refs_3_) | copy-start | bytes 2359300
  90.7 1.3 copy-start.20
  97.2 16.5 %copy-start.24 = (bf16[512,512]{1,0:T(8,128)(2,1)S(1)}, bf16[512,512]{1,0:T(8,128)(2,1)}, u32[]{:S(2)}) copy-start(bf16[512,512]{1,0:T(8,128)(2,1)} %constant.82.clone.refs_5_.refs_6_.refs_7_.refs_9_) | copy-start | bytes 1572868
  97.2 16.5 %copy-start.28 = (bf16[512,512]{1,0:T(8,128)(2,1)S(1)}, bf16[512,512]{1,0:T(8,128)(2,1)}, u32[]{:S(2)}) copy-start(bf16[512,512]{1,0:T(8,128)(2,1)} %constant.84.clone.refs_7_.refs_8_.refs_9_.refs_11_) | copy-start | bytes 1572868
  101.2 15.7 %copy-start.8 = (f32[2,3,256,128]{3,2,1,0:T(8,128)}, f32[2,3,256,128]{3,2,1,0:T(8,128)S(1)}, u32[]{:S(2)}) copy-start(f32[2,3,256,128]{3,2,1,0:T(8,128)S(1)} %get-tuple-element.66.refs_6_) | copy-start | bytes 2359300
  101.2 35.2 %collective-permute-start.12 = (f32[2,3,256,128]{3,2,1,0:T(8,128)}, f32[2,3,256,128]{3,2,1,0:T(8,128)}, u32[]{:S(2)}, u32[]{:S(2)}) collective-permute-start(f32[2,3,256,128]{3,2,1,0:T(8,128)} %get-tuple-element.57), channel_id=1, source_target_pairs={{0,4},{4,8},{8,12},{12,16},{16,20},{20,24},{24,28},{28,32},{32,36}... | collective-permute-start | bytes 2359304 | tf_op jit(solution)/shard_map/grad_4/ppermute | solution.py:337
  118.8 16.7 %collective-permute-start.11 = (f32[512,256]{1,0:T(8,128)S(1)}, f32[512,256]{1,0:T(8,128)S(1)}, u32[]{:S(2)}, u32[]{:S(2)}) collective-permute-start(f32[512,256]{1,0:T(8,128)S(1)} %dynamic-slice_bitcast_fusion), channel_id=1, source_target_pairs={{0,1},{1,0},{2,3},{3,2},{4,5},{5,4},{6,7},{7,6},{8,9},{9,8},{10,11... | collective-permute-start | bytes 1572872 | tf_op jit(solution)/shard_map/swap_c1/ppermute | solution.py:357
  137.4 35.9 %collective-permute-start.13 = (f32[128,256]{1,0:T(8,128)S(1)}, f32[128,256]{1,0:T(8,128)S(1)}, u32[]{:S(2)}, u32[]{:S(2)}) collective-permute-start(f32[128,256]{1,0:T(8,128)S(1)} %get-tuple-element.89), channel_id=1, source_target_pairs={{0,2},{1,3},{2,0},{3,1},{4,6},{5,7},{6,4},{7,5},{8,10},{9,11},{10,... | collective-permute-start | bytes 393224 | tf_op jit(solution)/shard_map/swap_y1/ppermute | solution.py:357
  137.5 40.7 %collective-permute-start.14 = (f32[128,256]{1,0:T(8,128)S(1)}, f32[128,256]{1,0:T(8,128)S(1)}, u32[]{:S(2)}, u32[]{:S(2)}) collective-permute-start(f32[128,256]{1,0:T(8,128)S(1)} %get-tuple-element.88), channel_id=1, source_target_pairs={{0,64},{1,65},{2,66},{3,67},{4,68},{5,69},{6,70},{7,71},{8,72},{9,... | collective-permute-start | bytes 393224 | tf_op jit(solution)/shard_map/swap_y2/ppermute | solution.py:357
  171.9 8.9 %collective-permute-start.15 = (f32[128,256]{1,0:T(8,128)S(1)}, f32[128,256]{1,0:T(8,128)S(1)}, u32[]{:S(2)}, u32[]{:S(2)}) collective-permute-start(f32[128,256]{1,0:T(8,128)S(1)} %get-tuple-element.87), channel_id=1, source_target_pairs={{0,66},{1,67},{2,64},{3,65},{4,70},{5,71},{6,68},{7,69},{8,74},{9,... | collective-permute-start | bytes 393224 | tf_op jit(solution)/shard_map/swap_y3/ppermute | solution.py:357
  171.9 29.1 %collective-permute-start.19 = (f32[2,3,256,128]{3,2,1,0:T(8,128)}, f32[2,3,256,128]{3,2,1,0:T(8,128)S(1)}, u32[]{:S(2)}, u32[]{:S(2)}) collective-permute-start(f32[2,3,256,128]{3,2,1,0:T(8,128)} %copy-done.18), channel_id=1, source_target_pairs={{0,4},{4,8},{8,12},{12,16},{16,20},{20,24},{24,28},{28,32},{32,36}... | collective-permute-start | bytes 2359304 | tf_op jit(solution)/shard_map/grad_5/ppermute | solution.py:337
  181.7 29.5 %collective-permute-start.23 = (f32[2,2,512,128]{3,2,1,0:T(8,128)}, f32[2,2,512,128]{3,2,1,0:T(8,128)S(1)}, u32[]{:S(2)}, u32[]{:S(2)}) collective-permute-start(f32[2,2,512,128]{3,2,1,0:T(8,128)} %copy-done.17), channel_id=1, source_target_pairs={{0,1},{1,2},{2,3},{4,5},{5,6},{6,7},{8,9},{9,10},{10,11},{12,13},{... | collective-permute-start | bytes 3145736 | tf_op jit(solution)/shard_map/over/ppermute | solution.py:337
  183.7 14.6 %collective-permute-start.16 = (f32[128,256]{1,0:T(8,128)S(1)}, f32[128,256]{1,0:T(8,128)S(1)}, u32[]{:S(2)}, u32[]{:S(2)}) collective-permute-start(f32[128,256]{1,0:T(8,128)S(1)} %fusion), channel_id=1, source_target_pairs={{0,16},{1,17},{2,18},{3,19},{4,20},{5,21},{6,22},{7,23},{8,24},{9,... | collective-permute-start | bytes 393224 | tf_op jit(solution)/shard_map/swap_z1/ppermute | solution.py:357
  184.8 16.2 %collective-permute-start.17 = (f32[128,256]{1,0:T(8,128)S(1)}, f32[128,256]{1,0:T(8,128)S(1)}, u32[]{:S(2)}, u32[]{:S(2)}) collective-permute-start(f32[128,256]{1,0:T(8,128)S(1)} %fusion), channel_id=1, source_target_pairs={{0,32},{1,33},{2,34},{3,35},{4,36},{5,37},{6,38},{7,39},{8,40},{9,... | collective-permute-start | bytes 393224 | tf_op jit(solution)/shard_map/swap_z2/ppermute | solution.py:357
  184.8 16.2 %collective-permute-start.18 = (f32[128,256]{1,0:T(8,128)S(1)}, f32[128,256]{1,0:T(8,128)S(1)}, u32[]{:S(2)}, u32[]{:S(2)}) collective-permute-start(f32[128,256]{1,0:T(8,128)S(1)} %fusion), channel_id=1, source_target_pairs={{0,48},{1,49},{2,50},{3,51},{4,52},{5,53},{6,54},{7,55},{8,56},{9,... | collective-permute-start | bytes 393224 | tf_op jit(solution)/shard_map/swap_z3/ppermute | solution.py:357
  195.4 15.9 %copy-start.11 = (f32[2,2,256,128]{3,2,1,0:T(8,128)S(1)}, f32[2,2,256,128]{3,2,1,0:T(8,128)}, u32[]{:S(2)}) copy-start(f32[2,2,256,128]{3,2,1,0:T(8,128)} %copy-done.10) | copy-start | bytes 1572868
  201.1 4.7 %collective-permute-start.20 = (f32[128,256]{1,0:T(8,128)S(1)}, f32[128,256]{1,0:T(8,128)S(1)}, u32[]{:S(2)}, u32[]{:S(2)}) collective-permute-start(f32[128,256]{1,0:T(8,128)S(1)} %add_add_fusion), channel_id=1, source_target_pairs={{0,4},{1,5},{2,6},{3,7},{4,0},{5,1},{6,2},{7,3},{8,12},{9,13},{10,... | collective-permute-start | bytes 393224 | tf_op jit(solution)/shard_map/swap_x1/ppermute | solution.py:357
  201.1 7.2 %collective-permute-start.21 = (f32[128,256]{1,0:T(8,128)S(1)}, f32[128,256]{1,0:T(8,128)S(1)}, u32[]{:S(2)}, u32[]{:S(2)}) collective-permute-start(f32[128,256]{1,0:T(8,128)S(1)} %add_add_fusion), channel_id=1, source_target_pairs={{0,8},{1,9},{2,10},{3,11},{4,12},{5,13},{6,14},{7,15},{8,0},{9,1},... | collective-permute-start | bytes 393224 | tf_op jit(solution)/shard_map/swap_x2/ppermute | solution.py:357
  203.5 7.7 %collective-permute-start.22 = (f32[128,256]{1,0:T(8,128)S(1)}, f32[128,256]{1,0:T(8,128)S(1)}, u32[]{:S(2)}, u32[]{:S(2)}) collective-permute-start(f32[128,256]{1,0:T(8,128)S(1)} %add_add_fusion), channel_id=1, source_target_pairs={{0,12},{1,13},{2,14},{3,15},{4,8},{5,9},{6,10},{7,11},{8,4},{9,5},... | collective-permute-start | bytes 393224 | tf_op jit(solution)/shard_map/swap_x3/ppermute | solution.py:357
  212.1 19.6 %collective-permute-start.27 = (f32[2,2,256,128]{3,2,1,0:T(8,128)}, f32[2,2,256,128]{3,2,1,0:T(8,128)}, u32[]{:S(2)}, u32[]{:S(2)}) collective-permute-start(f32[2,2,256,128]{3,2,1,0:T(8,128)} %slice_add_fusion), channel_id=1, source_target_pairs={{0,4},{4,8},{8,12},{12,16},{16,20},{20,24},{24,28},{28,32},{32,36}... | collective-permute-start | bytes 1572872 | tf_op jit(solution)/shard_map/grad_0/ppermute | solution.py:337
  215.0 6.5 %collective-permute-start.24 = (f32[128,256]{1,0:T(8,128)S(1)}, f32[128,256]{1,0:T(8,128)S(1)}, u32[]{:S(2)}, u32[]{:S(2)}) collective-permute-start(f32[128,256]{1,0:T(8,128)S(1)} %add_multiply_fusion), channel_id=1, source_target_pairs={{0,2},{1,3},{2,0},{3,1},{4,6},{5,7},{6,4},{7,5},{8,10},{9,11},{10,... | collective-permute-start | bytes 393224 | tf_op jit(solution)/shard_map/swap_y1/ppermute | solution.py:357
  215.0 12.3 %collective-permute-start.25 = (f32[128,256]{1,0:T(8,128)S(1)}, f32[128,256]{1,0:T(8,128)S(1)}, u32[]{:S(2)}, u32[]{:S(2)}) collective-permute-start(f32[128,256]{1,0:T(8,128)S(1)} %add_multiply_fusion), channel_id=1, source_target_pairs={{0,64},{1,65},{2,66},{3,67},{4,68},{5,69},{6,70},{7,71},{8,72},{9,... | collective-permute-start | bytes 393224 | tf_op jit(solution)/shard_map/swap_y2/ppermute | solution.py:357
  221.5 8.4 %collective-permute-start.26 = (f32[128,256]{1,0:T(8,128)S(1)}, f32[128,256]{1,0:T(8,128)}, u32[]{:S(2)}, u32[]{:S(2)}) collective-permute-start(f32[128,256]{1,0:T(8,128)S(1)} %add_multiply_fusion), channel_id=1, source_target_pairs={{0,66},{1,67},{2,64},{3,65},{4,70},{5,71},{6,68},{7,69},{8,74},{9,... | collective-permute-start | bytes 393224 | tf_op jit(solution)/shard_map/swap_y3/ppermute | solution.py:357
  231.8 3.4 %collective-permute-start.28 = (f32[512,256]{1,0:T(8,128)}, f32[512,256]{1,0:T(8,128)}, u32[]{:S(2)}, u32[]{:S(2)}) collective-permute-start(f32[512,256]{1,0:T(8,128)} %pad_maximum_fusion.1), channel_id=1, source_target_pairs={{0,1},{1,0},{2,3},{3,2},{4,5},{5,4},{6,7},{7,6},{8,9},{9,8},{10,11... | collective-permute-start | bytes 1572872 | tf_op jit(solution)/shard_map/swap_c1/ppermute | solution.py:357
  (23 other events, 23.6 us)

commit v6 on v5

--- a/solution.py
+++ b/solution.py
@@ -232,7 +232,7 @@
 IN_VMEM = pl.BlockSpec(memory_space=pltpu.VMEM)
 
 
-def run_group(first, count, bounds, live, off, field, halos, right, corner, measured, probe, tabs, carry, acc, after):
+def run_group(first, count, bounds, live, off, field, halos, right, measured, probe, tabs, carry, acc, after):
     wide = count + 2
     arrays, homes = [], [[], []]
 
@@ -244,20 +244,19 @@
         return len(arrays) - 1
 
     for b in range(first, first + wide):
-        if b < bounds[-1]:
-            chunk = next(i for i, end in enumerate(bounds) if b < end)
-            begin = bounds[chunk - 1] if chunk else 0
+        chunk = next(i for i, end in enumerate(bounds) if b < end)
+        begin = bounds[chunk - 1] if chunk else 0
+        own = field.shape[2] // LANE
+        if b < own:
             homes[0].append((index_in(field), 0, b * LANE))
-            homes[1].append((index_in(halos[chunk]), 0, (b - begin) * LANE))
         else:
-            at = (b - bounds[-1]) * LANE
-            homes[0].append((index_in(right), 0, at))
-            homes[1].append((index_in(corner), 0, at))
+            homes[0].append((index_in(right), 0, (b - own) * LANE))
+        homes[1].append((index_in(halos[chunk]), 0, (b - begin) * LANE))
     homes.append(arrays)
     args = [live, off, *arrays, *after, measured, probe, *tabs, carry, acc]
     specs = [IN_SMEM] * 2 + [IN_HBM] * (1 + len(arrays) + len(after)) + [IN_VMEM] * 7
     part = jax.ShapeDtypeStruct((2, count, SIZE, LANE), f32)
-    last = first + count == bounds[-1]
+    last = first + count + 2 == bounds[-1]
     whole = jax.ShapeDtypeStruct((2, 2, 2 * SIZE, LANE), f32)
     out_shape = (part, part, whole)
     out_shape += (jax.ShapeDtypeStruct((2, 2, SIZE, SIZE), f32),)
@@ -276,7 +275,7 @@
             pltpu.SemaphoreType.DMA((4,)),
         ],
         compiler_params=pltpu.CompilerParams(vmem_limit_bytes=44 * 2**20),
-        cost_estimate=pl.CostEstimate(flops=2**32, bytes_accessed=2**12, transcendentals=0),
+        cost_estimate=pl.CostEstimate(flops=2**33, bytes_accessed=2**12, transcendentals=0),
         name=f"group_{first}",
     )(*args)
 
@@ -357,18 +356,22 @@
         return lax.ppermute(array, AXES, pairs)
 
 
-def halved_sum(v, axis, here, pieces):
+def halved_sum(v, axis, here, pieces, held=None):
     v = v.reshape(pieces, -1, v.shape[-1])
     pick = functools.partial(lax.dynamic_index_in_dim, axis=0, keepdims=False)
     got = [swapped(pick(v, here ^ k), axis, k) for k in range(1, pieces)]
     if pieces == 2:
-        return pick(v, here) + got[0]
-    return (pick(v, here) + got[0]) + (got[1] + got[2])
-
-
-def exchanged_sum(v, axis):
+        return pick(v, here) + got[0], held
+    if held is not None:
+        got[0], held = lax.optimization_barrier((got[0], held))
+    return (pick(v, here) + got[0]) + (got[1] + got[2]), held
+
+
+def exchanged_sum(v, axis, held=None):
     a, b, c = [swapped(v, axis, k) for k in (1, 2, 3)]
-    return (v + a) + (b + c)
+    if held is not None:
+        a, held = lax.optimization_barrier((a, held))
+    return (v + a) + (b + c), held
 
 
 def gathered(v, axis, here, pieces):
@@ -387,7 +390,7 @@
     return jnp.concatenate([part_of(i) for i in range(pieces)], 0)
 
 
-BOUNDS = (4, 7, 10, 12, 15, 16)
+BOUNDS = (4, 7, 10, 13, 16, 18)
 
 
 def shards(field, probe, measured, offsets, live):
@@ -397,23 +400,23 @@
     tabs = [jnp.asarray(t) for t in tables()]
     probe_rows = probe.reshape(2, 2, 128, 2, 256).transpose(0, 1, 3, 2, 4).reshape(probe.shape)
     tie = lax.optimization_barrier
-    head, rest = tie((field[:, :, : LANE * BOUNDS[0]], field))
+    beside, rest = tie((field[:, :, :SIZE], field))
+    right = shifted(beside, "mode", -1, "right")
+    head, rest = tie((rest[:, :, : LANE * BOUNDS[0]], rest))
     halos = [shifted(head, "scan", -1, "halo_0")]
     for i, (a, b) in enumerate(zip(BOUNDS[:-1], BOUNDS[1:])):
-        part = rest[:, :, LANE * a : LANE * b]
+        part = right if a * LANE == cols else rest[:, :, LANE * a : LANE * b]
         halos.append(shifted(part, "scan", -1, f"halo_{i + 1}"))
-    right = shifted(field[:, :, :SIZE], "mode", -1, "right")
-    corner = shifted(halos[0][:, :, :SIZE], "mode", -1, "corner")
     carry = jnp.zeros((2, 2, 2 * SIZE, LANE), f32)
     acc = jnp.zeros(probe.shape, f32)
-    ends = [b - 2 for b in BOUNDS[:-1]] + [BOUNDS[-1]]
+    ends = [b - 2 for b in BOUNDS]
     plan = [(a, b - a) for a, b in zip([0] + ends[:-1], ends)]
     uppers, lowers, comings = [], [], []
     for i, (first, count) in enumerate(plan):
-        after = {2: (right,), 3: (1,), 4: (2,), 5: (3,)}.get(i, ())
+        after = {0: (right,), 3: (1,), 4: (2,), 5: (3,)}.get(i, ())
         after = [comings[j] if isinstance(j, int) else j for j in after]
         upper, lower, carry, acc = run_group(
-            first, count, BOUNDS, live, off, field, halos, right, corner, measured, probe_rows, tabs, carry, acc, after
+            first, count, BOUNDS, live, off, field, halos, right, measured, probe_rows, tabs, carry, acc, after
         )
         uppers.append(upper)
         lowers.append(lower)
@@ -421,26 +424,24 @@
         comings.append(shifted(lower, "scan", 1, f"grad_{i}") if early else None)
     s, m = lax.axis_index("scan"), lax.axis_index("mode")
     core, y = m % 2, (s // 16) * 2 + m // 2
-    v = halved_sum(acc.reshape(1024, 256), 0, core, 2)
-    v, comings[4], final = tie((v, comings[4], lowers[5]))
+    v, _ = halved_sum(acc.reshape(1024, 256), 0, core, 2)
+    v, comings[4], final, carry = tie((v, comings[4], lowers[5], carry))
     comings[5] = shifted(final, "scan", 1, "grad_5")
-    v = halved_sum(v, 1, y, 4)
-    v, carry = tie((v, carry))
     over = shifted(carry, "mode", 1, "over")
-    v = exchanged_sum(v, 2)
+    v, _ = halved_sum(v, 1, y, 4)
+    v, _ = exchanged_sum(v, 2)
     sources = [(first, array) for (first, _), pair in zip(plan, zip(uppers, comings)) for array in pair]
-    step = finish(range(2, 13), sources[2:10], field.shape, None)
+    step = finish(range(2, 14), sources[2:10], field.shape, None)
     v, comings[5], step = tie((v, comings[5], step))
-    v = exchanged_sum(v, 3)
+    v, over = exchanged_sum(v, 3, over)
     slots_all = lax.axis_size("scan") * lax.axis_size("mode") * SLOTS
     v = v * (1.0 / math.sqrt(slots_all))
-    v, over = tie((v, over))
     comings[0] = shifted(lowers[0] + over[:, :, SIZE:], "scan", 1, "grad_0")
     v = gathered(v, 1, y, 4)
     v, comings[0] = tie((v, comings[0]))
     probe_step = gathered(v, 0, core, 2).reshape(probe.shape)
-    rest = [(0, uppers[0]), (0, comings[0]), (0, over), (13, uppers[5]), (13, comings[5])]
-    step = finish([0, 1, 13, 14, 15], rest, field.shape, step)
+    rest = [(0, uppers[0]), (0, comings[0]), (0, over), *sources[10:]]
+    step = finish([0, 1, 14, 15], rest, field.shape, step)
     return (step, probe_step)
 
 

time: 238 us -> 257 us (1.080)
  starting transfers between devices: 109 us -> 139 us
  waiting for transfers between devices: 54.1 us -> 64.4 us
  Pallas kernels: 27.6 us -> 18 us
  local copies, waits for them, and re-layouts: 37.9 us -> 31.3 us
  other arithmetic: 6.95 us -> 4.26 us
    ppermute x14, starting transfers between devices: 65.2 us -> 81.5 us  [swapped(): return lax.ppermute(array, AXES, pairs)]
    ppermute x15 -> x14, starting transfers between devices: 43.8 us -> 57.1 us  [shifted(): return lax.ppermute(array, axis, pairs)]
    ppermute x15 -> x14, waiting for transfers between devices: 27.8 us -> 39.2 us  [shifted(): return lax.ppermute(array, axis, pairs)]
    pallas_call x6, Pallas kernels: 22.6 us -> 14 us  [run_group(): pl.pallas_call(functools.partial(group_kernel, first, count, (homes[0], h...]
    slice x6 -> x3, local copies, waits for them, and re-layouts: 10.9 us -> 6.96 us  [the longest x1 3.53 us: shards(): part = right if a * LANE == cols else rest[:, :, LANE * a:LANE * b]]
    unnamed x85 -> x71, local copies, waits for them, and re-layouts: 25 us -> 21.2 us
  transfers between devices with their start and end apart: 29 -> 28, of which waited for: 12 -> 12; matrix products, arithmetic and copies ran while one was open for 6% -> 3% of each run, Pallas kernels for 12% -> 7%
where the time goes in v6:
time: 257 us; the launch traced here: 258 us
  starting transfers between devices  139 us (54%)
  waiting for transfers between devices  64.4 us (25%)
  local copies, waits for them, and re-layouts  31.3 us (12%)
  Pallas kernels  18 us (7%)
  other arithmetic  4.26 us (2%)
    ppermute x14, starting transfers between devices, swapped(): return lax.ppermute(array, AXES, pairs)  81.5 us
    ppermute x14, starting transfers between devices, shifted(): return lax.ppermute(array, axis, pairs)  57.1 us
    ppermute x14, waiting for transfers between devices, shifted(): return lax.ppermute(array, axis, pairs)  39.2 us
    ppermute x14, waiting for transfers between devices, swapped(): return lax.ppermute(array, AXES, pairs)  25.2 us
    unnamed x71, local copies, waits for them, and re-layouts  21.2 us
    pallas_call x6, Pallas kernels, run_group(): pl.pallas_call(functools.partial(group_kernel, first, count, (homes[0], h...  14 us
  transfers between devices with their start and end apart: 28, of which 12 were waited for; matrix products, arithmetic and copies ran while one was open for 3% of the time, Pallas kernels for 7%

profile of v6, /device:TPU:1, one launch (start us, length us, event | category | flops | bytes accessed | tf_op | source)
XLA Modules:
  0.0 258.5 jit_solution(2712131637037811000)
XLA Ops:
  1.7 2.4 slice.22
  4.1 1.3 collective-permute-start
  5.4 3.3 %collective-permute-start.1 = (f32[2,256,256]{2,1,0:T(8,128)S(1)}, f32[2,256,256]{2,1,0:T(8,128)}, u32[]{:S(2)}, u32[]{:S(2)}) collective-permute-start(f32[2,256,256]{2,1,0:T(8,128)S(1)} %slice.21), channel_id=1, source_target_pairs={{1,0},{2,1},{3,2},{5,4},{6,5},{7,6},{9,8},{10,9},{11,10},{13,12},{... | collective-permute-start | bytes 1572872 | tf_op jit(solution)/shard_map/right/ppermute | solution.py:336
  8.7 3.5 %fusion.1 = (f32[2,256,384]{2,1,0:T(8,128)}, f32[2,256,384]{2,1,0:T(8,128)}, f32[2,256,384]{2,1,0:T(8,128)}, f32[2,256,384]{2,1,0:T(8,128)}) fusion(f32[2,256,2048]{2,1,0:T(8,128)} %refs_0_.11), kind=kLoop, calls=%fused_computation.20 | loop fusion | bytes 6291456 | tf_op jit(solution)/shard_map/slice | solution.py:408
  12.2 1.3 collective-permute-start.6
  13.5 1.3 collective-permute-start.4
  14.8 1.3 collective-permute-start.5
  16.2 1.6 reshape.17
  17.8 1.3 copy.13
  19.9 1.3 collective-permute-start.2
  21.2 9.4 %collective-permute-done.refs_1_ = f32[2,256,512]{2,1,0:T(8,128)S(1)} collective-permute-done((f32[2,256,512]{2,1,0:T(8,128)}, f32[2,256,512]{2,1,0:T(8,128)S(1)}, u32[]{:S(2)}, u32[]{:S(2)}) %collective-permute-start) | collective-permute-done | bytes 1048608 | tf_op jit(solution)/shard_map/halo_0/ppermute | solution.py:336
  30.6 1.3 collective-permute-start.3
  36.1 4.2 %group_0.1 = (f32[2,2,256,128]{3,2,1,0:T(8,128)S(1)}, f32[2,2,256,128]{3,2,1,0:T(8,128)S(1)}, f32[2,2,512,128]{3,2,1,0:T(8,128)S(1)}, f32[2,2,256,256]{3,2,1,0:T(8,128)S(1)}) custom-call(s32[1]{0:T(128)S(6)} %copy.15.live, s32[16,2]{1,0:T(8,128)S(1)} %broadcast_subtract_fusion.off, f32[2,256,2048]{2,1,0:T(8,128)} %refs_0_.11, ...), custom_call_target="tpu_custom_call" | custom-call | flops 8589934592 | bytes 4096 | tf_op jit(solution)/shard_map/group_0/pallas_call | solution.py:263
  40.3 7.2 %collective-permute-done.6.refs_2_.refs_1_ = f32[2,256,384]{2,1,0:T(8,128)S(1)} collective-permute-done((f32[2,256,384]{2,1,0:T(8,128)}, f32[2,256,384]{2,1,0:T(8,128)S(1)}, u32[]{:S(2)}, u32[]{:S(2)}) %collective-permute-start.6) | collective-permute-done | bytes 786464 | tf_op jit(solution)/shard_map/halo_1/ppermute | solution.py:336
  49.5 1.2 group_2.1
  50.7 14.7 %collective-permute-start.7 = (f32[2,3,256,128]{3,2,1,0:T(8,128)S(1)}, f32[2,3,256,128]{3,2,1,0:T(8,128)S(1)}, u32[]{:S(2)}, u32[]{:S(2)}) collective-permute-start(f32[2,3,256,128]{3,2,1,0:T(8,128)S(1)} %get-tuple-element.47), channel_id=1, source_target_pairs={{0,4},{4,8},{8,12},{12,16},{16,20},{20,24},{24,28},{28,32},{32,36}... | collective-permute-start | bytes 2359304 | tf_op jit(solution)/shard_map/grad_1/ppermute | solution.py:336
  65.4 1.2 group_5.1
  68.6 13.9 %collective-permute-start.9 = (f32[2,3,256,128]{3,2,1,0:T(8,128)S(1)}, f32[2,3,256,128]{3,2,1,0:T(8,128)S(1)}, u32[]{:S(2)}, u32[]{:S(2)}) collective-permute-start(f32[2,3,256,128]{3,2,1,0:T(8,128)S(1)} %get-tuple-element.53), channel_id=1, source_target_pairs={{0,4},{4,8},{8,12},{12,16},{16,20},{20,24},{24,28},{28,32},{32,36}... | collective-permute-start | bytes 2359304 | tf_op jit(solution)/shard_map/grad_2/ppermute | solution.py:336
  82.5 2.1 group_8.1
  85.6 2.6 collective-permute-start.8
  88.2 9.8 %collective-permute-done.2.refs_2_.refs_1_ = f32[2,256,384]{2,1,0:T(8,128)S(1)} collective-permute-done((f32[2,256,384]{2,1,0:T(8,128)}, f32[2,256,384]{2,1,0:T(8,128)S(1)}, u32[]{:S(2)}, u32[]{:S(2)}) %collective-permute-start.2) | collective-permute-done | bytes 786464 | tf_op jit(solution)/shard_map/halo_4/ppermute | solution.py:336
  98.0 1.8 collective-permute-done.9.refs_3_
  99.8 3.0 %group_11.1 = (f32[2,3,256,128]{3,2,1,0:T(8,128)S(1)}, f32[2,3,256,128]{3,2,1,0:T(8,128)}, f32[2,2,512,128]{3,2,1,0:T(8,128)S(1)}, f32[2,2,256,256]{3,2,1,0:T(8,128)S(1)}) custom-call(s32[1]{0:T(128)S(6)} %copy.15.live, s32[16,2]{1,0:T(8,128)S(1)} %broadcast_subtract_fusion.off, f32[2,256,2048]{2,1,0:T(8,128)} %refs_0_.11, ...), custom_call_target="tpu_custom_call" | custom-call | flops 8589934592 | bytes 4096 | tf_op jit(solution)/shard_map/group_11/pallas_call | solution.py:263
  104.7 8.2 %collective-permute-start.11 = (f32[2,3,256,128]{3,2,1,0:T(8,128)}, f32[2,3,256,128]{3,2,1,0:T(8,128)}, u32[]{:S(2)}, u32[]{:S(2)}) collective-permute-start(f32[2,3,256,128]{3,2,1,0:T(8,128)} %get-tuple-element.59), channel_id=1, source_target_pairs={{0,4},{4,8},{8,12},{12,16},{16,20},{20,24},{24,28},{28,32},{32,36}... | collective-permute-start | bytes 2359304 | tf_op jit(solution)/shard_map/grad_4/ppermute | solution.py:336
  113.0 3.2 %collective-permute-done.8.refs_4_.refs_5_ = f32[2,3,256,128]{3,2,1,0:T(8,128)S(1)} collective-permute-done((f32[2,3,256,128]{3,2,1,0:T(8,128)S(1)}, f32[2,3,256,128]{3,2,1,0:T(8,128)S(1)}, u32[]{:S(2)}, u32[]{:S(2)}) %collective-permute-start.8) | collective-permute-done | bytes 786464 | tf_op jit(solution)/shard_map/grad_3/ppermute | solution.py:336
  116.2 2.1 group_14.1
  121.0 1.9 collective-permute-done.10
  123.0 7.7 %collective-permute-done.11.refs_7_ = f32[2,3,256,128]{3,2,1,0:T(8,128)} collective-permute-done((f32[2,3,256,128]{3,2,1,0:T(8,128)}, f32[2,3,256,128]{3,2,1,0:T(8,128)}, u32[]{:S(2)}, u32[]{:S(2)}) %collective-permute-start.11) | collective-permute-done | bytes 786464 | tf_op jit(solution)/shard_map/grad_4/ppermute | solution.py:336
  130.7 1.9 collective-permute-start.20
  132.8 64.8 %collective-permute-start.13 = (f32[128,256]{1,0:T(8,128)S(1)}, f32[128,256]{1,0:T(8,128)S(1)}, u32[]{:S(2)}, u32[]{:S(2)}) collective-permute-start(f32[128,256]{1,0:T(8,128)S(1)} %get-tuple-element.89), channel_id=1, source_target_pairs={{0,64},{1,65},{2,66},{3,67},{4,68},{5,69},{6,70},{7,71},{8,72},{9,... | collective-permute-start | bytes 393224 | tf_op jit(solution)/shard_map/swap_y2/ppermute | solution.py:356
  197.8 3.1 %collective-permute-start.18 = (f32[2,2,256,128]{3,2,1,0:T(8,128)}, f32[2,2,256,128]{3,2,1,0:T(8,128)S(1)}, u32[]{:S(2)}, u32[]{:S(2)}) collective-permute-start(f32[2,2,256,128]{3,2,1,0:T(8,128)} %copy-done.22), channel_id=1, source_target_pairs={{0,4},{4,8},{8,12},{12,16},{16,20},{20,24},{24,28},{28,32},{32,36}... | collective-permute-start | bytes 1572872 | tf_op jit(solution)/shard_map/grad_5/ppermute | solution.py:336
  200.9 14.7 %collective-permute-done.13 = f32[128,256]{1,0:T(8,128)S(1)} collective-permute-done((f32[128,256]{1,0:T(8,128)S(1)}, f32[128,256]{1,0:T(8,128)S(1)}, u32[]{:S(2)}, u32[]{:S(2)}) %collective-permute-start.13) | collective-permute-done | bytes 131104 | tf_op jit(solution)/shard_map/swap_y2/ppermute | solution.py:356
  216.5 2.6 %collective-permute-start.15 = (f32[128,256]{1,0:T(8,128)S(1)}, f32[128,256]{1,0:T(8,128)S(1)}, u32[]{:S(2)}, u32[]{:S(2)}) collective-permute-start(f32[128,256]{1,0:T(8,128)S(1)} %fusion), channel_id=1, source_target_pairs={{0,16},{1,17},{2,18},{3,19},{4,20},{5,21},{6,22},{7,23},{8,24},{9,... | collective-permute-start | bytes 393224 | tf_op jit(solution)/shard_map/swap_z1/ppermute | solution.py:356
  219.2 2.5 collective-permute-start.17
  221.6 1.1 copy-done.1
  222.8 1.1 copy-done.3
  223.9 1.1 copy-done.5
  225.0 1.1 copy-done.7
  226.2 1.1 copy-done.9
  227.3 1.1 copy-done.11
  228.4 3.0 %finish_2.1.refs_5_ = f32[2,256,2048]{2,1,0:T(8,128)} custom-call(f32[2,3,256,128]{3,2,1,0:T(8,128)S(1)} %get-tuple-element.64.refs_0_, f32[2,3,256,128]{3,2,1,0:T(8,128)S(1)} %copy-done.1, f32[2,3,256,128]{3,2,1,0:T(8,128)S(1)} %copy-done.3, f32[2,3,256,128]{3,2,1,0:T(8,128)S(1)} %copy-done.5, f32[2,3,256,128]{3,2,1,0:T(8,128)S(1)} %copy-done.7, ...), custom_call_target="tpu_custom_call" | custom-call | tf_op jit(solution)/shard_map/finish_2/pallas_call | solution.py:317
  231.6 7.2 %collective-permute-start.21 = (f32[128,256]{1,0:T(8,128)S(1)}, f32[128,256]{1,0:T(8,128)S(1)}, u32[]{:S(2)}, u32[]{:S(2)}) collective-permute-start(f32[128,256]{1,0:T(8,128)S(1)} %add_add_fusion), channel_id=1, source_target_pairs={{0,8},{1,9},{2,10},{3,11},{4,12},{5,13},{6,14},{7,15},{8,0},{9,1},... | collective-permute-start | bytes 393224 | tf_op jit(solution)/shard_map/swap_x2/ppermute | solution.py:356
  239.7 1.6 collective-permute-start.26
  241.3 4.3 %collective-permute-done.21 = f32[128,256]{1,0:T(8,128)S(1)} collective-permute-done((f32[128,256]{1,0:T(8,128)S(1)}, f32[128,256]{1,0:T(8,128)S(1)}, u32[]{:S(2)}, u32[]{:S(2)}) %collective-permute-start.21) | collective-permute-done | bytes 131104 | tf_op jit(solution)/shard_map/swap_x2/ppermute | solution.py:356
  245.6 1.5 collective-permute-done.22
  247.3 3.8 %collective-permute-start.25 = (f32[128,256]{1,0:T(8,128)S(1)}, f32[128,256]{1,0:T(8,128)S(1)}, u32[]{:S(2)}, u32[]{:S(2)}) collective-permute-start(f32[128,256]{1,0:T(8,128)S(1)} %add_multiply_fusion), channel_id=1, source_target_pairs={{0,66},{1,67},{2,64},{3,65},{4,70},{5,71},{6,68},{7,69},{8,74},{9,... | collective-permute-start | bytes 393224 | tf_op jit(solution)/shard_map/swap_y3/ppermute | solution.py:356
  251.0 1.6 collective-permute-done.24
  252.6 1.3 collective-permute-done.25
  (107 shorter events, 21.7 us)
Async XLA Ops:
  1.7 14.4 %copy-start.34 = (s32[16,2]{0,1:T(2,128)S(1)}, s32[16,2]{0,1:T(2,128)}, u32[]{:S(2)}) copy-start(s32[16,2]{0,1:T(2,128)} %param.12) | copy-start | bytes 388
  1.7 14.5 %copy-start.33 = (f32[2,2,256,256]{3,2,1,0:T(8,128)S(1)}, f32[2,2,256,256]{3,2,1,0:T(8,128)}, u32[]{:S(2)}) copy-start(f32[2,2,256,256]{3,2,1,0:T(8,128)} %param.10) | copy-start | bytes 3145732
  4.1 26.5 %collective-permute-start = (f32[2,256,512]{2,1,0:T(8,128)}, f32[2,256,512]{2,1,0:T(8,128)S(1)}, u32[]{:S(2)}, u32[]{:S(2)}) collective-permute-start(f32[2,256,512]{2,1,0:T(8,128)} %slice.22), channel_id=1, source_target_pairs={{4,0},{8,4},{12,8},{16,12},{20,16},{24,20},{28,24},{32,28},{36,32}... | collective-permute-start | bytes 3145736 | tf_op jit(solution)/shard_map/halo_0/ppermute | solution.py:336
  5.4 14.5 %collective-permute-start.1 = (f32[2,256,256]{2,1,0:T(8,128)S(1)}, f32[2,256,256]{2,1,0:T(8,128)}, u32[]{:S(2)}, u32[]{:S(2)}) collective-permute-start(f32[2,256,256]{2,1,0:T(8,128)S(1)} %slice.21), channel_id=1, source_target_pairs={{1,0},{2,1},{3,2},{5,4},{6,5},{7,6},{9,8},{10,9},{11,10},{13,12},{... | collective-permute-start | bytes 1572872 | tf_op jit(solution)/shard_map/right/ppermute | solution.py:336
  12.2 35.2 %collective-permute-start.6 = (f32[2,256,384]{2,1,0:T(8,128)}, f32[2,256,384]{2,1,0:T(8,128)S(1)}, u32[]{:S(2)}, u32[]{:S(2)}) collective-permute-start(f32[2,256,384]{2,1,0:T(8,128)} %get-tuple-element.78), channel_id=1, source_target_pairs={{4,0},{8,4},{12,8},{16,12},{20,16},{24,20},{28,24},{32,28},{36,32}... | collective-permute-start | bytes 2359304 | tf_op jit(solution)/shard_map/halo_1/ppermute | solution.py:336
  13.5 51.9 %collective-permute-start.4 = (f32[2,256,384]{2,1,0:T(8,128)}, f32[2,256,384]{2,1,0:T(8,128)}, u32[]{:S(2)}, u32[]{:S(2)}) collective-permute-start(f32[2,256,384]{2,1,0:T(8,128)} %get-tuple-element.80), channel_id=1, source_target_pairs={{4,0},{8,4},{12,8},{16,12},{20,16},{24,20},{28,24},{32,28},{36,32}... | collective-permute-start | bytes 2359304 | tf_op jit(solution)/shard_map/halo_2/ppermute | solution.py:336
  14.8 67.6 %collective-permute-start.5 = (f32[2,256,384]{2,1,0:T(8,128)}, f32[2,256,384]{2,1,0:T(8,128)}, u32[]{:S(2)}, u32[]{:S(2)}) collective-permute-start(f32[2,256,384]{2,1,0:T(8,128)} %get-tuple-element.79), channel_id=1, source_target_pairs={{4,0},{8,4},{12,8},{16,12},{20,16},{24,20},{28,24},{32,28},{36,32}... | collective-permute-start | bytes 2359304 | tf_op jit(solution)/shard_map/halo_3/ppermute | solution.py:336
  19.9 78.1 %collective-permute-start.2 = (f32[2,256,384]{2,1,0:T(8,128)}, f32[2,256,384]{2,1,0:T(8,128)S(1)}, u32[]{:S(2)}, u32[]{:S(2)}) collective-permute-start(f32[2,256,384]{2,1,0:T(8,128)} %get-tuple-element.81), channel_id=1, source_target_pairs={{4,0},{8,4},{12,8},{16,12},{20,16},{24,20},{28,24},{32,28},{36,32}... | collective-permute-start | bytes 2359304 | tf_op jit(solution)/shard_map/halo_4/ppermute | solution.py:336
  30.6 82.4 %collective-permute-start.3 = (f32[2,256,256]{2,1,0:T(8,128)}, f32[2,256,256]{2,1,0:T(8,128)S(1)}, u32[]{:S(2)}, u32[]{:S(2)}) collective-permute-start(f32[2,256,256]{2,1,0:T(8,128)} %collective-permute-done.1.refs_2_), channel_id=1, source_target_pairs={{4,0},{8,4},{12,8},{16,12},{20,16},{24,20},{28,24},{32,28},{36,32}... | collective-permute-start | bytes 1572872 | tf_op jit(solution)/shard_map/halo_5/ppermute | solution.py:336
  36.0 12.3 %copy-start.24 = (bf16[512,512]{1,0:T(8,128)(2,1)S(1)}, bf16[512,512]{1,0:T(8,128)(2,1)}, u32[]{:S(2)}) copy-start(bf16[512,512]{1,0:T(8,128)(2,1)} %constant.82.clone.refs_6_.refs_7_.refs_8_) | copy-start | bytes 1572868
  36.0 12.3 %copy-start.26 = (bf16[512,512]{1,0:T(8,128)(2,1)S(1)}, bf16[512,512]{1,0:T(8,128)(2,1)}, u32[]{:S(2)}) copy-start(bf16[512,512]{1,0:T(8,128)(2,1)} %constant.84.clone.refs_8_.refs_9_.refs_10_) | copy-start | bytes 1572868
  36.0 12.3 %copy-start.28 = (bf16[2,256,256]{2,1,0:T(8,128)(2,1)S(1)}, bf16[2,256,256]{2,1,0:T(8,128)(2,1)}, u32[]{:S(2)}) copy-start(bf16[2,256,256]{2,1,0:T(8,128)(2,1)} %constant.81.clone.refs_5_.refs_6_.refs_7_) | copy-start | bytes 786436
  40.2 10.5 %copy-start.14 = (f32[2,2,256,128]{3,2,1,0:T(8,128)}, f32[2,2,256,128]{3,2,1,0:T(8,128)S(1)}, u32[]{:S(2)}) copy-start(f32[2,2,256,128]{3,2,1,0:T(8,128)S(1)} %get-tuple-element.72) | copy-start | bytes 1572868
  48.3 1.1 copy-start.20
  49.5 16.0 %copy-start.21 = (f32[2,256,384]{2,1,0:T(8,128)S(1)}, f32[2,256,384]{2,1,0:T(8,128)}, u32[]{:S(2)}) copy-start(f32[2,256,384]{2,1,0:T(8,128)} %copy-done.19) | copy-start | bytes 2359300
  50.7 31.7 %collective-permute-start.7 = (f32[2,3,256,128]{3,2,1,0:T(8,128)S(1)}, f32[2,3,256,128]{3,2,1,0:T(8,128)S(1)}, u32[]{:S(2)}, u32[]{:S(2)}) collective-permute-start(f32[2,3,256,128]{3,2,1,0:T(8,128)S(1)} %get-tuple-element.47), channel_id=1, source_target_pairs={{0,4},{4,8},{8,12},{12,16},{16,20},{20,24},{24,28},{28,32},{32,36}... | collective-permute-start | bytes 2359304 | tf_op jit(solution)/shard_map/grad_1/ppermute | solution.py:336
  68.6 31.2 %collective-permute-start.9 = (f32[2,3,256,128]{3,2,1,0:T(8,128)S(1)}, f32[2,3,256,128]{3,2,1,0:T(8,128)S(1)}, u32[]{:S(2)}, u32[]{:S(2)}) collective-permute-start(f32[2,3,256,128]{3,2,1,0:T(8,128)S(1)} %get-tuple-element.53), channel_id=1, source_target_pairs={{0,4},{4,8},{8,12},{12,16},{16,20},{20,24},{24,28},{28,32},{32,36}... | collective-permute-start | bytes 2359304 | tf_op jit(solution)/shard_map/grad_2/ppermute | solution.py:336
  82.5 2.2 copy-start
  85.6 17.3 %copy-start.6 = (f32[2,3,256,128]{3,2,1,0:T(8,128)}, f32[2,3,256,128]{3,2,1,0:T(8,128)S(1)}, u32[]{:S(2)}) copy-start(f32[2,3,256,128]{3,2,1,0:T(8,128)S(1)} %get-tuple-element.66.refs_4_) | copy-start | bytes 2359300
  85.6 30.6 %collective-permute-start.8 = (f32[2,3,256,128]{3,2,1,0:T(8,128)S(1)}, f32[2,3,256,128]{3,2,1,0:T(8,128)S(1)}, u32[]{:S(2)}, u32[]{:S(2)}) collective-permute-start(f32[2,3,256,128]{3,2,1,0:T(8,128)S(1)} %get-tuple-element.52), channel_id=1, source_target_pairs={{0,4},{4,8},{8,12},{12,16},{16,20},{20,24},{24,28},{28,32},{32,36}... | collective-permute-start | bytes 2359304 | tf_op jit(solution)/shard_map/grad_3/ppermute | solution.py:336
  99.8 3.1 %copy-start.4 = (f32[2,3,256,128]{3,2,1,0:T(8,128)}, f32[2,3,256,128]{3,2,1,0:T(8,128)S(1)}, u32[]{:S(2)}) copy-start(f32[2,3,256,128]{3,2,1,0:T(8,128)S(1)} %collective-permute-done.9.refs_3_) | copy-start | bytes 2359300
  104.7 26.0 %collective-permute-start.11 = (f32[2,3,256,128]{3,2,1,0:T(8,128)}, f32[2,3,256,128]{3,2,1,0:T(8,128)}, u32[]{:S(2)}, u32[]{:S(2)}) collective-permute-start(f32[2,3,256,128]{3,2,1,0:T(8,128)} %get-tuple-element.59), channel_id=1, source_target_pairs={{0,4},{4,8},{8,12},{12,16},{16,20},{20,24},{24,28},{28,32},{32,36}... | collective-permute-start | bytes 2359304 | tf_op jit(solution)/shard_map/grad_4/ppermute | solution.py:336
  116.2 2.2 copy-start.8
  120.9 2.0 collective-permute-start.10
  130.7 108.1 %collective-permute-start.20 = (f32[2,2,512,128]{3,2,1,0:T(8,128)}, f32[2,2,512,128]{3,2,1,0:T(8,128)S(1)}, u32[]{:S(2)}, u32[]{:S(2)}) collective-permute-start(f32[2,2,512,128]{3,2,1,0:T(8,128)} %copy-done.18), channel_id=1, source_target_pairs={{0,1},{1,2},{2,3},{4,5},{5,6},{6,7},{8,9},{9,10},{10,11},{12,13},{... | collective-permute-start | bytes 3145736 | tf_op jit(solution)/shard_map/over/ppermute | solution.py:336
  132.7 68.2 %collective-permute-start.12 = (f32[128,256]{1,0:T(8,128)S(1)}, f32[128,256]{1,0:T(8,128)S(1)}, u32[]{:S(2)}, u32[]{:S(2)}) collective-permute-start(f32[128,256]{1,0:T(8,128)S(1)} %get-tuple-element.90), channel_id=1, source_target_pairs={{0,2},{1,3},{2,0},{3,1},{4,6},{5,7},{6,4},{7,5},{8,10},{9,11},{10,... | collective-permute-start | bytes 393224 | tf_op jit(solution)/shard_map/swap_y1/ppermute | solution.py:356
  132.8 82.8 %collective-permute-start.13 = (f32[128,256]{1,0:T(8,128)S(1)}, f32[128,256]{1,0:T(8,128)S(1)}, u32[]{:S(2)}, u32[]{:S(2)}) collective-permute-start(f32[128,256]{1,0:T(8,128)S(1)} %get-tuple-element.89), channel_id=1, source_target_pairs={{0,64},{1,65},{2,66},{3,67},{4,68},{5,69},{6,70},{7,71},{8,72},{9,... | collective-permute-start | bytes 393224 | tf_op jit(solution)/shard_map/swap_y2/ppermute | solution.py:356
  197.6 18.0 %collective-permute-start.14 = (f32[128,256]{1,0:T(8,128)S(1)}, f32[128,256]{1,0:T(8,128)}, u32[]{:S(2)}, u32[]{:S(2)}) collective-permute-start(f32[128,256]{1,0:T(8,128)S(1)} %get-tuple-element.88), channel_id=1, source_target_pairs={{0,66},{1,67},{2,64},{3,65},{4,70},{5,71},{6,68},{7,69},{8,74},{9,... | collective-permute-start | bytes 393224 | tf_op jit(solution)/shard_map/swap_y3/ppermute | solution.py:356
  197.8 33.7 %collective-permute-start.18 = (f32[2,2,256,128]{3,2,1,0:T(8,128)}, f32[2,2,256,128]{3,2,1,0:T(8,128)S(1)}, u32[]{:S(2)}, u32[]{:S(2)}) collective-permute-start(f32[2,2,256,128]{3,2,1,0:T(8,128)} %copy-done.22), channel_id=1, source_target_pairs={{0,4},{4,8},{8,12},{12,16},{16,20},{20,24},{24,28},{28,32},{32,36}... | collective-permute-start | bytes 1572872 | tf_op jit(solution)/shard_map/grad_5/ppermute | solution.py:336
  216.5 14.9 %collective-permute-start.15 = (f32[128,256]{1,0:T(8,128)S(1)}, f32[128,256]{1,0:T(8,128)S(1)}, u32[]{:S(2)}, u32[]{:S(2)}) collective-permute-start(f32[128,256]{1,0:T(8,128)S(1)} %fusion), channel_id=1, source_target_pairs={{0,16},{1,17},{2,18},{3,19},{4,20},{5,21},{6,22},{7,23},{8,24},{9,... | collective-permute-start | bytes 393224 | tf_op jit(solution)/shard_map/swap_z1/ppermute | solution.py:356
  219.2 12.3 %collective-permute-start.16 = (f32[128,256]{1,0:T(8,128)S(1)}, f32[128,256]{1,0:T(8,128)S(1)}, u32[]{:S(2)}, u32[]{:S(2)}) collective-permute-start(f32[128,256]{1,0:T(8,128)S(1)} %fusion), channel_id=1, source_target_pairs={{0,32},{1,33},{2,34},{3,35},{4,36},{5,37},{6,38},{7,39},{8,40},{9,... | collective-permute-start | bytes 393224 | tf_op jit(solution)/shard_map/swap_z2/ppermute | solution.py:356
  219.2 12.3 %collective-permute-start.17 = (f32[128,256]{1,0:T(8,128)S(1)}, f32[128,256]{1,0:T(8,128)S(1)}, u32[]{:S(2)}, u32[]{:S(2)}) collective-permute-start(f32[128,256]{1,0:T(8,128)S(1)} %fusion), channel_id=1, source_target_pairs={{0,48},{1,49},{2,50},{3,51},{4,52},{5,53},{6,54},{7,55},{8,56},{9,... | collective-permute-start | bytes 393224 | tf_op jit(solution)/shard_map/swap_z3/ppermute | solution.py:356
  221.6 1.1 copy-start.1
  222.8 1.1 copy-start.3
  223.9 1.1 copy-start.5
  225.0 1.1 copy-start.7
  226.2 1.1 copy-start.9
  228.4 10.4 %copy-start.15 = (f32[2,2,256,128]{3,2,1,0:T(8,128)S(1)}, f32[2,2,256,128]{3,2,1,0:T(8,128)}, u32[]{:S(2)}) copy-start(f32[2,2,256,128]{3,2,1,0:T(8,128)} %copy-done.14) | copy-start | bytes 1572868
  231.4 22.8 %copy-start.13 = (f32[2,2,256,128]{3,2,1,0:T(8,128)S(1)}, f32[2,2,256,128]{3,2,1,0:T(8,128)}, u32[]{:S(2)}) copy-start(f32[2,2,256,128]{3,2,1,0:T(8,128)} %copy-done.12) | copy-start | bytes 1572868
  231.5 8.2 %copy-start.16 = (f32[2,2,256,128]{3,2,1,0:T(8,128)}, f32[2,2,256,128]{3,2,1,0:T(8,128)S(1)}, u32[]{:S(2)}) copy-start(f32[2,2,256,128]{3,2,1,0:T(8,128)S(1)} %collective-permute-done.18.refs_4_) | copy-start | bytes 1572868
  231.5 7.3 %collective-permute-start.19 = (f32[128,256]{1,0:T(8,128)S(1)}, f32[128,256]{1,0:T(8,128)S(1)}, u32[]{:S(2)}, u32[]{:S(2)}) collective-permute-start(f32[128,256]{1,0:T(8,128)S(1)} %add_add_fusion), channel_id=1, source_target_pairs={{0,4},{1,5},{2,6},{3,7},{4,0},{5,1},{6,2},{7,3},{8,12},{9,13},{10,... | collective-permute-start | bytes 393224 | tf_op jit(solution)/shard_map/swap_x1/ppermute | solution.py:356
  231.6 14.0 %collective-permute-start.21 = (f32[128,256]{1,0:T(8,128)S(1)}, f32[128,256]{1,0:T(8,128)S(1)}, u32[]{:S(2)}, u32[]{:S(2)}) collective-permute-start(f32[128,256]{1,0:T(8,128)S(1)} %add_add_fusion), channel_id=1, source_target_pairs={{0,8},{1,9},{2,10},{3,11},{4,12},{5,13},{6,14},{7,15},{8,0},{9,1},... | collective-permute-start | bytes 393224 | tf_op jit(solution)/shard_map/swap_x2/ppermute | solution.py:356
  238.8 8.2 %collective-permute-start.22 = (f32[128,256]{1,0:T(8,128)S(1)}, f32[128,256]{1,0:T(8,128)S(1)}, u32[]{:S(2)}, u32[]{:S(2)}) collective-permute-start(f32[128,256]{1,0:T(8,128)S(1)} %add_add_fusion), channel_id=1, source_target_pairs={{0,12},{1,13},{2,14},{3,15},{4,8},{5,9},{6,10},{7,11},{8,4},{9,5},... | collective-permute-start | bytes 393224 | tf_op jit(solution)/shard_map/swap_x3/ppermute | solution.py:356
  239.7 14.4 %collective-permute-start.26 = (f32[2,2,256,128]{3,2,1,0:T(8,128)}, f32[2,2,256,128]{3,2,1,0:T(8,128)S(1)}, u32[]{:S(2)}, u32[]{:S(2)}) collective-permute-start(f32[2,2,256,128]{3,2,1,0:T(8,128)} %slice_add_fusion), channel_id=1, source_target_pairs={{0,4},{4,8},{8,12},{12,16},{16,20},{20,24},{24,28},{28,32},{32,36}... | collective-permute-start | bytes 1572872 | tf_op jit(solution)/shard_map/grad_0/ppermute | solution.py:336
  247.1 3.9 %collective-permute-start.23 = (f32[128,256]{1,0:T(8,128)S(1)}, f32[128,256]{1,0:T(8,128)S(1)}, u32[]{:S(2)}, u32[]{:S(2)}) collective-permute-start(f32[128,256]{1,0:T(8,128)S(1)} %add_multiply_fusion), channel_id=1, source_target_pairs={{0,2},{1,3},{2,0},{3,1},{4,6},{5,7},{6,4},{7,5},{8,10},{9,11},{10,... | collective-permute-start | bytes 393224 | tf_op jit(solution)/shard_map/swap_y1/ppermute | solution.py:356
  247.2 5.5 %collective-permute-start.24 = (f32[128,256]{1,0:T(8,128)S(1)}, f32[128,256]{1,0:T(8,128)S(1)}, u32[]{:S(2)}, u32[]{:S(2)}) collective-permute-start(f32[128,256]{1,0:T(8,128)S(1)} %add_multiply_fusion), channel_id=1, source_target_pairs={{0,64},{1,65},{2,66},{3,67},{4,68},{5,69},{6,70},{7,71},{8,72},{9,... | collective-permute-start | bytes 393224 | tf_op jit(solution)/shard_map/swap_y2/ppermute | solution.py:356
  247.3 6.7 %collective-permute-start.25 = (f32[128,256]{1,0:T(8,128)S(1)}, f32[128,256]{1,0:T(8,128)S(1)}, u32[]{:S(2)}, u32[]{:S(2)}) collective-permute-start(f32[128,256]{1,0:T(8,128)S(1)} %add_multiply_fusion), channel_id=1, source_target_pairs={{0,66},{1,67},{2,64},{3,65},{4,70},{5,71},{6,68},{7,69},{8,74},{9,... | collective-permute-start | bytes 393224 | tf_op jit(solution)/shard_map/swap_y3/ppermute | solution.py:356
  254.1 2.2 collective-permute-start.27
  (15 other events, 14.3 us)
